TPU v7x, 32 devices: a whole 2x2x4 slice. The times are simulated.
32 devices in a mesh: inp: 8 (over y, x, core), tf: 4 (over z).
Axes of the slice: x: 2, y: 2, z: 4, core: 2. Of those that a mesh axis runs over, the one named last changes fastest.
Arguments:
- voltages: bfloat16 [2, 2048, 16384], P(None, 'inp', 'tf'), may hold values from -6 to 6
- window: float32 [4, 128], replicated, may hold values from -3 to 3
Outputs:
- visibilities: float32 [128, 2, 2048, 1280], P('tf', None, 'inp')
All inputs are finite; a program needn't handle non-finite values.
Results may differ from a plain program's by a relative error of at most 0.0034.
Values may be sent and summed in bfloat16 or wider, within the bound.
No kernel may reach another device: no remote copies, remote signals or barrier semaphores. Data moves between devices by JAX's collectives and lax.ppermute only.
A program may use at most 320 MiB of HBM per device.

v0:
```python
import functools
import math

import jax
import jax.numpy as jnp
import numpy as np
from jax import lax
from jax.experimental import pallas as pl
from jax.experimental.pallas import tpu as pltpu
from jax.sharding import PartitionSpec as P

GROUP = 4


def dft_tables(length):
    indices = np.arange(length)
    phase = 2.0 * np.pi / length * (indices[:, None] * indices[None, :] % length)
    cosine = np.cos(phase) / math.sqrt(length)
    sine = np.sin(phase) / math.sqrt(length)
    upper = np.concatenate([cosine, sine], axis=1)
    lower = np.concatenate([-sine, cosine], axis=1)
    table = np.concatenate([upper, lower], axis=0).astype(np.float32)
    high = table.astype(jnp.bfloat16)
    low = (table - high.astype(np.float32)).astype(jnp.bfloat16)
    return np.stack([high, low])


def spectra_kernel(place, groups, kept, chunks, merge, *refs):
    refs = list(refs)
    me_ref = refs.pop(0)
    here, after = refs.pop(0), refs.pop(0)
    halo = refs.pop(0) if place["halo"] else None
    window, table = refs.pop(0), refs.pop(0)
    earlier = refs.pop(0) if merge else None
    store = refs.pop()
    own_ref = refs.pop(0)
    outs = refs
    step = pl.program_id(0)
    channels = window.shape[1]
    taps = window.shape[0]
    inputs = here.shape[1]
    frames = groups * GROUP
    rows = 2 * frames
    lane_tiles = inputs // 128

    def run(tail):
        weights = [window[t : t + 1, :] for t in range(taps)]
        filtered = []
        for part in range(2):
            loaded = [here[part, :, i * channels : (i + 1) * channels] for i in range(GROUP)]
            loaded += [tail[part, :, i * channels : (i + 1) * channels] for i in range(taps - 1)]
            loaded = [x.astype(jnp.float32) for x in loaded]
            filtered.append(
                [sum(weights[t] * loaded[i + t] for t in range(taps)) for i in range(GROUP)]
            )
        for i in range(GROUP):
            both = jnp.concatenate([filtered[0][i], filtered[1][i]], axis=1)
            high = both.astype(jnp.bfloat16)
            low = (both - high.astype(jnp.float32)).astype(jnp.bfloat16)
            nt = functools.partial(
                lax.dot_general,
                dimension_numbers=(((1,), (1,)), ((), ())),
                preferred_element_type=jnp.float32,
            )
            out = nt(table[0], high) + (nt(table[1], high) + nt(table[0], low))
            for part in range(2):
                first = part * frames + step * GROUP + i
                for lane in range(lane_tiles):
                    store[lane, pl.ds(first, channels, stride=rows), :] = out[
                        part * channels : (part + 1) * channels, lane * 128 : (lane + 1) * 128
                    ]

    if halo is None:
        run(after)
    else:
        last = pl.num_programs(0) - 1

        @pl.when(step < last)
        def _():
            run(after)

        @pl.when(step == last)
        def _():
            run(halo)

    @pl.when(step == pl.num_programs(0) - 1)
    def _():
        devices = channels // kept

        def piece(channel):
            start = pl.multiple_of(channel * rows, rows)
            got = [store[lane, pl.ds(start, rows), :] for lane in range(lane_tiles)]
            return jnp.concatenate(got, axis=1).astype(jnp.bfloat16)

        me = me_ref[0]

        def own(i, carry):
            own_ref[i] = piece(me * kept + i)
            return carry

        lax.fori_loop(0, kept, own, 0)
        for hop in range(1, devices):
            base = lax.rem(me + hop, devices) * kept
            if merge:
                first = 0
                for q, size in enumerate(chunks):
                    out = outs[(hop - 1) * len(chunks) + q]

                    def one(i, carry, out=out, first=first, base=base, hop=hop):
                        out[i, :rows, :] = earlier[hop - 1, first + i]
                        out[i, rows:, :] = piece(base + first + i)
                        return carry

                    lax.fori_loop(0, size, one, 0)
                    first += size
            else:

                def rest(i, carry, base=base, hop=hop):
                    outs[0][hop - 1, i] = piece(base + i)
                    return carry

                lax.fori_loop(0, kept, rest, 0)


def spectra_part(voltages, halo, window, table, me, devices, first, groups, chunks, earlier):
    parts, inputs, samples = voltages.shape
    channels = window.shape[1]
    kept = channels // devices
    rows = 2 * groups * GROUP
    width = GROUP * channels
    last = samples // width - 1
    merge = earlier is not None
    operands = [me, voltages, voltages]
    in_specs = [
        pl.BlockSpec(memory_space=pltpu.SMEM),
        pl.BlockSpec((2, inputs, width), lambda i: (0, 0, first + i)),
        pl.BlockSpec((2, inputs, width), lambda i: (0, 0, jnp.minimum(first + i + 1, last))),
    ]
    whole = lambda shape: pl.BlockSpec(shape, lambda i: (0,) * len(shape))
    if halo is not None:
        operands.append(halo)
        in_specs.append(whole(halo.shape))
    operands += [window, table]
    in_specs += [whole(window.shape), whole(table.shape)]
    shapes = [(kept, rows, inputs)]
    if merge:
        operands.append(earlier)
        in_specs.append(whole(earlier.shape))
        shapes += [(size, 2 * rows, inputs) for _ in range(devices - 1) for size in chunks]
    else:
        shapes.append((devices - 1, kept, rows, inputs))
    return pl.pallas_call(
        functools.partial(
            spectra_kernel, {"halo": halo is not None}, groups, kept, chunks, merge
        ),
        grid=(groups,),
        out_shape=[jax.ShapeDtypeStruct(s, jnp.bfloat16) for s in shapes],
        in_specs=in_specs,
        out_specs=[whole(s) for s in shapes],
        scratch_shapes=[pltpu.VMEM((inputs // 128, channels * rows, 128), jnp.float32)],
        compiler_params=pltpu.CompilerParams(
            vmem_limit_bytes=48 * 1024 * 1024, dimension_semantics=("arbitrary",)
        ),
        cost_estimate=pl.CostEstimate(
            flops=2 * 3 * 4 * channels * channels * inputs * groups * GROUP,
            bytes_accessed=2 * voltages.size,
            transcendentals=0,
        ),
    )(*operands)


def pairs_kernel(scale, half, count, counts, *refs):
    out = refs[-1]
    per_block = [refs[n * count : (n + 1) * count] for n in range(half + 1)]

    def pieces(block):
        got = []
        for ref, many in zip(per_block[block], counts):
            values = [ref[0]] if many is None else [ref[m, 0] for m in range(many)]
            for value in values:
                got.append(value)
        return got

    mine = pieces(0)
    turned = []
    for value in mine:
        size = 2 * PART_FRAMES
        for first in range(0, value.shape[0], size):
            turned.append(value[first + PART_FRAMES : first + size])
            turned.append(-value[first : first + PART_FRAMES])
    left = jnp.concatenate(mine, axis=0).T
    left_turned = jnp.concatenate(turned, axis=0).T
    width = left.shape[0]
    for block in range(half + 1):
        right = jnp.concatenate(pieces(block), axis=0)
        columns = slice(block * width, (block + 1) * width)
        out[0, 0, :, columns] = (
            jnp.dot(left, right, preferred_element_type=jnp.float32) * scale
        )
        out[0, 1, :, columns] = (
            jnp.dot(left_turned, right, preferred_element_type=jnp.float32) * scale
        )


PART_FRAMES = 16


def pairs(blocks, total, first, size, kept, scale):
    half = len(blocks) - 1
    inputs = blocks[0][0][0].shape[-1]
    operands, in_specs, counts = [], [], []
    depth = 0
    for number, block in enumerate(blocks):
        for array, stack, offset in block:
            operands.append(array)
            if array.ndim - (stack is not None) == 3:
                rows = array.shape[-2]
                if number == 0:
                    counts.append(None)
                    depth += rows
                if stack is None:
                    spec = pl.BlockSpec((1, rows, inputs), lambda i, o=offset: (o + i, 0, 0))
                else:
                    spec = pl.BlockSpec(
                        (None, 1, rows, inputs), lambda i, o=offset, s=stack: (s, o + i, 0, 0)
                    )
            else:
                many, rows = array.shape[-4], array.shape[-2]
                if number == 0:
                    counts.append(many)
                    depth += many * rows
                if stack is None:
                    spec = pl.BlockSpec(
                        (many, 1, rows, inputs), lambda i, o=offset: (0, o + i, 0, 0)
                    )
                else:
                    spec = pl.BlockSpec(
                        (None, many, 1, rows, inputs),
                        lambda i, o=offset, s=stack: (s, 0, o + i, 0, 0),
                    )
            in_specs.append(spec)
    count = len(counts)
    slots = (half + 1) * inputs
    aliases = {}
    if total is not None:
        aliases = {len(operands): 0}
        operands.append(total)
        in_specs.append(pl.BlockSpec(memory_space=pl.ANY))

    def body(*refs):
        refs = list(refs)
        if total is not None:
            refs.pop(-2)
        pairs_kernel(scale, half, count, counts, *refs)

    return pl.pallas_call(
        body,
        grid=(size,),
        out_shape=jax.ShapeDtypeStruct((kept, 2, inputs, slots), jnp.float32),
        in_specs=in_specs,
        out_specs=pl.BlockSpec((1, 2, inputs, slots), lambda i: (first + i, 0, 0, 0)),
        input_output_aliases=aliases,
        compiler_params=pltpu.CompilerParams(
            vmem_limit_bytes=32 * 1024 * 1024, dimension_semantics=("arbitrary",)
        ),
        cost_estimate=pl.CostEstimate(
            flops=2 * size * 2 * inputs * slots * depth,
            bytes_accessed=size * 2 * inputs * slots * 4,
            transcendentals=0,
        ),
    )(*operands)


def shifted(x, axis, by):
    devices = lax.axis_size(axis)
    return lax.ppermute(x, axis, [(i, (i + by) % devices) for i in range(devices)])


def swapped(x, axis, bit):
    devices = lax.axis_size(axis)
    return lax.ppermute(x, axis, [(i, i ^ bit) for i in range(devices)])


def partners(own, axis):
    devices = lax.axis_size(axis)
    if devices != 8:
        return [(shifted(own, axis, -hop), None) for hop in range(1, devices // 2 + 1)]
    place = lax.axis_index(axis)
    is_far = (place & 2) == 2
    is_odd = (place & 1) == 1
    over_y = swapped(own, axis, 4)
    over_x = swapped(jnp.where(is_far, own, over_y), axis, 2)
    sent = jnp.where(is_odd, jnp.stack([own, over_x]), jnp.stack([over_x, over_y]))
    over_core = swapped(sent, axis, 1)
    return [(over_core, 0), (over_x, None), (over_core, 1), (over_y, None)]


def chunk_sizes(kept):
    if kept < 16:
        return [kept]
    return [kept // 4] * 4


def on_device(voltages, window):
    tap_count, channels = window.shape
    frames_dev = voltages.shape[2] // channels
    devices = lax.axis_size("tf")
    kept = channels // devices
    chunks = chunk_sizes(kept)
    groups = frames_dev // GROUP // 2
    leading = voltages[:, :, : (tap_count - 1) * channels]
    halo = lax.ppermute(leading, "tf", [(i, i - 1) for i in range(1, devices)])
    table = jnp.asarray(dft_tables(channels))
    me = lax.axis_index("tf").astype(jnp.int32).reshape(1)
    own_a, rest = spectra_part(
        voltages, None, window, table, me, devices, 0, groups, chunks, None
    )
    own_b, *pieces = spectra_part(
        voltages, halo, window, table, me, devices, groups, groups, chunks, rest
    )
    scale = 1.0 / math.sqrt(frames_dev * devices)
    first_a = [(own_a, None)] + partners(own_a, "inp")
    first_b = [(own_b, None)] + partners(own_b, "inp")
    total = None
    first = 0
    for q, size in enumerate(chunks):
        arrived = [
            shifted(pieces[(hop - 1) * len(chunks) + q], "tf", hop) for hop in range(1, devices)
        ]
        own = jnp.stack(arrived)
        later = [(own, None)] + partners(own, "inp")
        blocks = [
            [(*a, first), (*b, first), (*c, 0)] for a, b, c in zip(first_a, first_b, later)
        ]
        total = pairs(blocks, total, first, size, kept, scale)
        first += size
    return total


def solution(mesh):
    in_specs = (P(None, "inp", "tf"), P())
    out_specs = P("tf", None, "inp", None)
    return jax.shard_map(
        on_device, mesh=mesh, in_specs=in_specs, out_specs=out_specs, check_vma=False
    )
```

profile of v0, /device:TPU:17, one launch (start us, length us, event | category | flops | bytes accessed | tf_op | source)
XLA Modules:
  0.0 263.0 jit_solution(10748867080456652097)
XLA Ops:
  1.0 2.1 collective-permute-start
  4.8 8.6 %shard_map.37 = (bf16[32,32,256]{2,1,0:T(8,128)(2,1)S(1)}, bf16[3,32,32,256]{3,2,1,0:T(8,128)(2,1)S(1)}) custom-call(s32[1]{0:T(128)} %bitcast.refs_0_, bf16[2,256,4096]{2,1,0:T(8,128)(2,1)} %refs_2_.3, bf16[2,256,4096]{2,1,0:T(8,128)(2,1)} %refs_2_.3, f32[4,128]{1,0:T(4,128)S(1)} %copy-done.1, bf16[2,256,256]{2,1,0:T(8,128)(2,1)S(1)} %copy-done), custom_call_target="tpu_custom_call" | custom-call | flops 1610612736 | bytes 4194304 | tf_op jit(solution)/shard_map/pallas_call | solution.py:152
  14.7 9.7 %shard_map.38 = (bf16[32,32,256]{2,1,0:T(8,128)(2,1)S(1)}, bf16[8,64,256]{2,1,0:T(8,128)(2,1)S(1)}, bf16[8,64,256]{2,1,0:T(8,128)(2,1)S(1)}, bf16[8,64,256]{2,1,...) custom-call(s32[1]{0:T(128)} %bitcast.refs_0_, ...), custom_call_target="tpu_custom_call" | custom-call | flops 1610612736 | bytes 4194304 | tf_op jit(solution)/shard_map/pallas_call | solution.py:152
  27.3 3.9 %collective-permute-done.25 = bf16[8,64,256]{2,1,0:T(8,128)(2,1)} collective-permute-done((bf16[8,64,256]{2,1,0:T(8,128)(2,1)S(1)}, bf16[8,64,256]{2,1,0:T(8,128)(2,1)}, u32[]{:S(2)}, u32[]{:S(2)}) %collective-permute-start.25) | collective-permute-done | bytes 262176 | tf_op jit(solution)/shard_map/ppermute | solution.py:276
  31.2 2.2 collective-permute-start.20
  33.4 10.2 %collective-permute-done.26 = bf16[8,64,256]{2,1,0:T(8,128)(2,1)} collective-permute-done((bf16[8,64,256]{2,1,0:T(8,128)(2,1)S(1)}, bf16[8,64,256]{2,1,0:T(8,128)(2,1)}, u32[]{:S(2)}, u32[]{:S(2)}) %collective-permute-start.26) | collective-permute-done | bytes 262176 | tf_op jit(solution)/shard_map/ppermute | solution.py:276
  43.6 3.5 %collective-permute-start.21 = (bf16[8,64,256]{2,1,0:T(8,128)(2,1)S(1)}, bf16[8,64,256]{2,1,0:T(8,128)(2,1)}, u32[]{:S(2)}, u32[]{:S(2)}) collective-permute-start(bf16[8,64,256]{2,1,0:T(8,128)(2,1)S(1)} %get-tuple-element.31), channel_id=1, source_target_pairs={{0,3},{1,0},{2,1},{3,2},{4,7},{5,4},{6,5},{7,6},{8,11},{9,8},{10,9... | collective-permute-start | bytes 786440 | tf_op jit(solution)/shard_map/ppermute | solution.py:276
  47.1 15.4 %collective-permute-done.27 = bf16[8,64,256]{2,1,0:T(8,128)(2,1)} collective-permute-done((bf16[8,64,256]{2,1,0:T(8,128)(2,1)}, bf16[8,64,256]{2,1,0:T(8,128)(2,1)}, u32[]{:S(2)}, u32[]{:S(2)}) %collective-permute-start.27) | collective-permute-done | bytes 262176 | tf_op jit(solution)/shard_map/ppermute | solution.py:276
  62.5 2.1 pad_maximum_fusion.3.refs_2_
  64.6 3.4 %collective-permute-start.14 = (bf16[8,64,256]{2,1,0:T(8,128)(2,1)}, bf16[8,64,256]{2,1,0:T(8,128)(2,1)S(1)}, u32[]{:S(2)}, u32[]{:S(2)}) collective-permute-start(bf16[8,64,256]{2,1,0:T(8,128)(2,1)} %get-tuple-element.27), channel_id=1, source_target_pairs={{0,2},{1,3},{2,0},{3,1},{4,6},{5,7},{6,4},{7,5},{8,10},{9,11},{10,... | collective-permute-start | bytes 786440 | tf_op jit(solution)/shard_map/ppermute | solution.py:276
  68.0 8.5 %collective-permute-done.20 = bf16[8,64,256]{2,1,0:T(8,128)(2,1)} collective-permute-done((bf16[8,64,256]{2,1,0:T(8,128)(2,1)S(1)}, bf16[8,64,256]{2,1,0:T(8,128)(2,1)}, u32[]{:S(2)}, u32[]{:S(2)}) %collective-permute-start.20) | collective-permute-done | bytes 262176 | tf_op jit(solution)/shard_map/ppermute | solution.py:276
  76.6 8.3 %collective-permute-done.21 = bf16[8,64,256]{2,1,0:T(8,128)(2,1)} collective-permute-done((bf16[8,64,256]{2,1,0:T(8,128)(2,1)S(1)}, bf16[8,64,256]{2,1,0:T(8,128)(2,1)}, u32[]{:S(2)}, u32[]{:S(2)}) %collective-permute-start.21) | collective-permute-done | bytes 262176 | tf_op jit(solution)/shard_map/ppermute | solution.py:276
  88.6 5.0 %collective-permute-done.14 = bf16[8,64,256]{2,1,0:T(8,128)(2,1)S(1)} collective-permute-done((bf16[8,64,256]{2,1,0:T(8,128)(2,1)}, bf16[8,64,256]{2,1,0:T(8,128)(2,1)S(1)}, u32[]{:S(2)}, u32[]{:S(2)}) %collective-permute-start.14) | collective-permute-done | bytes 262176 | tf_op jit(solution)/shard_map/ppermute | solution.py:276
  93.5 3.0 %collective-permute-start.2 = (bf16[8,64,256]{2,1,0:T(8,128)(2,1)S(1)}, bf16[8,64,256]{2,1,0:T(8,128)(2,1)}, u32[]{:S(2)}, u32[]{:S(2)}) collective-permute-start(bf16[8,64,256]{2,1,0:T(8,128)(2,1)S(1)} %get-tuple-element.24), channel_id=1, source_target_pairs={{0,2},{1,3},{2,0},{3,1},{4,6},{5,7},{6,4},{7,5},{8,10},{9,11},{10,... | collective-permute-start | bytes 786440 | tf_op jit(solution)/shard_map/ppermute | solution.py:276
  96.5 8.2 %collective-permute-done.15 = bf16[8,64,256]{2,1,0:T(8,128)(2,1)S(1)} collective-permute-done((bf16[8,64,256]{2,1,0:T(8,128)(2,1)}, bf16[8,64,256]{2,1,0:T(8,128)(2,1)S(1)}, u32[]{:S(2)}, u32[]{:S(2)}) %collective-permute-start.15) | collective-permute-done | bytes 262176 | tf_op jit(solution)/shard_map/ppermute | solution.py:276
  104.8 2.1 collective-permute-start.3
  106.9 2.1 pad_maximum_fusion.2.refs_2_
  112.6 3.3 %collective-permute-done.3 = bf16[8,64,256]{2,1,0:T(8,128)(2,1)} collective-permute-done((bf16[8,64,256]{2,1,0:T(8,128)(2,1)S(1)}, bf16[8,64,256]{2,1,0:T(8,128)(2,1)}, u32[]{:S(2)}, u32[]{:S(2)}) %collective-permute-start.3) | collective-permute-done | bytes 262176 | tf_op jit(solution)/shard_map/ppermute | solution.py:276
  118.9 1.8 collective-permute-start.6
  121.9 3.4 %collective-permute-done.22.refs_14_ = bf16[3,8,64,256]{3,2,1,0:T(8,128)(2,1)} collective-permute-done((bf16[3,8,64,256]{3,2,1,0:T(8,128)(2,1)}, bf16[3,8,64,256]{3,2,1,0:T(8,128)(2,1)}, u32[]{:S(2)}, u32[]{:S(2)}) %collective-permute-start.22) | collective-permute-done | bytes 786464 | tf_op jit(solution)/shard_map/ppermute | solution.py:281
  128.0 25.3 %collective-permute-done.16.refs_14_ = bf16[3,8,64,256]{3,2,1,0:T(8,128)(2,1)S(1)} collective-permute-done((bf16[3,8,64,256]{3,2,1,0:T(8,128)(2,1)S(1)}, bf16[3,8,64,256]{3,2,1,0:T(8,128)(2,1)S(1)}, u32[]{:S(2)}, u32[]{:S(2)}) %collective-permute-start.16) | collective-permute-done | bytes 786464 | tf_op jit(solution)/shard_map/ppermute | solution.py:281
  155.6 14.5 %collective-permute-done.10.refs_14_ = bf16[3,8,64,256]{3,2,1,0:T(8,128)(2,1)S(1)} collective-permute-done((bf16[3,8,64,256]{3,2,1,0:T(8,128)(2,1)S(1)}, bf16[3,8,64,256]{3,2,1,0:T(8,128)(2,1)S(1)}, u32[]{:S(2)}, u32[]{:S(2)}) %collective-permute-start.10) | collective-permute-done | bytes 786464 | tf_op jit(solution)/shard_map/ppermute | solution.py:281
  174.5 5.7 %collective-permute-start.30 = (bf16[2,3,8,64,256]{4,3,2,1,0:T(8,128)(2,1)S(1)}, bf16[2,3,8,64,256]{4,3,2,1,0:T(8,128)(2,1)S(1)}, u32[]{:S(2)}, u32[]{:S(2)}) collective-permute-start(bf16[2,3,8,64,256]{4,3,2,1,0:T(8,128)(2,1)S(1)} %maximum_select_fusion.3), channel_id=1, source_target_pairs={{0,4},{4,0},{8,12},{12,8},{16,20},{20,16},{24,28},{28,24},{1,5},{5... | collective-permute-start | bytes 4718600 | tf_op jit(solution)/shard_map/ppermute | solution.py:281
  181.6 5.4 %collective-permute-done.17.refs_8_ = bf16[3,8,64,256]{3,2,1,0:T(8,128)(2,1)S(1)} collective-permute-done((bf16[3,8,64,256]{3,2,1,0:T(8,128)(2,1)S(1)}, bf16[3,8,64,256]{3,2,1,0:T(8,128)(2,1)S(1)}, u32[]{:S(2)}, u32[]{:S(2)}) %collective-permute-start.17) | collective-permute-done | bytes 786464 | tf_op jit(solution)/shard_map/ppermute | solution.py:281
  187.0 8.4 %collective-permute-start.24 = (bf16[2,3,8,64,256]{4,3,2,1,0:T(8,128)(2,1)S(1)}, bf16[2,3,8,64,256]{4,3,2,1,0:T(8,128)(2,1)S(1)}, u32[]{:S(2)}, u32[]{:S(2)}) collective-permute-start(bf16[2,3,8,64,256]{4,3,2,1,0:T(8,128)(2,1)S(1)} %maximum_select_fusion.2), channel_id=1, source_target_pairs={{0,4},{4,0},{8,12},{12,8},{16,20},{20,16},{24,28},{28,24},{1,5},{5... | collective-permute-start | bytes 4718600 | tf_op jit(solution)/shard_map/ppermute | solution.py:281
  195.7 19.4 %collective-permute-done.8.refs_7_ = bf16[32,32,256]{2,1,0:T(8,128)(2,1)S(1)} collective-permute-done((bf16[32,32,256]{2,1,0:T(8,128)(2,1)S(1)}, bf16[32,32,256]{2,1,0:T(8,128)(2,1)S(1)}, u32[]{:S(2)}, u32[]{:S(2)}) %collective-permute-start.8) | collective-permute-done | bytes 524320 | tf_op jit(solution)/shard_map/ppermute | solution.py:281
  215.1 4.4 %collective-permute-start.18 = (bf16[2,3,8,64,256]{4,3,2,1,0:T(8,128)(2,1)S(1)}, bf16[2,3,8,64,256]{4,3,2,1,0:T(8,128)(2,1)S(1)}, u32[]{:S(2)}, u32[]{:S(2)}) collective-permute-start(bf16[2,3,8,64,256]{4,3,2,1,0:T(8,128)(2,1)S(1)} %maximum_select_fusion.1), channel_id=1, source_target_pairs={{0,4},{4,0},{8,12},{12,8},{16,20},{20,16},{24,28},{28,24},{1,5},{5... | collective-permute-start | bytes 4718600 | tf_op jit(solution)/shard_map/ppermute | solution.py:281
  220.6 3.5 %collective-permute-done.9.refs_4_.refs_10_ = bf16[2,32,32,256]{3,2,1,0:T(8,128)(2,1)S(1)} collective-permute-done((bf16[2,32,32,256]{3,2,1,0:T(8,128)(2,1)S(1)}, bf16[2,32,32,256]{3,2,1,0:T(8,128)(2,1)S(1)}, u32[]{:S(2)}, u32[]{:S(2)}) %collective-permute-start.9) | collective-permute-done | bytes 1048608 | tf_op jit(solution)/shard_map/ppermute | solution.py:281
  224.1 10.1 %shard_map.39.refs_15_ = f32[32,2,256,1280]{3,2,1,0:T(8,128)} custom-call(bf16[32,32,256]{2,1,0:T(8,128)(2,1)S(1)} %get-tuple-element.20.refs_0_, bf16[32,32,256]{2,1,0:T(8,128)(2,1)S(1)} %get-tuple-element.22.refs_1_, bf16[3,8,64,256]{3,2,1,0:T(8,128)(2,1)} %pad_maximum_fusion.3.refs_2_, ...), custom_call_target="tpu_custom_call" | custom-call | flops 2684354560 | bytes 20971520 | tf_op jit(solution)/shard_map/pallas_call | solution.py:256
  234.2 10.4 %shard_map.40.refs_15_ = f32[32,2,256,1280]{3,2,1,0:T(8,128)} custom-call(bf16[32,32,256]{2,1,0:T(8,128)(2,1)S(1)} %get-tuple-element.20.refs_0_, bf16[32,32,256]{2,1,0:T(8,128)(2,1)S(1)} %get-tuple-element.22.refs_1_, bf16[3,8,64,256]{3,2,1,0:T(8,128)(2,1)} %pad_maximum_fusion.2.refs_2_, ...), custom_call_target="tpu_custom_call", output_to_operand_aliasing={{}: (15, {})} | custom-call | flops 2684354560 | bytes 20971520 | tf_op jit(solution)/shard_map/pallas_call | solution.py:256
  244.5 9.2 %shard_map.41.refs_15_ = f32[32,2,256,1280]{3,2,1,0:T(8,128)} custom-call(bf16[32,32,256]{2,1,0:T(8,128)(2,1)S(1)} %get-tuple-element.20.refs_0_, bf16[32,32,256]{2,1,0:T(8,128)(2,1)S(1)} %get-tuple-element.22.refs_1_, bf16[3,8,64,256]{3,2,1,0:T(8,128)(2,1)S(1)} %pad_maximum_fusion.1.refs_2_, ...), custom_call_target="tpu_custom_call", output_to_operand_aliasing={{}: (15, {})} | custom-call | flops 2684354560 | bytes 20971520 | tf_op jit(solution)/shard_map/pallas_call | solution.py:256
  253.7 9.2 %shard_map.42 = f32[32,2,256,1280]{3,2,1,0:T(8,128)} custom-call(bf16[32,32,256]{2,1,0:T(8,128)(2,1)S(1)} %get-tuple-element.20.refs_0_, bf16[32,32,256]{2,1,0:T(8,128)(2,1)S(1)} %get-tuple-element.22.refs_1_, bf16[3,8,64,256]{3,2,1,0:T(8,128)(2,1)S(1)} %pad_maximum_fusion.refs_2_, ...), custom_call_target="tpu_custom_call", output_to_operand_aliasing={{}: (15, {})} | custom-call | flops 2684354560 | bytes 20971520 | tf_op jit(solution)/shard_map/pallas_call | solution.py:256
  (69 shorter events, 30.4 us)
Async XLA Ops:
  1.0 13.6 %collective-permute-start = (bf16[2,256,384]{2,1,0:T(8,128)(2,1)S(1)}, bf16[2,256,384]{2,1,0:T(8,128)(2,1)S(1)}, u32[]{:S(2)}, u32[]{:S(2)}) collective-permute-start(bf16[2,256,384]{2,1,0:T(8,128)(2,1)S(1)} %slice.3), channel_id=1, source_target_pairs={{1,0},{2,1},{3,2},{5,4},{6,5},{7,6},{9,8},{10,9},{11,10},{13,12},{... | collective-permute-start | bytes 1179656 | tf_op jit(solution)/shard_map/ppermute | solution.py:312
  13.4 51.3 %collective-permute-start.4 = (bf16[32,32,256]{2,1,0:T(8,128)(2,1)S(1)}, bf16[32,32,256]{2,1,0:T(8,128)(2,1)S(1)}, u32[]{:S(2)}, u32[]{:S(2)}) collective-permute-start(bf16[32,32,256]{2,1,0:T(8,128)(2,1)S(1)} %get-tuple-element.20.refs_0_), channel_id=1, source_target_pairs={{0,16},{4,20},{8,24},{12,28},{16,0},{20,4},{24,8},{28,12},{1,17},{... | collective-permute-start | bytes 1572872 | tf_op jit(solution)/shard_map/ppermute | solution.py:281
  24.4 6.7 %collective-permute-start.25 = (bf16[8,64,256]{2,1,0:T(8,128)(2,1)S(1)}, bf16[8,64,256]{2,1,0:T(8,128)(2,1)}, u32[]{:S(2)}, u32[]{:S(2)}) collective-permute-start(bf16[8,64,256]{2,1,0:T(8,128)(2,1)S(1)} %get-tuple-element.32), channel_id=1, source_target_pairs={{0,1},{1,2},{2,3},{3,0},{4,5},{5,6},{6,7},{7,4},{8,9},{9,10},{10,1... | collective-permute-start | bytes 786440 | tf_op jit(solution)/shard_map/ppermute | solution.py:276
  25.7 17.9 %collective-permute-start.26 = (bf16[8,64,256]{2,1,0:T(8,128)(2,1)S(1)}, bf16[8,64,256]{2,1,0:T(8,128)(2,1)}, u32[]{:S(2)}, u32[]{:S(2)}) collective-permute-start(bf16[8,64,256]{2,1,0:T(8,128)(2,1)S(1)} %get-tuple-element.33), channel_id=1, source_target_pairs={{0,2},{1,3},{2,0},{3,1},{4,6},{5,7},{6,4},{7,5},{8,10},{9,11},{10,... | collective-permute-start | bytes 786440 | tf_op jit(solution)/shard_map/ppermute | solution.py:276
  25.8 36.8 %collective-permute-start.27 = (bf16[8,64,256]{2,1,0:T(8,128)(2,1)}, bf16[8,64,256]{2,1,0:T(8,128)(2,1)}, u32[]{:S(2)}, u32[]{:S(2)}) collective-permute-start(bf16[8,64,256]{2,1,0:T(8,128)(2,1)} %get-tuple-element.34), channel_id=1, source_target_pairs={{0,3},{1,0},{2,1},{3,2},{4,7},{5,4},{6,5},{7,6},{8,11},{9,8},{10,9... | collective-permute-start | bytes 786440 | tf_op jit(solution)/shard_map/ppermute | solution.py:276
  27.0 41.1 %collective-permute-start.19 = (bf16[8,64,256]{2,1,0:T(8,128)(2,1)S(1)}, bf16[8,64,256]{2,1,0:T(8,128)(2,1)S(1)}, u32[]{:S(2)}, u32[]{:S(2)}) collective-permute-start(bf16[8,64,256]{2,1,0:T(8,128)(2,1)S(1)} %get-tuple-element.29), channel_id=1, source_target_pairs={{0,1},{1,2},{2,3},{3,0},{4,5},{5,6},{6,7},{7,4},{8,9},{9,10},{10,1... | collective-permute-start | bytes 786440 | tf_op jit(solution)/shard_map/ppermute | solution.py:276
  31.2 45.4 %collective-permute-start.20 = (bf16[8,64,256]{2,1,0:T(8,128)(2,1)S(1)}, bf16[8,64,256]{2,1,0:T(8,128)(2,1)}, u32[]{:S(2)}, u32[]{:S(2)}) collective-permute-start(bf16[8,64,256]{2,1,0:T(8,128)(2,1)S(1)} %get-tuple-element.30), channel_id=1, source_target_pairs={{0,2},{1,3},{2,0},{3,1},{4,6},{5,7},{6,4},{7,5},{8,10},{9,11},{10,... | collective-permute-start | bytes 786440 | tf_op jit(solution)/shard_map/ppermute | solution.py:276
  43.6 41.2 %collective-permute-start.21 = (bf16[8,64,256]{2,1,0:T(8,128)(2,1)S(1)}, bf16[8,64,256]{2,1,0:T(8,128)(2,1)}, u32[]{:S(2)}, u32[]{:S(2)}) collective-permute-start(bf16[8,64,256]{2,1,0:T(8,128)(2,1)S(1)} %get-tuple-element.31), channel_id=1, source_target_pairs={{0,3},{1,0},{2,1},{3,2},{4,7},{5,4},{6,5},{7,6},{8,11},{9,8},{10,9... | collective-permute-start | bytes 786440 | tf_op jit(solution)/shard_map/ppermute | solution.py:276
  62.5 24.8 %collective-permute-start.13 = (bf16[8,64,256]{2,1,0:T(8,128)(2,1)}, bf16[8,64,256]{2,1,0:T(8,128)(2,1)}, u32[]{:S(2)}, u32[]{:S(2)}) collective-permute-start(bf16[8,64,256]{2,1,0:T(8,128)(2,1)} %get-tuple-element.26), channel_id=1, source_target_pairs={{0,1},{1,2},{2,3},{3,0},{4,5},{5,6},{6,7},{7,4},{8,9},{9,10},{10,1... | collective-permute-start | bytes 786440 | tf_op jit(solution)/shard_map/ppermute | solution.py:276
  64.6 28.9 %collective-permute-start.14 = (bf16[8,64,256]{2,1,0:T(8,128)(2,1)}, bf16[8,64,256]{2,1,0:T(8,128)(2,1)S(1)}, u32[]{:S(2)}, u32[]{:S(2)}) collective-permute-start(bf16[8,64,256]{2,1,0:T(8,128)(2,1)} %get-tuple-element.27), channel_id=1, source_target_pairs={{0,2},{1,3},{2,0},{3,1},{4,6},{5,7},{6,4},{7,5},{8,10},{9,11},{10,... | collective-permute-start | bytes 786440 | tf_op jit(solution)/shard_map/ppermute | solution.py:276
  68.0 36.7 %collective-permute-start.15 = (bf16[8,64,256]{2,1,0:T(8,128)(2,1)}, bf16[8,64,256]{2,1,0:T(8,128)(2,1)S(1)}, u32[]{:S(2)}, u32[]{:S(2)}) collective-permute-start(bf16[8,64,256]{2,1,0:T(8,128)(2,1)} %get-tuple-element.28), channel_id=1, source_target_pairs={{0,3},{1,0},{2,1},{3,2},{4,7},{5,4},{6,5},{7,6},{8,11},{9,8},{10,9... | collective-permute-start | bytes 786440 | tf_op jit(solution)/shard_map/ppermute | solution.py:276
  76.6 33.3 %collective-permute-start.1 = (bf16[8,64,256]{2,1,0:T(8,128)(2,1)}, bf16[8,64,256]{2,1,0:T(8,128)(2,1)}, u32[]{:S(2)}, u32[]{:S(2)}) collective-permute-start(bf16[8,64,256]{2,1,0:T(8,128)(2,1)} %get-tuple-element.23), channel_id=1, source_target_pairs={{0,1},{1,2},{2,3},{3,0},{4,5},{5,6},{6,7},{7,4},{8,9},{9,10},{10,1... | collective-permute-start | bytes 786440 | tf_op jit(solution)/shard_map/ppermute | solution.py:276
  84.8 34.0 %collective-permute-start.28 = (bf16[3,8,64,256]{3,2,1,0:T(8,128)(2,1)}, bf16[3,8,64,256]{3,2,1,0:T(8,128)(2,1)S(1)}, u32[]{:S(2)}, u32[]{:S(2)}) collective-permute-start(bf16[3,8,64,256]{3,2,1,0:T(8,128)(2,1)} %pad_maximum_fusion.3.refs_2_), channel_id=1, source_target_pairs={{0,16},{4,20},{8,24},{12,28},{16,0},{20,4},{24,8},{28,12},{1,17},{... | collective-permute-start | bytes 2359304 | tf_op jit(solution)/shard_map/ppermute | solution.py:281
  87.3 30.0 %collective-permute-start.5 = (bf16[32,32,256]{2,1,0:T(8,128)(2,1)}, bf16[32,32,256]{2,1,0:T(8,128)(2,1)S(1)}, u32[]{:S(2)}, u32[]{:S(2)}) collective-permute-start(bf16[32,32,256]{2,1,0:T(8,128)(2,1)} %broadcast_select_fusion.5), channel_id=1, source_target_pairs={{0,8},{4,12},{8,0},{12,4},{16,24},{20,28},{24,16},{28,20},{1,9},{5... | collective-permute-start | bytes 1572872 | tf_op jit(solution)/shard_map/ppermute | solution.py:281
  93.5 17.8 %collective-permute-start.2 = (bf16[8,64,256]{2,1,0:T(8,128)(2,1)S(1)}, bf16[8,64,256]{2,1,0:T(8,128)(2,1)}, u32[]{:S(2)}, u32[]{:S(2)}) collective-permute-start(bf16[8,64,256]{2,1,0:T(8,128)(2,1)S(1)} %get-tuple-element.24), channel_id=1, source_target_pairs={{0,2},{1,3},{2,0},{3,1},{4,6},{5,7},{6,4},{7,5},{8,10},{9,11},{10,... | collective-permute-start | bytes 786440 | tf_op jit(solution)/shard_map/ppermute | solution.py:276
  104.8 11.2 %collective-permute-start.3 = (bf16[8,64,256]{2,1,0:T(8,128)(2,1)S(1)}, bf16[8,64,256]{2,1,0:T(8,128)(2,1)}, u32[]{:S(2)}, u32[]{:S(2)}) collective-permute-start(bf16[8,64,256]{2,1,0:T(8,128)(2,1)S(1)} %get-tuple-element.25), channel_id=1, source_target_pairs={{0,3},{1,0},{2,1},{3,2},{4,7},{5,4},{6,5},{7,6},{8,11},{9,8},{10,9... | collective-permute-start | bytes 786440 | tf_op jit(solution)/shard_map/ppermute | solution.py:276
  109.9 15.4 %collective-permute-start.22 = (bf16[3,8,64,256]{3,2,1,0:T(8,128)(2,1)}, bf16[3,8,64,256]{3,2,1,0:T(8,128)(2,1)}, u32[]{:S(2)}, u32[]{:S(2)}) collective-permute-start(bf16[3,8,64,256]{3,2,1,0:T(8,128)(2,1)} %pad_maximum_fusion.2.refs_2_), channel_id=1, source_target_pairs={{0,16},{4,20},{8,24},{12,28},{16,0},{20,4},{24,8},{28,12},{1,17},{... | collective-permute-start | bytes 2359304 | tf_op jit(solution)/shard_map/ppermute | solution.py:281
  111.3 61.3 %collective-permute-start.7 = (bf16[32,32,256]{2,1,0:T(8,128)(2,1)S(1)}, bf16[32,32,256]{2,1,0:T(8,128)(2,1)S(1)}, u32[]{:S(2)}, u32[]{:S(2)}) collective-permute-start(bf16[32,32,256]{2,1,0:T(8,128)(2,1)S(1)} %get-tuple-element.22.refs_1_), channel_id=1, source_target_pairs={{0,16},{4,20},{8,24},{12,28},{16,0},{20,4},{24,8},{28,12},{1,17},{... | collective-permute-start | bytes 1572872 | tf_op jit(solution)/shard_map/ppermute | solution.py:281
  115.9 37.3 %collective-permute-start.16 = (bf16[3,8,64,256]{3,2,1,0:T(8,128)(2,1)S(1)}, bf16[3,8,64,256]{3,2,1,0:T(8,128)(2,1)S(1)}, u32[]{:S(2)}, u32[]{:S(2)}) collective-permute-start(bf16[3,8,64,256]{3,2,1,0:T(8,128)(2,1)S(1)} %pad_maximum_fusion.1.refs_2_), channel_id=1, source_target_pairs={{0,16},{4,20},{8,24},{12,28},{16,0},{20,4},{24,8},{28,12},{1,17},{... | collective-permute-start | bytes 2359304 | tf_op jit(solution)/shard_map/ppermute | solution.py:281
  117.4 52.7 %collective-permute-start.10 = (bf16[3,8,64,256]{3,2,1,0:T(8,128)(2,1)S(1)}, bf16[3,8,64,256]{3,2,1,0:T(8,128)(2,1)S(1)}, u32[]{:S(2)}, u32[]{:S(2)}) collective-permute-start(bf16[3,8,64,256]{3,2,1,0:T(8,128)(2,1)S(1)} %pad_maximum_fusion.refs_2_), channel_id=1, source_target_pairs={{0,16},{4,20},{8,24},{12,28},{16,0},{20,4},{24,8},{28,12},{1,17},{... | collective-permute-start | bytes 2359304 | tf_op jit(solution)/shard_map/ppermute | solution.py:281
  118.9 101.2 %collective-permute-start.6 = (bf16[2,32,32,256]{3,2,1,0:T(8,128)(2,1)S(1)}, bf16[2,32,32,256]{3,2,1,0:T(8,128)(2,1)S(1)}, u32[]{:S(2)}, u32[]{:S(2)}) collective-permute-start(bf16[2,32,32,256]{3,2,1,0:T(8,128)(2,1)S(1)} %maximum_select_fusion.4), channel_id=1, source_target_pairs={{0,4},{4,0},{8,12},{12,8},{16,20},{20,16},{24,28},{28,24},{1,5},{5... | collective-permute-start | bytes 3145736 | tf_op jit(solution)/shard_map/ppermute | solution.py:281
  125.3 29.2 %copy-start.7 = (bf16[8,64,256]{2,1,0:T(8,128)(2,1)S(1)}, bf16[8,64,256]{2,1,0:T(8,128)(2,1)}, u32[]{:S(2)}) copy-start(bf16[8,64,256]{2,1,0:T(8,128)(2,1)} %copy-done.6) | copy-start | bytes 786436
  125.3 47.7 %collective-permute-start.29 = (bf16[3,8,64,256]{3,2,1,0:T(8,128)(2,1)S(1)}, bf16[3,8,64,256]{3,2,1,0:T(8,128)(2,1)S(1)}, u32[]{:S(2)}, u32[]{:S(2)}) collective-permute-start(bf16[3,8,64,256]{3,2,1,0:T(8,128)(2,1)S(1)} %get-tuple-element.36), channel_id=1, source_target_pairs={{0,8},{4,12},{8,0},{12,4},{16,24},{20,28},{24,16},{28,20},{1,9},{5... | collective-permute-start | bytes 2359304 | tf_op jit(solution)/shard_map/ppermute | solution.py:281
  153.3 21.3 %collective-permute-start.23 = (bf16[3,8,64,256]{3,2,1,0:T(8,128)(2,1)S(1)}, bf16[3,8,64,256]{3,2,1,0:T(8,128)(2,1)S(1)}, u32[]{:S(2)}, u32[]{:S(2)}) collective-permute-start(bf16[3,8,64,256]{3,2,1,0:T(8,128)(2,1)S(1)} %get-tuple-element.38), channel_id=1, source_target_pairs={{0,8},{4,12},{8,0},{12,4},{16,24},{20,28},{24,16},{28,20},{1,9},{5... | collective-permute-start | bytes 2359304 | tf_op jit(solution)/shard_map/ppermute | solution.py:281
  170.1 16.9 %collective-permute-start.17 = (bf16[3,8,64,256]{3,2,1,0:T(8,128)(2,1)S(1)}, bf16[3,8,64,256]{3,2,1,0:T(8,128)(2,1)S(1)}, u32[]{:S(2)}, u32[]{:S(2)}) collective-permute-start(bf16[3,8,64,256]{3,2,1,0:T(8,128)(2,1)S(1)} %get-tuple-element.40), channel_id=1, source_target_pairs={{0,8},{4,12},{8,0},{12,4},{16,24},{20,28},{24,16},{28,20},{1,9},{5... | collective-permute-start | bytes 2359304 | tf_op jit(solution)/shard_map/ppermute | solution.py:281
  172.6 47.1 %collective-permute-start.11 = (bf16[3,8,64,256]{3,2,1,0:T(8,128)(2,1)S(1)}, bf16[3,8,64,256]{3,2,1,0:T(8,128)(2,1)S(1)}, u32[]{:S(2)}, u32[]{:S(2)}) collective-permute-start(bf16[3,8,64,256]{3,2,1,0:T(8,128)(2,1)S(1)} %get-tuple-element.42), channel_id=1, source_target_pairs={{0,8},{4,12},{8,0},{12,4},{16,24},{20,28},{24,16},{28,20},{1,9},{5... | collective-permute-start | bytes 2359304 | tf_op jit(solution)/shard_map/ppermute | solution.py:281
  173.0 42.1 %collective-permute-start.8 = (bf16[32,32,256]{2,1,0:T(8,128)(2,1)S(1)}, bf16[32,32,256]{2,1,0:T(8,128)(2,1)S(1)}, u32[]{:S(2)}, u32[]{:S(2)}) collective-permute-start(bf16[32,32,256]{2,1,0:T(8,128)(2,1)S(1)} %broadcast_select_fusion.4), channel_id=1, source_target_pairs={{0,8},{4,12},{8,0},{12,4},{16,24},{20,28},{24,16},{28,20},{1,9},{5... | collective-permute-start | bytes 1572872 | tf_op jit(solution)/shard_map/ppermute | solution.py:281
  174.5 49.5 %collective-permute-start.30 = (bf16[2,3,8,64,256]{4,3,2,1,0:T(8,128)(2,1)S(1)}, bf16[2,3,8,64,256]{4,3,2,1,0:T(8,128)(2,1)S(1)}, u32[]{:S(2)}, u32[]{:S(2)}) collective-permute-start(bf16[2,3,8,64,256]{4,3,2,1,0:T(8,128)(2,1)S(1)} %maximum_select_fusion.3), channel_id=1, source_target_pairs={{0,4},{4,0},{8,12},{12,8},{16,20},{20,16},{24,28},{28,24},{1,5},{5... | collective-permute-start | bytes 4718600 | tf_op jit(solution)/shard_map/ppermute | solution.py:281
  187.0 47.2 %collective-permute-start.24 = (bf16[2,3,8,64,256]{4,3,2,1,0:T(8,128)(2,1)S(1)}, bf16[2,3,8,64,256]{4,3,2,1,0:T(8,128)(2,1)S(1)}, u32[]{:S(2)}, u32[]{:S(2)}) collective-permute-start(bf16[2,3,8,64,256]{4,3,2,1,0:T(8,128)(2,1)S(1)} %maximum_select_fusion.2), channel_id=1, source_target_pairs={{0,4},{4,0},{8,12},{12,8},{16,20},{20,16},{24,28},{28,24},{1,5},{5... | collective-permute-start | bytes 4718600 | tf_op jit(solution)/shard_map/ppermute | solution.py:281
  215.1 29.4 %collective-permute-start.18 = (bf16[2,3,8,64,256]{4,3,2,1,0:T(8,128)(2,1)S(1)}, bf16[2,3,8,64,256]{4,3,2,1,0:T(8,128)(2,1)S(1)}, u32[]{:S(2)}, u32[]{:S(2)}) collective-permute-start(bf16[2,3,8,64,256]{4,3,2,1,0:T(8,128)(2,1)S(1)} %maximum_select_fusion.1), channel_id=1, source_target_pairs={{0,4},{4,0},{8,12},{12,8},{16,20},{20,16},{24,28},{28,24},{1,5},{5... | collective-permute-start | bytes 4718600 | tf_op jit(solution)/shard_map/ppermute | solution.py:281
  219.7 4.4 %collective-permute-start.9 = (bf16[2,32,32,256]{3,2,1,0:T(8,128)(2,1)S(1)}, bf16[2,32,32,256]{3,2,1,0:T(8,128)(2,1)S(1)}, u32[]{:S(2)}, u32[]{:S(2)}) collective-permute-start(bf16[2,32,32,256]{3,2,1,0:T(8,128)(2,1)S(1)} %maximum_select_fusion.5), channel_id=1, source_target_pairs={{0,4},{4,0},{8,12},{12,8},{16,20},{20,16},{24,28},{28,24},{1,5},{5... | collective-permute-start | bytes 3145736 | tf_op jit(solution)/shard_map/ppermute | solution.py:281
  220.0 33.7 %collective-permute-start.12 = (bf16[2,3,8,64,256]{4,3,2,1,0:T(8,128)(2,1)S(1)}, bf16[2,3,8,64,256]{4,3,2,1,0:T(8,128)(2,1)S(1)}, u32[]{:S(2)}, u32[]{:S(2)}) collective-permute-start(bf16[2,3,8,64,256]{4,3,2,1,0:T(8,128)(2,1)S(1)} %maximum_select_fusion), channel_id=1, source_target_pairs={{0,4},{4,0},{8,12},{12,8},{16,20},{20,16},{24,28},{28,24},{1,5},{5... | collective-permute-start | bytes 4718600 | tf_op jit(solution)/shard_map/ppermute | solution.py:281
  (7 other events, 71.9 us)
where the time goes:
time: 264 us; the launch traced here: 263 us
  waiting for transfers between devices  137 us (52%)
  Pallas kernels  57.2 us (22%)
  starting transfers between devices  51.3 us (19%)
  other arithmetic  14.9 us (6%)
  local copies, waits for them, and re-layouts  2.68 us (1%)
    ppermute x18, waiting for transfers between devices, swapped(): return lax.ppermute(x, axis, [(i, i ^ bit) for i in range(devices)])  71.5 us
    ppermute x12, waiting for transfers between devices, shifted(): lax.ppermute(x, axis, [(i, (i + by) % devices) for i in range(devices)])  65.2 us
    pallas_call x4, Pallas kernels, pairs(): pl.pallas_call(body, grid=(size,), out_shape=jax.ShapeDtypeStruct((kept,...  38.9 us
    ppermute x18, starting transfers between devices, swapped(): return lax.ppermute(x, axis, [(i, i ^ bit) for i in range(devices)])  32.2 us
    pallas_call x2, Pallas kernels, spectra_part(): pl.pallas_call(functools.partial(spectra_kernel, {'halo': halo is not Non...  18.3 us
    ppermute x12, starting transfers between devices, shifted(): lax.ppermute(x, axis, [(i, (i + by) % devices) for i in range(devices)])  17 us
    another operation x4, other arithmetic, on_device(): own = jnp.stack(arrived)  6.57 us
  transfers between devices with their start and end apart: 31, of which 16 were waited for; matrix products, arithmetic and copies ran while one was open for 6% of the time, Pallas kernels for 18%

commit v1 on v0

v1 whole, which is shorter than its diff:
```python
import functools
import math

import jax
import jax.numpy as jnp
import numpy as np
from jax import lax
from jax.experimental import pallas as pl
from jax.experimental.pallas import tpu as pltpu
from jax.sharding import PartitionSpec as P

GROUP = 4
PAD = 8


def dft_tables(length):
    indices = np.arange(length)
    phase = 2.0 * np.pi / length * (indices[:, None] * indices[None, :] % length)
    cosine = np.cos(phase) / math.sqrt(length)
    sine = np.sin(phase) / math.sqrt(length)
    upper = np.concatenate([cosine, sine], axis=1)
    lower = np.concatenate([-sine, cosine], axis=1)
    table = np.concatenate([upper, lower], axis=0).astype(np.float32)
    high = table.astype(jnp.bfloat16)
    low = (table - high.astype(np.float32)).astype(jnp.bfloat16)
    return np.stack([high, low])


def spectra_kernel(place, groups, kept, cuts, merge, *refs):
    refs = list(refs)
    me_ref = refs.pop(0)
    here, after = refs.pop(0), refs.pop(0)
    halo = refs.pop(0) if place["halo"] else None
    window, table = refs.pop(0), refs.pop(0)
    earlier = refs.pop(0) if merge else None
    store = refs.pop()
    own_ref = refs.pop(0)
    outs = refs
    step = pl.program_id(0)
    channels = window.shape[1]
    taps = window.shape[0]
    inputs = here.shape[1]
    frames = groups * GROUP
    rows = 2 * frames
    lane_tiles = inputs // 128

    def run(tail):
        weights = [window[t : t + 1, :] for t in range(taps)]
        filtered = []
        for part in range(2):
            loaded = [here[part, :, i * channels : (i + 1) * channels] for i in range(GROUP)]
            loaded += [tail[part, :, i * channels : (i + 1) * channels] for i in range(taps - 1)]
            loaded = [x.astype(jnp.float32) for x in loaded]
            filtered.append(
                [sum(weights[t] * loaded[i + t] for t in range(taps)) for i in range(GROUP)]
            )
        for i in range(GROUP):
            both = jnp.concatenate([filtered[0][i], filtered[1][i]], axis=1)
            high = both.astype(jnp.bfloat16)
            low = (both - high.astype(jnp.float32)).astype(jnp.bfloat16)
            nt = functools.partial(
                lax.dot_general,
                dimension_numbers=(((1,), (1,)), ((), ())),
                preferred_element_type=jnp.float32,
            )
            out = nt(table[0], high) + (nt(table[1], high) + nt(table[0], low))
            for part in range(2):
                first = part * frames + step * GROUP + i
                for lane in range(lane_tiles):
                    store[lane, pl.ds(first, channels, stride=rows + PAD), :] = out[
                        part * channels : (part + 1) * channels, lane * 128 : (lane + 1) * 128
                    ]

    if halo is None:
        run(after)
    else:
        last = pl.num_programs(0) - 1

        @pl.when(step < last)
        def _():
            run(after)

        @pl.when(step == last)
        def _():
            run(halo)

    @pl.when(step == pl.num_programs(0) - 1)
    def _():
        devices = channels // kept

        def piece(channel):
            start = pl.multiple_of(channel * (rows + PAD), 8)
            got = [store[lane, pl.ds(start, rows), :] for lane in range(lane_tiles)]
            return jnp.concatenate(got, axis=1).astype(jnp.bfloat16)

        me = me_ref[0]

        def own(i, carry):
            own_ref[i] = piece(me * kept + i)
            return carry

        lax.fori_loop(0, kept, own, 0, unroll=2)
        for number, cut in enumerate(cuts):
            at = 0
            for hop, first, size in cut:
                base = (me ^ hop) * kept + first

                def one(i, carry, out=outs[number], at=at, base=base, hop=hop, first=first):
                    if merge:
                        out[at + i, :rows, :] = earlier[hop - 1, first + i]
                        out[at + i, rows:, :] = piece(base + i)
                    else:
                        out[at + i] = piece(base + i)
                    return carry

                lax.fori_loop(0, size, one, 0, unroll=2)
                at += size


def spectra_part(voltages, halo, window, table, me, devices, first, groups, cuts, earlier):
    parts, inputs, samples = voltages.shape
    channels = window.shape[1]
    kept = channels // devices
    rows = 2 * groups * GROUP
    width = GROUP * channels
    last = samples // width - 1
    merge = earlier is not None
    operands = [me, voltages, voltages]
    in_specs = [
        pl.BlockSpec(memory_space=pltpu.SMEM),
        pl.BlockSpec((2, inputs, width), lambda i: (0, 0, first + i)),
        pl.BlockSpec((2, inputs, width), lambda i: (0, 0, jnp.minimum(first + i + 1, last))),
    ]
    whole = lambda shape: pl.BlockSpec(shape, lambda i: (0,) * len(shape))
    if halo is not None:
        operands.append(halo)
        in_specs.append(whole(halo.shape))
    operands += [window, table]
    in_specs += [whole(window.shape), whole(table.shape)]
    shapes = [(kept, rows, inputs)]
    if merge:
        operands.append(earlier)
        in_specs.append(whole(earlier.shape))
    depth = 2 * rows if merge else rows
    shapes += [(sum(size for _, _, size in cut), depth, inputs) for cut in cuts]
    return pl.pallas_call(
        functools.partial(
            spectra_kernel, {"halo": halo is not None}, groups, kept, cuts, merge
        ),
        grid=(groups,),
        out_shape=[jax.ShapeDtypeStruct(s, jnp.bfloat16) for s in shapes],
        in_specs=in_specs,
        out_specs=[whole(s) for s in shapes],
        scratch_shapes=[pltpu.VMEM((inputs // 128, channels * (rows + PAD), 128), jnp.float32)],
        compiler_params=pltpu.CompilerParams(
            vmem_limit_bytes=48 * 1024 * 1024, dimension_semantics=("arbitrary",)
        ),
        cost_estimate=pl.CostEstimate(
            flops=2 * 3 * 4 * channels * channels * inputs * groups * GROUP,
            bytes_accessed=2 * voltages.size,
            transcendentals=0,
        ),
    )(*operands)


def pairs_kernel(scale, half, count, step, *refs):
    out = refs[-1]
    per_block = [refs[n * count : (n + 1) * count] for n in range(half + 1)]
    for channel in range(step):

        def pieces(block):
            got = []
            for ref in per_block[block]:
                if ref.ndim == 3:
                    got.append(ref[channel])
                else:
                    got += [ref[m, channel] for m in range(ref.shape[0])]
            return got

        mine = pieces(0)
        turned = []
        for value in mine:
            size = 2 * PART_FRAMES
            for first in range(0, value.shape[0], size):
                turned.append(value[first + PART_FRAMES : first + size])
                turned.append(-value[first : first + PART_FRAMES])
        left = jnp.concatenate(mine, axis=0).T
        left_turned = jnp.concatenate(turned, axis=0).T
        width = left.shape[0]
        for block in range(half + 1):
            right = jnp.concatenate(pieces(block), axis=0)
            columns = slice(block * width, (block + 1) * width)
            out[channel, 0, :, columns] = (
                jnp.dot(left, right, preferred_element_type=jnp.float32) * scale
            )
            out[channel, 1, :, columns] = (
                jnp.dot(left_turned, right, preferred_element_type=jnp.float32) * scale
            )


PART_FRAMES = 16


def pairs(blocks, total, first, size, kept, scale):
    half = len(blocks) - 1
    inputs = blocks[0][0][0].shape[-1]
    operands, in_specs = [], []
    count = len(blocks[0])
    offsets = [offset for block in blocks for _, _, offset in block]
    step = 2 if all(x % 2 == 0 for x in [size, first, *offsets]) else 1
    for block in blocks:
        for array, stack, offset in block:
            operands.append(array)
            rows = array.shape[-2]
            at = offset // step
            lead = array.shape[:-3] if stack is None else array.shape[1:-3]
            zeros = (0,) * len(lead)
            if stack is None:
                shape, index = (*lead, step, rows, inputs), lambda i, a=at, z=zeros: (*z, a + i, 0, 0)
            else:
                shape = (None, *lead, step, rows, inputs)
                index = lambda i, a=at, s=stack, z=zeros: (s, *z, a + i, 0, 0)
            in_specs.append(pl.BlockSpec(shape, index))
    depth = sum(math.prod(x.shape[:-3] if st is None else x.shape[1:-3]) * x.shape[-2] for x, st, _ in blocks[0])
    slots = (half + 1) * inputs
    aliases = {}
    if total is not None:
        aliases = {len(operands): 0}
        operands.append(total)
        in_specs.append(pl.BlockSpec(memory_space=pl.ANY))

    def body(*refs):
        refs = list(refs)
        if total is not None:
            refs.pop(-2)
        pairs_kernel(scale, half, count, step, *refs)

    return pl.pallas_call(
        body,
        grid=(size // step,),
        out_shape=jax.ShapeDtypeStruct((kept, 2, inputs, slots), jnp.float32),
        in_specs=in_specs,
        out_specs=pl.BlockSpec((step, 2, inputs, slots), lambda i: (first // step + i, 0, 0, 0)),
        input_output_aliases=aliases,
        compiler_params=pltpu.CompilerParams(
            vmem_limit_bytes=32 * 1024 * 1024, dimension_semantics=("arbitrary",)
        ),
        cost_estimate=pl.CostEstimate(
            flops=2 * size * 2 * inputs * slots * depth,
            bytes_accessed=size * 2 * inputs * slots * 4,
            transcendentals=0,
        ),
    )(*operands)


def shifted(x, axis, by):
    devices = lax.axis_size(axis)
    return lax.ppermute(x, axis, [(i, (i + by) % devices) for i in range(devices)])


def swapped(x, axis, bit):
    devices = lax.axis_size(axis)
    return lax.ppermute(x, axis, [(i, i ^ bit) for i in range(devices)])


def after(x, *earlier):
    return lax.optimization_barrier((x, *earlier))[0]


def partners(own, axis):
    devices = lax.axis_size(axis)
    return [(own, None)] + [(shifted(own, axis, -hop), None) for hop in range(1, devices // 2 + 1)]


def tick(x, *earlier):
    x = lax.optimization_barrier((x, *earlier))[0]

    def body(x_ref, out_ref):
        out_ref[...] = x_ref[...] + 1.0

    return pl.pallas_call(
        body,
        out_shape=jax.ShapeDtypeStruct(x.shape, x.dtype),
        cost_estimate=pl.CostEstimate(
            flops=10**15, bytes_accessed=2 * x.size * 4, transcendentals=0
        ),
    )(x)


def after(x, *earlier):
    return lax.optimization_barrier((x, *earlier))[0]


class Exchange:
    def __init__(self, own, axis):
        self.own, self.axis = own, axis
        place = lax.axis_index(axis)
        self.is_far = (place & 2) == 2
        self.is_odd = (place & 1) == 1

    def y(self, *earlier):
        self.over_y = swapped(after(self.own, *earlier), self.axis, 4)

    def x(self, *earlier):
        own, over_y = lax.optimization_barrier((self.own, self.over_y, *earlier))[:2]
        self.over_x = swapped(jnp.where(self.is_far, own, over_y), self.axis, 2)

    def for_core(self, *earlier):
        own, over_x, over_y = lax.optimization_barrier(
            (self.own, self.over_x, self.over_y, *earlier)
        )[:3]
        return [jnp.where(self.is_odd, own, over_x), jnp.where(self.is_odd, over_x, over_y)]

    def core(self, *earlier):
        sent = jnp.stack(self.for_core(*earlier))
        self.over_core, self.slots = swapped(sent, self.axis, 1), (0, 1)

    def blocks(self):
        return [
            (self.own, None),
            (self.over_core, self.slots[0]),
            (self.over_x, None),
            (self.over_core, self.slots[1]),
            (self.over_y, None),
        ]


def core_of_both(a, b, *earlier):
    sent = jnp.stack(a.for_core(*earlier) + b.for_core(*earlier))
    a.over_core = b.over_core = swapped(sent, a.axis, 1)
    a.slots, b.slots = (0, 1), (2, 3)


def on_device(voltages, window):
    tap_count, channels = window.shape
    frames_dev = voltages.shape[2] // channels
    devices = lax.axis_size("tf")
    kept = channels // devices
    planned = devices == 4 and lax.axis_size("inp") == 8 and kept == 32
    sizes = [6, 6, 6, 6, 4, 4] if planned else [kept]
    nears = [12, 12, 8] if planned else [kept]
    count = len(sizes)
    firsts = [sum(sizes[:q]) for q in range(count)]
    near_firsts = [sum(nears[:h]) for h in range(len(nears))]
    cuts = [[(1, first, size)] for first, size in zip(near_firsts, nears)]
    for hop in range(2, devices):
        cuts += [[(hop, first, size)] for first, size in zip(firsts, sizes)]
    rest_cuts = [[(hop, 0, kept) for hop in range(1, devices)]]
    groups = frames_dev // GROUP // 2
    leading = voltages[:, :, : (tap_count - 1) * channels]
    halo = lax.ppermute(leading, "tf", [(i, i - 1) for i in range(1, devices)])
    table = jnp.asarray(dft_tables(channels))
    me = lax.axis_index("tf").astype(jnp.int32).reshape(1)
    own_a, rest = spectra_part(
        voltages, None, window, table, me, devices, 0, groups, rest_cuts, None
    )
    rest = rest.reshape(devices - 1, kept, *rest.shape[1:])
    own_b, *pieces = spectra_part(
        voltages, halo, window, table, me, devices, groups, groups, cuts, rest
    )
    near = pieces[: len(nears)]
    far = [pieces[len(nears) + q :: count] for q in range(count)]
    scale = 1.0 / math.sqrt(frames_dev * devices)

    def run_pairs(total, q, *groups_):
        blocks = [
            [(*entry, at) for entry, (_, at) in zip(entries, groups_)]
            for entries in zip(*[g for g, _ in groups_])
        ]
        return pairs(blocks, total, firsts[q], sizes[q], kept, scale)

    if not planned:
        near = swapped(near[0], "tf", 1)
        far = jnp.stack([swapped(x, "tf", hop + 2) for hop, x in enumerate(far[0])])
        return run_pairs(None, 0, *[(partners(x, "inp"), 0) for x in (own_a, own_b, near, far)])

    def over_z(q, *earlier):
        sent = lax.optimization_barrier((*far[q], *earlier))
        return [swapped(sent[hop - 2], "tf", hop) for hop in range(2, devices)]

    near_over_z = lambda h, *earlier: swapped(after(near[h], *earlier), "tf", 1)
    exchange = lambda *parts: Exchange(jnp.concatenate(parts), "inp")
    a, b = Exchange(own_a, "inp"), Exchange(own_b, "inp")
    t = jnp.zeros((8, 128), jnp.float32)

    def chunk(q):
        h = max(i for i, first in enumerate(near_firsts) if first <= firsts[q])
        at = nears[q] if q < len(nears) else 0
        return run_pairs(
            total,
            q,
            (a.blocks(), firsts[q]),
            (b.blocks(), firsts[q]),
            (lines[h].blocks(), firsts[q] - near_firsts[h]),
            (lines[q].blocks(), at),
            (lines[q].blocks(), at + sizes[q]),
        )

    total = None
    a.y()
    t = tick(t, own_b[:1, :8, :128])
    z, n, lines = [over_z(0, t)], [near_over_z(0, t)], []
    b.y(t)
    a.x(t)
    t = tick(t, *z[0])
    z.append(over_z(1, t))
    n.append(near_over_z(1, n[0], t))
    lines.append(exchange(n[0], *z[0]))
    lines[0].y(b.over_y, t)
    b.x(a.over_x, t)
    t = tick(t, *z[1], b.over_y, a.over_x)
    z.append(over_z(2, t))
    n.append(near_over_z(2, n[1], t))
    lines.append(exchange(n[1], *z[1]))
    lines[1].y(lines[0].over_y, t)
    lines[0].x(b.over_x, t)
    t = tick(t, *z[2], lines[0].over_y, b.over_x)
    z.append(over_z(3, t))
    lines.append(exchange(n[2], *z[2]))
    lines[2].y(lines[1].over_y, t)
    lines[1].x(lines[0].over_x, t)
    core_of_both(a, b, t)
    t = tick(t, *z[3], lines[1].over_y, lines[0].over_x)
    z.append(over_z(4, t))
    lines.append(exchange(*z[3]))
    lines[3].y(lines[2].over_y, t)
    lines[2].x(lines[1].over_x, t)
    lines[0].core(a.over_core, t)
    t = tick(t, *z[4], lines[2].over_y, lines[1].over_x, a.over_core)
    z.append(over_z(5, t))
    lines.append(exchange(*z[4]))
    lines[4].y(lines[3].over_y, t)
    lines[3].x(lines[2].over_x, t)
    total = chunk(0)
    lines[1].core(lines[0].over_core, t, total)
    t = tick(t, *z[5], lines[3].over_y, lines[2].over_x, lines[0].over_core)
    lines.append(exchange(*z[5]))
    lines[5].y(lines[4].over_y, t)
    lines[4].x(lines[3].over_x, t)
    lines[2].core(lines[1].over_core, t)
    total = chunk(1)
    t = tick(t, lines[4].over_y, lines[3].over_x, lines[1].over_core, total)
    lines[5].x(lines[4].over_x, t)
    lines[3].core(lines[2].over_core, t)
    total = chunk(2)
    t = tick(t, lines[5].over_y, lines[4].over_x, lines[2].over_core, total)
    core_of_both(lines[4], lines[5], t, lines[3].over_core)
    total = chunk(3)
    total = chunk(4)
    total = chunk(5)
    return total


def solution(mesh):
    in_specs = (P(None, "inp", "tf"), P())
    out_specs = P("tf", None, "inp", None)
    return jax.shard_map(
        on_device, mesh=mesh, in_specs=in_specs, out_specs=out_specs, check_vma=False
    )
```

time: 264 us -> 179 us (0.68)
  waiting for transfers between devices: 137 us -> 84.9 us
  starting transfers between devices: 51.3 us -> 38.3 us
  other arithmetic: 14.9 us -> 2.11 us
  Pallas kernels: 57.2 us -> 47.7 us
    ppermute x12 -> x0, waiting for transfers between devices: 65.2 us -> none  [shifted(): lax.ppermute(x, axis, [(i, (i + by) % devices) for i in range(devices)])]
    ppermute x12 -> x0, starting transfers between devices: 17 us -> none  [shifted(): lax.ppermute(x, axis, [(i, (i + by) % devices) for i in range(devices)])]
    ppermute x18 -> x37, waiting for transfers between devices: 71.5 us -> 83.5 us  [swapped(): return lax.ppermute(x, axis, [(i, i ^ bit) for i in range(devices)])]
    another operation x8 -> x13, other arithmetic: 11.5 us -> 1.65 us  [the longest x8 0.93 us: core(): sent = jnp.stack(self.for_core(*earlier))]
    pallas_call x2, Pallas kernels: 18.3 us -> 11.4 us  [spectra_part(): pl.pallas_call(functools.partial(spectra_kernel, {'halo': halo is not Non...]
    ppermute x18 -> x37, starting transfers between devices: 32.2 us -> 36.2 us  [swapped(): return lax.ppermute(x, axis, [(i, i ^ bit) for i in range(devices)])]
    select_n x8, other arithmetic: 3.31 us -> 0.46 us  [x(): self.over_x = swapped(jnp.where(self.is_far, own, over_y), self.axis, 2)]
    pallas_call x4 -> x6, Pallas kernels: 38.9 us -> 36.2 us  [pairs(): pl.pallas_call(body, grid=(size // step,), out_shape=jax.ShapeDtypeStruct...]
  transfers between devices with their start and end apart: 31 -> 38, of which waited for: 16 -> 20; matrix products, arithmetic and copies ran while one was open for 6% -> 1% of each run, Pallas kernels for 18% -> 21%
where the time goes in v1:
time: 179 us; the launch traced here: 177 us
  waiting for transfers between devices  84.9 us (47%)
  Pallas kernels  47.7 us (27%)
  starting transfers between devices  38.3 us (21%)
  local copies, waits for them, and re-layouts  3.64 us (2%)
  other arithmetic  2.11 us (1%)
    ppermute x37, waiting for transfers between devices, swapped(): return lax.ppermute(x, axis, [(i, i ^ bit) for i in range(devices)])  83.5 us
    pallas_call x6, Pallas kernels, pairs(): pl.pallas_call(body, grid=(size // step,), out_shape=jax.ShapeDtypeStruct...  36.2 us
    ppermute x37, starting transfers between devices, swapped(): return lax.ppermute(x, axis, [(i, i ^ bit) for i in range(devices)])  36.2 us
    pallas_call x2, Pallas kernels, spectra_part(): pl.pallas_call(functools.partial(spectra_kernel, {'halo': halo is not Non...  11.4 us
  transfers between devices with their start and end apart: 38, of which 20 were waited for; matrix products, arithmetic and copies ran while one was open for 1% of the time, Pallas kernels for 21%

profile of v1, /device:TPU:17, one launch (start us, length us, event | category | flops | bytes accessed | tf_op | source)
XLA Modules:
  0.0 176.9 jit_solution(4586306570853307972)
XLA Ops:
  0.0 1.8 %slice.4 = bf16[2,256,384]{2,1,0:T(8,128)(2,1)} slice(bf16[2,256,4096]{2,1,0:T(8,128)(2,1)} %refs_2_.3), slice={[0:2], [0:256], [0:384]} | slice | bytes 786432 | tf_op jit(solution)/shard_map/slice | solution.py:350
  1.8 2.1 %collective-permute-start = (bf16[2,256,384]{2,1,0:T(8,128)(2,1)}, bf16[2,256,384]{2,1,0:T(8,128)(2,1)S(1)}, u32[]{:S(2)}, u32[]{:S(2)}) collective-permute-start(bf16[2,256,384]{2,1,0:T(8,128)(2,1)} %slice.4), channel_id=1, source_target_pairs={{1,0},{2,1},{3,2},{5,4},{6,5},{7,6},{9,8},{10,9},{11,10},{13,12},{... | collective-permute-start | bytes 1179656 | tf_op jit(solution)/shard_map/ppermute | solution.py:351
  5.5 5.7 %shard_map.37 = (bf16[32,32,256]{2,1,0:T(8,128)(2,1)S(1)}, bf16[96,32,256]{2,1,0:T(8,128)(2,1)S(1)}) custom-call(s32[1]{0:T(128)} %bitcast.refs_0_, bf16[2,256,4096]{2,1,0:T(8,128)(2,1)} %refs_2_.3, bf16[2,256,4096]{2,1,0:T(8,128)(2,1)} %refs_2_.3, f32[4,128]{1,0:T(4,128)S(1)} %copy-done.2, bf16[2,256,256]{2,1,0:T(8,128)(2,1)S(1)} %copy-done), custom_call_target="tpu_custom_call" | custom-call | flops 1610612736 | bytes 4194304 | tf_op jit(solution)/shard_map/pallas_call | solution.py:146
  13.9 5.8 %shard_map.38 = (bf16[32,32,256]{2,1,0:T(8,128)(2,1)S(1)}, bf16[12,64,256]{2,1,0:T(8,128)(2,1)S(1)}, bf16[12,64,256]{2,1,0:T(8,128)(2,1)S(1)}, bf16[8,64,256]{2,...) custom-call(s32[1]{0:T(128)} %bitcast.refs_0_, ...), custom_call_target="tpu_custom_call" | custom-call | flops 1610612736 | bytes 4194304 | tf_op jit(solution)/shard_map/pallas_call | solution.py:146
  21.5 3.0 %collective-permute-start.1 = (bf16[12,64,256]{2,1,0:T(8,128)(2,1)S(1)}, bf16[12,64,256]{2,1,0:T(8,128)(2,1)S(1)}, u32[]{:S(2)}, u32[]{:S(2)}) collective-permute-start(bf16[12,64,256]{2,1,0:T(8,128)(2,1)S(1)} %get-tuple-element.99), channel_id=1, source_target_pairs={{0,1},{1,0},{2,3},{3,2},{4,5},{5,4},{6,7},{7,6},{8,9},{9,8},{10,11... | collective-permute-start | bytes 1179656 | tf_op jit(solution)/shard_map/ppermute | solution.py:263
  25.8 6.1 %collective-permute-done.2 = bf16[6,64,256]{2,1,0:T(8,128)(2,1)S(1)} collective-permute-done((bf16[6,64,256]{2,1,0:T(8,128)(2,1)S(1)}, bf16[6,64,256]{2,1,0:T(8,128)(2,1)S(1)}, u32[]{:S(2)}, u32[]{:S(2)}) %collective-permute-start.2) | collective-permute-done | bytes 196640 | tf_op jit(solution)/shard_map/ppermute | solution.py:263
  31.9 5.7 %collective-permute-done.3 = bf16[6,64,256]{2,1,0:T(8,128)(2,1)S(1)} collective-permute-done((bf16[6,64,256]{2,1,0:T(8,128)(2,1)S(1)}, bf16[6,64,256]{2,1,0:T(8,128)(2,1)S(1)}, u32[]{:S(2)}, u32[]{:S(2)}) %collective-permute-start.3) | collective-permute-done | bytes 196640 | tf_op jit(solution)/shard_map/ppermute | solution.py:263
  38.9 3.7 %collective-permute-start.4 = (bf16[12,64,256]{2,1,0:T(8,128)(2,1)S(1)}, bf16[12,64,256]{2,1,0:T(8,128)(2,1)S(1)}, u32[]{:S(2)}, u32[]{:S(2)}) collective-permute-start(bf16[12,64,256]{2,1,0:T(8,128)(2,1)S(1)} %get-tuple-element.105), channel_id=1, source_target_pairs={{0,1},{1,0},{2,3},{3,2},{4,5},{5,4},{6,7},{7,6},{8,9},{9,8},{10,11... | collective-permute-start | bytes 1179656 | tf_op jit(solution)/shard_map/ppermute | solution.py:263
  44.4 2.7 %collective-permute-done.5 = bf16[6,64,256]{2,1,0:T(8,128)(2,1)S(1)} collective-permute-done((bf16[6,64,256]{2,1,0:T(8,128)(2,1)S(1)}, bf16[6,64,256]{2,1,0:T(8,128)(2,1)S(1)}, u32[]{:S(2)}, u32[]{:S(2)}) %collective-permute-start.5) | collective-permute-done | bytes 196640 | tf_op jit(solution)/shard_map/ppermute | solution.py:263
  47.1 8.0 %collective-permute-done.6 = bf16[6,64,256]{2,1,0:T(8,128)(2,1)S(1)} collective-permute-done((bf16[6,64,256]{2,1,0:T(8,128)(2,1)S(1)}, bf16[6,64,256]{2,1,0:T(8,128)(2,1)S(1)}, u32[]{:S(2)}, u32[]{:S(2)}) %collective-permute-start.6) | collective-permute-done | bytes 196640 | tf_op jit(solution)/shard_map/ppermute | solution.py:263
  55.4 3.4 %collective-permute-done.4 = bf16[12,64,256]{2,1,0:T(8,128)(2,1)S(1)} collective-permute-done((bf16[12,64,256]{2,1,0:T(8,128)(2,1)S(1)}, bf16[12,64,256]{2,1,0:T(8,128)(2,1)S(1)}, u32[]{:S(2)}, u32[]{:S(2)}) %collective-permute-start.4) | collective-permute-done | bytes 393248 | tf_op jit(solution)/shard_map/ppermute | solution.py:263
  58.8 2.2 %collective-permute-start.10 = (bf16[8,64,256]{2,1,0:T(8,128)(2,1)S(1)}, bf16[8,64,256]{2,1,0:T(8,128)(2,1)S(1)}, u32[]{:S(2)}, u32[]{:S(2)}) collective-permute-start(bf16[8,64,256]{2,1,0:T(8,128)(2,1)S(1)} %get-tuple-element.114), channel_id=1, source_target_pairs={{0,1},{1,0},{2,3},{3,2},{4,5},{5,4},{6,7},{7,6},{8,9},{9,8},{10,11... | collective-permute-start | bytes 786440 | tf_op jit(solution)/shard_map/ppermute | solution.py:263
  61.1 9.8 %collective-permute-done.10 = bf16[8,64,256]{2,1,0:T(8,128)(2,1)S(1)} collective-permute-done((bf16[8,64,256]{2,1,0:T(8,128)(2,1)S(1)}, bf16[8,64,256]{2,1,0:T(8,128)(2,1)S(1)}, u32[]{:S(2)}, u32[]{:S(2)}) %collective-permute-start.10) | collective-permute-done | bytes 262176 | tf_op jit(solution)/shard_map/ppermute | solution.py:263
  71.6 2.4 %collective-permute-start.18 = (bf16[24,64,256]{2,1,0:T(8,128)(2,1)S(1)}, bf16[24,64,256]{2,1,0:T(8,128)(2,1)S(1)}, u32[]{:S(2)}, u32[]{:S(2)}) collective-permute-start(bf16[24,64,256]{2,1,0:T(8,128)(2,1)S(1)} %broadcast_select_fusion.1), channel_id=1, source_target_pairs={{0,8},{4,12},{8,0},{12,4},{16,24},{20,28},{24,16},{28,20},{1,9},{5... | collective-permute-start | bytes 2359304 | tf_op jit(solution)/shard_map/ppermute | solution.py:263
  74.6 2.2 %collective-permute-start.16 = (bf16[6,64,256]{2,1,0:T(8,128)(2,1)S(1)}, bf16[6,64,256]{2,1,0:T(8,128)(2,1)S(1)}, u32[]{:S(2)}, u32[]{:S(2)}) collective-permute-start(bf16[6,64,256]{2,1,0:T(8,128)(2,1)S(1)} %get-tuple-element.128), channel_id=1, source_target_pairs={{0,3},{1,2},{2,1},{3,0},{4,7},{5,6},{6,5},{7,4},{8,11},{9,10},{10,... | collective-permute-start | bytes 589832 | tf_op jit(solution)/shard_map/ppermute | solution.py:263
  77.3 2.1 %collective-permute-start.23 = (bf16[4,32,32,256]{3,2,1,0:T(8,128)(2,1)S(1)}, bf16[4,32,32,256]{3,2,1,0:T(8,128)(2,1)S(1)}, u32[]{:S(2)}, u32[]{:S(2)}) collective-permute-start(bf16[4,32,32,256]{3,2,1,0:T(8,128)(2,1)S(1)} %pad_maximum_fusion), channel_id=1, source_target_pairs={{0,4},{4,0},{8,12},{12,8},{16,20},{20,16},{24,28},{28,24},{1,5},{5... | collective-permute-start | bytes 6291464 | tf_op jit(solution)/shard_map/ppermute | solution.py:263
  80.1 14.5 %collective-permute-done.16 = bf16[6,64,256]{2,1,0:T(8,128)(2,1)S(1)} collective-permute-done((bf16[6,64,256]{2,1,0:T(8,128)(2,1)S(1)}, bf16[6,64,256]{2,1,0:T(8,128)(2,1)S(1)}, u32[]{:S(2)}, u32[]{:S(2)}) %collective-permute-start.16) | collective-permute-done | bytes 196640 | tf_op jit(solution)/shard_map/ppermute | solution.py:263
  95.9 8.4 %collective-permute-done.19 = bf16[4,64,256]{2,1,0:T(8,128)(2,1)S(1)} collective-permute-done((bf16[4,64,256]{2,1,0:T(8,128)(2,1)S(1)}, bf16[4,64,256]{2,1,0:T(8,128)(2,1)S(1)}, u32[]{:S(2)}, u32[]{:S(2)}) %collective-permute-start.19) | collective-permute-done | bytes 131104 | tf_op jit(solution)/shard_map/ppermute | solution.py:263
  104.3 2.9 %collective-permute-done.20 = bf16[4,64,256]{2,1,0:T(8,128)(2,1)S(1)} collective-permute-done((bf16[4,64,256]{2,1,0:T(8,128)(2,1)S(1)}, bf16[4,64,256]{2,1,0:T(8,128)(2,1)S(1)}, u32[]{:S(2)}, u32[]{:S(2)}) %collective-permute-start.20) | collective-permute-done | bytes 131104 | tf_op jit(solution)/shard_map/ppermute | solution.py:263
  107.3 3.0 %collective-permute-done.21.refs_23_.refs_24_.refs_22_ = bf16[20,64,256]{2,1,0:T(8,128)(2,1)S(1)} collective-permute-done((bf16[20,64,256]{2,1,0:T(8,128)(2,1)S(1)}, bf16[20,64,256]{2,1,0:T(8,128)(2,1)S(1)}, u32[]{:S(2)}, u32[]{:S(2)}) %collective-permute-start.21) | collective-permute-done | bytes 655392 | tf_op jit(solution)/shard_map/ppermute | solution.py:263
  111.1 2.0 %collective-permute-done.22.refs_13_.refs_14_.refs_12_ = bf16[24,64,256]{2,1,0:T(8,128)(2,1)S(1)} collective-permute-done((bf16[24,64,256]{2,1,0:T(8,128)(2,1)S(1)}, bf16[24,64,256]{2,1,0:T(8,128)(2,1)S(1)}, u32[]{:S(2)}, u32[]{:S(2)}) %collective-permute-start.22) | collective-permute-done | bytes 786464 | tf_op jit(solution)/shard_map/ppermute | solution.py:263
  113.9 1.9 %collective-permute-start.27 = (bf16[2,24,64,256]{3,2,1,0:T(8,128)(2,1)S(1)}, bf16[2,24,64,256]{3,2,1,0:T(8,128)(2,1)S(1)}, u32[]{:S(2)}, u32[]{:S(2)}) collective-permute-start(bf16[2,24,64,256]{3,2,1,0:T(8,128)(2,1)S(1)} %pad_maximum_fusion.1), channel_id=1, source_target_pairs={{0,4},{4,0},{8,12},{12,8},{16,20},{20,16},{24,28},{28,24},{1,5},{5... | collective-permute-start | bytes 4718600 | tf_op jit(solution)/shard_map/ppermute | solution.py:263
  115.8 3.3 %collective-permute-done.29.refs_23_.refs_24_ = bf16[12,64,256]{2,1,0:T(8,128)(2,1)S(1)} collective-permute-done((bf16[12,64,256]{2,1,0:T(8,128)(2,1)S(1)}, bf16[12,64,256]{2,1,0:T(8,128)(2,1)S(1)}, u32[]{:S(2)}, u32[]{:S(2)}) %collective-permute-start.29) | collective-permute-done | bytes 393248 | tf_op jit(solution)/shard_map/ppermute | solution.py:263
  120.0 8.1 %collective-permute-done.26.refs_13_.refs_14_.refs_12_ = bf16[20,64,256]{2,1,0:T(8,128)(2,1)S(1)} collective-permute-done((bf16[20,64,256]{2,1,0:T(8,128)(2,1)S(1)}, bf16[20,64,256]{2,1,0:T(8,128)(2,1)S(1)}, u32[]{:S(2)}, u32[]{:S(2)}) %collective-permute-start.26) | collective-permute-done | bytes 655392 | tf_op jit(solution)/shard_map/ppermute | solution.py:263
  128.4 1.6 collective-permute-done.25
  130.1 6.6 %shard_map.39.refs_25_ = f32[32,2,256,1280]{3,2,1,0:T(8,128)} custom-call(bf16[32,32,256]{2,1,0:T(8,128)(2,1)S(1)} %get-tuple-element.140.refs_0_, bf16[32,32,256]{2,1,0:T(8,128)(2,1)S(1)} %get-tuple-element.143.refs_1_, bf16[24,64,256]{2,1,0:T(8,128)(2,1)S(1)} %constant_dynamic-update-slice_fusion.3.refs_2_.refs_3_.refs_4_, ...), custom_call_target="tpu_custom_call" | custom-call | flops 2013265920 | bytes 15728640 | tf_op jit(solution)/shard_map/pallas_call | solution.py:238
  137.0 2.9 %collective-permute-start.28 = (bf16[2,24,64,256]{3,2,1,0:T(8,128)(2,1)S(1)}, bf16[2,24,64,256]{3,2,1,0:T(8,128)(2,1)S(1)}, u32[]{:S(2)}, u32[]{:S(2)}) collective-permute-start(bf16[2,24,64,256]{3,2,1,0:T(8,128)(2,1)S(1)} %pad_maximum_fusion.2), channel_id=1, source_target_pairs={{0,4},{4,0},{8,12},{12,8},{16,20},{20,16},{24,28},{28,24},{1,5},{5... | collective-permute-start | bytes 4718600 | tf_op jit(solution)/shard_map/ppermute | solution.py:263
  142.9 6.6 %shard_map.40.refs_25_ = f32[32,2,256,1280]{3,2,1,0:T(8,128)} custom-call(bf16[32,32,256]{2,1,0:T(8,128)(2,1)S(1)} %get-tuple-element.140.refs_0_, bf16[32,32,256]{2,1,0:T(8,128)(2,1)S(1)} %get-tuple-element.143.refs_1_, bf16[24,64,256]{2,1,0:T(8,128)(2,1)S(1)} %constant_dynamic-update-slice_fusion.3.refs_2_.refs_3_.refs_4_, ...), custom_call_target="tpu_custom_call", output_to_operand_aliasing={{}: (25, {})} | custom-call | flops 2013265920 | bytes 15728640 | tf_op jit(solution)/shard_map/pallas_call | solution.py:238
  153.4 6.5 %shard_map.41.refs_25_ = f32[32,2,256,1280]{3,2,1,0:T(8,128)} custom-call(bf16[32,32,256]{2,1,0:T(8,128)(2,1)S(1)} %get-tuple-element.140.refs_0_, bf16[32,32,256]{2,1,0:T(8,128)(2,1)S(1)} %get-tuple-element.143.refs_1_, bf16[24,64,256]{2,1,0:T(8,128)(2,1)S(1)} %constant_dynamic-update-slice_fusion.6.refs_3_.refs_4_.refs_2_, ...), custom_call_target="tpu_custom_call", output_to_operand_aliasing={{}: (25, {})} | custom-call | flops 2013265920 | bytes 15728640 | tf_op jit(solution)/shard_map/pallas_call | solution.py:238
  160.4 6.6 %shard_map.42.refs_25_ = f32[32,2,256,1280]{3,2,1,0:T(8,128)} custom-call(bf16[32,32,256]{2,1,0:T(8,128)(2,1)S(1)} %get-tuple-element.140.refs_0_, bf16[32,32,256]{2,1,0:T(8,128)(2,1)S(1)} %get-tuple-element.143.refs_1_, bf16[24,64,256]{2,1,0:T(8,128)(2,1)S(1)} %constant_dynamic-update-slice_fusion.6.refs_3_.refs_4_.refs_2_, ...), custom_call_target="tpu_custom_call", output_to_operand_aliasing={{}: (25, {})} | custom-call | flops 2013265920 | bytes 15728640 | tf_op jit(solution)/shard_map/pallas_call | solution.py:238
  167.0 5.0 %shard_map.43.refs_25_ = f32[32,2,256,1280]{3,2,1,0:T(8,128)} custom-call(bf16[32,32,256]{2,1,0:T(8,128)(2,1)S(1)} %get-tuple-element.140.refs_0_, bf16[32,32,256]{2,1,0:T(8,128)(2,1)S(1)} %get-tuple-element.143.refs_1_, bf16[20,64,256]{2,1,0:T(8,128)(2,1)S(1)} %constant_dynamic-update-slice_fusion.refs_3_.refs_4_.refs_2_, ...), custom_call_target="tpu_custom_call", output_to_operand_aliasing={{}: (25, {})} | custom-call | flops 1342177280 | bytes 10485760 | tf_op jit(solution)/shard_map/pallas_call | solution.py:238
  172.0 5.0 %shard_map.44 = f32[32,2,256,1280]{3,2,1,0:T(8,128)} custom-call(bf16[32,32,256]{2,1,0:T(8,128)(2,1)S(1)} %get-tuple-element.140.refs_0_, bf16[32,32,256]{2,1,0:T(8,128)(2,1)S(1)} %get-tuple-element.143.refs_1_, bf16[20,64,256]{2,1,0:T(8,128)(2,1)S(1)} %constant_dynamic-update-slice_fusion.refs_3_.refs_4_.refs_2_, ...), custom_call_target="tpu_custom_call", output_to_operand_aliasing={{}: (25, {})} | custom-call | flops 1342177280 | bytes 10485760 | tf_op jit(solution)/shard_map/pallas_call | solution.py:238
  (97 shorter events, 25.1 us)
Async XLA Ops:
  1.8 12.1 %collective-permute-start = (bf16[2,256,384]{2,1,0:T(8,128)(2,1)}, bf16[2,256,384]{2,1,0:T(8,128)(2,1)S(1)}, u32[]{:S(2)}, u32[]{:S(2)}) collective-permute-start(bf16[2,256,384]{2,1,0:T(8,128)(2,1)} %slice.4), channel_id=1, source_target_pairs={{1,0},{2,1},{3,2},{5,4},{6,5},{7,6},{9,8},{10,9},{11,10},{13,12},{... | collective-permute-start | bytes 1179656 | tf_op jit(solution)/shard_map/ppermute | solution.py:351
  11.2 13.3 %collective-permute-start.8 = (bf16[32,32,256]{2,1,0:T(8,128)(2,1)S(1)}, bf16[32,32,256]{2,1,0:T(8,128)(2,1)S(1)}, u32[]{:S(2)}, u32[]{:S(2)}) collective-permute-start(bf16[32,32,256]{2,1,0:T(8,128)(2,1)S(1)} %get-tuple-element.140.refs_0_), channel_id=1, source_target_pairs={{0,16},{4,20},{8,24},{12,28},{16,0},{20,4},{24,8},{28,12},{1,17},{... | collective-permute-start | bytes 1572872 | tf_op jit(solution)/shard_map/ppermute | solution.py:263
  19.6 12.3 %collective-permute-start.2 = (bf16[6,64,256]{2,1,0:T(8,128)(2,1)S(1)}, bf16[6,64,256]{2,1,0:T(8,128)(2,1)S(1)}, u32[]{:S(2)}, u32[]{:S(2)}) collective-permute-start(bf16[6,64,256]{2,1,0:T(8,128)(2,1)S(1)} %get-tuple-element.102), channel_id=1, source_target_pairs={{0,2},{1,3},{2,0},{3,1},{4,6},{5,7},{6,4},{7,5},{8,10},{9,11},{10,... | collective-permute-start | bytes 589832 | tf_op jit(solution)/shard_map/ppermute | solution.py:263
  19.9 17.7 %collective-permute-start.3 = (bf16[6,64,256]{2,1,0:T(8,128)(2,1)S(1)}, bf16[6,64,256]{2,1,0:T(8,128)(2,1)S(1)}, u32[]{:S(2)}, u32[]{:S(2)}) collective-permute-start(bf16[6,64,256]{2,1,0:T(8,128)(2,1)S(1)} %get-tuple-element.103), channel_id=1, source_target_pairs={{0,3},{1,2},{2,1},{3,0},{4,7},{5,6},{6,5},{7,4},{8,11},{9,10},{10,... | collective-permute-start | bytes 589832 | tf_op jit(solution)/shard_map/ppermute | solution.py:263
  20.9 21.8 %collective-permute-start.7 = (bf16[32,32,256]{2,1,0:T(8,128)(2,1)S(1)}, bf16[32,32,256]{2,1,0:T(8,128)(2,1)S(1)}, u32[]{:S(2)}, u32[]{:S(2)}) collective-permute-start(bf16[32,32,256]{2,1,0:T(8,128)(2,1)S(1)} %get-tuple-element.143.refs_1_), channel_id=1, source_target_pairs={{0,16},{4,20},{8,24},{12,28},{16,0},{20,4},{24,8},{28,12},{1,17},{... | collective-permute-start | bytes 1572872 | tf_op jit(solution)/shard_map/ppermute | solution.py:263
  21.5 17.4 %collective-permute-start.1 = (bf16[12,64,256]{2,1,0:T(8,128)(2,1)S(1)}, bf16[12,64,256]{2,1,0:T(8,128)(2,1)S(1)}, u32[]{:S(2)}, u32[]{:S(2)}) collective-permute-start(bf16[12,64,256]{2,1,0:T(8,128)(2,1)S(1)} %get-tuple-element.99), channel_id=1, source_target_pairs={{0,1},{1,0},{2,3},{3,2},{4,5},{5,4},{6,7},{7,6},{8,9},{9,8},{10,11... | collective-permute-start | bytes 1179656 | tf_op jit(solution)/shard_map/ppermute | solution.py:263
  24.6 18.2 %collective-permute-start.9 = (bf16[32,32,256]{2,1,0:T(8,128)(2,1)S(1)}, bf16[32,32,256]{2,1,0:T(8,128)(2,1)S(1)}, u32[]{:S(2)}, u32[]{:S(2)}) collective-permute-start(bf16[32,32,256]{2,1,0:T(8,128)(2,1)S(1)} %broadcast_select_fusion.4), channel_id=1, source_target_pairs={{0,8},{4,12},{8,0},{12,4},{16,24},{20,28},{24,16},{28,20},{1,9},{5... | collective-permute-start | bytes 1572872 | tf_op jit(solution)/shard_map/ppermute | solution.py:263
  37.6 9.5 %collective-permute-start.5 = (bf16[6,64,256]{2,1,0:T(8,128)(2,1)S(1)}, bf16[6,64,256]{2,1,0:T(8,128)(2,1)S(1)}, u32[]{:S(2)}, u32[]{:S(2)}) collective-permute-start(bf16[6,64,256]{2,1,0:T(8,128)(2,1)S(1)} %get-tuple-element.108), channel_id=1, source_target_pairs={{0,2},{1,3},{2,0},{3,1},{4,6},{5,7},{6,4},{7,5},{8,10},{9,11},{10,... | collective-permute-start | bytes 589832 | tf_op jit(solution)/shard_map/ppermute | solution.py:263
  37.6 17.5 %collective-permute-start.6 = (bf16[6,64,256]{2,1,0:T(8,128)(2,1)S(1)}, bf16[6,64,256]{2,1,0:T(8,128)(2,1)S(1)}, u32[]{:S(2)}, u32[]{:S(2)}) collective-permute-start(bf16[6,64,256]{2,1,0:T(8,128)(2,1)S(1)} %get-tuple-element.109), channel_id=1, source_target_pairs={{0,3},{1,2},{2,1},{3,0},{4,7},{5,6},{6,5},{7,4},{8,11},{9,10},{10,... | collective-permute-start | bytes 589832 | tf_op jit(solution)/shard_map/ppermute | solution.py:263
  38.9 20.0 %collective-permute-start.4 = (bf16[12,64,256]{2,1,0:T(8,128)(2,1)S(1)}, bf16[12,64,256]{2,1,0:T(8,128)(2,1)S(1)}, u32[]{:S(2)}, u32[]{:S(2)}) collective-permute-start(bf16[12,64,256]{2,1,0:T(8,128)(2,1)S(1)} %get-tuple-element.105), channel_id=1, source_target_pairs={{0,1},{1,0},{2,3},{3,2},{4,5},{5,4},{6,7},{7,6},{8,9},{9,8},{10,11... | collective-permute-start | bytes 1179656 | tf_op jit(solution)/shard_map/ppermute | solution.py:263
  42.7 28.8 %collective-permute-start.13 = (bf16[24,64,256]{2,1,0:T(8,128)(2,1)S(1)}, bf16[24,64,256]{2,1,0:T(8,128)(2,1)S(1)}, u32[]{:S(2)}, u32[]{:S(2)}) collective-permute-start(bf16[24,64,256]{2,1,0:T(8,128)(2,1)S(1)} %constant_dynamic-update-slice_fusion.3.refs_2_.refs_3_.refs_4_), channel_id=1, source_target_pairs={{0,16},{4,20},{8,24},{12,28},{16,0},{20,4},{24,8},{28,12},{1,17},{... | collective-permute-start | bytes 2359304 | tf_op jit(solution)/shard_map/ppermute | solution.py:263
  42.8 28.7 %collective-permute-start.14 = (bf16[32,32,256]{2,1,0:T(8,128)(2,1)S(1)}, bf16[32,32,256]{2,1,0:T(8,128)(2,1)S(1)}, u32[]{:S(2)}, u32[]{:S(2)}) collective-permute-start(bf16[32,32,256]{2,1,0:T(8,128)(2,1)S(1)} %broadcast_select_fusion.3), channel_id=1, source_target_pairs={{0,8},{4,12},{8,0},{12,4},{16,24},{20,28},{24,16},{28,20},{1,9},{5... | collective-permute-start | bytes 1572872 | tf_op jit(solution)/shard_map/ppermute | solution.py:263
  55.1 15.8 %collective-permute-start.11 = (bf16[6,64,256]{2,1,0:T(8,128)(2,1)S(1)}, bf16[6,64,256]{2,1,0:T(8,128)(2,1)S(1)}, u32[]{:S(2)}, u32[]{:S(2)}) collective-permute-start(bf16[6,64,256]{2,1,0:T(8,128)(2,1)S(1)} %get-tuple-element.117), channel_id=1, source_target_pairs={{0,2},{1,3},{2,0},{3,1},{4,6},{5,7},{6,4},{7,5},{8,10},{9,11},{10,... | collective-permute-start | bytes 589832 | tf_op jit(solution)/shard_map/ppermute | solution.py:263
  55.1 16.4 %collective-permute-start.12 = (bf16[6,64,256]{2,1,0:T(8,128)(2,1)S(1)}, bf16[6,64,256]{2,1,0:T(8,128)(2,1)S(1)}, u32[]{:S(2)}, u32[]{:S(2)}) collective-permute-start(bf16[6,64,256]{2,1,0:T(8,128)(2,1)S(1)} %get-tuple-element.118), channel_id=1, source_target_pairs={{0,3},{1,2},{2,1},{3,0},{4,7},{5,6},{6,5},{7,4},{8,11},{9,10},{10,... | collective-permute-start | bytes 589832 | tf_op jit(solution)/shard_map/ppermute | solution.py:263
  58.8 12.0 %collective-permute-start.10 = (bf16[8,64,256]{2,1,0:T(8,128)(2,1)S(1)}, bf16[8,64,256]{2,1,0:T(8,128)(2,1)S(1)}, u32[]{:S(2)}, u32[]{:S(2)}) collective-permute-start(bf16[8,64,256]{2,1,0:T(8,128)(2,1)S(1)} %get-tuple-element.114), channel_id=1, source_target_pairs={{0,1},{1,0},{2,3},{3,2},{4,5},{5,4},{6,7},{7,6},{8,9},{9,8},{10,11... | collective-permute-start | bytes 786440 | tf_op jit(solution)/shard_map/ppermute | solution.py:263
  71.6 23.0 %collective-permute-start.18 = (bf16[24,64,256]{2,1,0:T(8,128)(2,1)S(1)}, bf16[24,64,256]{2,1,0:T(8,128)(2,1)S(1)}, u32[]{:S(2)}, u32[]{:S(2)}) collective-permute-start(bf16[24,64,256]{2,1,0:T(8,128)(2,1)S(1)} %broadcast_select_fusion.1), channel_id=1, source_target_pairs={{0,8},{4,12},{8,0},{12,4},{16,24},{20,28},{24,16},{28,20},{1,9},{5... | collective-permute-start | bytes 2359304 | tf_op jit(solution)/shard_map/ppermute | solution.py:263
  74.0 20.6 %collective-permute-start.17 = (bf16[24,64,256]{2,1,0:T(8,128)(2,1)S(1)}, bf16[24,64,256]{2,1,0:T(8,128)(2,1)S(1)}, u32[]{:S(2)}, u32[]{:S(2)}) collective-permute-start(bf16[24,64,256]{2,1,0:T(8,128)(2,1)S(1)} %constant_dynamic-update-slice_fusion.6.refs_3_.refs_4_.refs_2_), channel_id=1, source_target_pairs={{0,16},{4,20},{8,24},{12,28},{16,0},{20,4},{24,8},{28,12},{1,17},{... | collective-permute-start | bytes 2359304 | tf_op jit(solution)/shard_map/ppermute | solution.py:263
  74.6 20.0 %collective-permute-start.16 = (bf16[6,64,256]{2,1,0:T(8,128)(2,1)S(1)}, bf16[6,64,256]{2,1,0:T(8,128)(2,1)S(1)}, u32[]{:S(2)}, u32[]{:S(2)}) collective-permute-start(bf16[6,64,256]{2,1,0:T(8,128)(2,1)S(1)} %get-tuple-element.128), channel_id=1, source_target_pairs={{0,3},{1,2},{2,1},{3,0},{4,7},{5,6},{6,5},{7,4},{8,11},{9,10},{10,... | collective-permute-start | bytes 589832 | tf_op jit(solution)/shard_map/ppermute | solution.py:263
  77.3 36.3 %collective-permute-start.23 = (bf16[4,32,32,256]{3,2,1,0:T(8,128)(2,1)S(1)}, bf16[4,32,32,256]{3,2,1,0:T(8,128)(2,1)S(1)}, u32[]{:S(2)}, u32[]{:S(2)}) collective-permute-start(bf16[4,32,32,256]{3,2,1,0:T(8,128)(2,1)S(1)} %pad_maximum_fusion), channel_id=1, source_target_pairs={{0,4},{4,0},{8,12},{12,8},{16,20},{20,16},{24,28},{28,24},{1,5},{5... | collective-permute-start | bytes 6291464 | tf_op jit(solution)/shard_map/ppermute | solution.py:263
  94.7 18.5 %collective-permute-start.22 = (bf16[24,64,256]{2,1,0:T(8,128)(2,1)S(1)}, bf16[24,64,256]{2,1,0:T(8,128)(2,1)S(1)}, u32[]{:S(2)}, u32[]{:S(2)}) collective-permute-start(bf16[24,64,256]{2,1,0:T(8,128)(2,1)S(1)} %broadcast_select_fusion), channel_id=1, source_target_pairs={{0,8},{4,12},{8,0},{12,4},{16,24},{20,28},{24,16},{28,20},{1,9},{5... | collective-permute-start | bytes 2359304 | tf_op jit(solution)/shard_map/ppermute | solution.py:263
  95.0 15.3 %collective-permute-start.21 = (bf16[20,64,256]{2,1,0:T(8,128)(2,1)S(1)}, bf16[20,64,256]{2,1,0:T(8,128)(2,1)S(1)}, u32[]{:S(2)}, u32[]{:S(2)}) collective-permute-start(bf16[20,64,256]{2,1,0:T(8,128)(2,1)S(1)} %constant_dynamic-update-slice_fusion.refs_3_.refs_4_.refs_2_), channel_id=1, source_target_pairs={{0,16},{4,20},{8,24},{12,28},{16,0},{20,4},{24,8},{28,12},{1,17},{... | collective-permute-start | bytes 1966088 | tf_op jit(solution)/shard_map/ppermute | solution.py:263
  95.8 8.5 %collective-permute-start.19 = (bf16[4,64,256]{2,1,0:T(8,128)(2,1)S(1)}, bf16[4,64,256]{2,1,0:T(8,128)(2,1)S(1)}, u32[]{:S(2)}, u32[]{:S(2)}) collective-permute-start(bf16[4,64,256]{2,1,0:T(8,128)(2,1)S(1)} %get-tuple-element.135), channel_id=1, source_target_pairs={{0,2},{1,3},{2,0},{3,1},{4,6},{5,7},{6,4},{7,5},{8,10},{9,11},{10,... | collective-permute-start | bytes 393224 | tf_op jit(solution)/shard_map/ppermute | solution.py:263
  95.8 11.5 %collective-permute-start.20 = (bf16[4,64,256]{2,1,0:T(8,128)(2,1)S(1)}, bf16[4,64,256]{2,1,0:T(8,128)(2,1)S(1)}, u32[]{:S(2)}, u32[]{:S(2)}) collective-permute-start(bf16[4,64,256]{2,1,0:T(8,128)(2,1)S(1)} %get-tuple-element.136), channel_id=1, source_target_pairs={{0,3},{1,2},{2,1},{3,0},{4,7},{5,6},{6,5},{7,4},{8,11},{9,10},{10,... | collective-permute-start | bytes 393224 | tf_op jit(solution)/shard_map/ppermute | solution.py:263
  110.3 8.8 %collective-permute-start.29 = (bf16[12,64,256]{2,1,0:T(8,128)(2,1)S(1)}, bf16[12,64,256]{2,1,0:T(8,128)(2,1)S(1)}, u32[]{:S(2)}, u32[]{:S(2)}) collective-permute-start(bf16[12,64,256]{2,1,0:T(8,128)(2,1)S(1)} %constant_dynamic-update-slice_fusion.11.refs_3_.refs_4_), channel_id=1, source_target_pairs={{0,16},{4,20},{8,24},{12,28},{16,0},{20,4},{24,8},{28,12},{1,17},{... | collective-permute-start | bytes 1179656 | tf_op jit(solution)/shard_map/ppermute | solution.py:263
  113.3 14.8 %collective-permute-start.26 = (bf16[20,64,256]{2,1,0:T(8,128)(2,1)S(1)}, bf16[20,64,256]{2,1,0:T(8,128)(2,1)S(1)}, u32[]{:S(2)}, u32[]{:S(2)}) collective-permute-start(bf16[20,64,256]{2,1,0:T(8,128)(2,1)S(1)} %broadcast_select_fusion.2), channel_id=1, source_target_pairs={{0,8},{4,12},{8,0},{12,4},{16,24},{20,28},{24,16},{28,20},{1,9},{5... | collective-permute-start | bytes 1966088 | tf_op jit(solution)/shard_map/ppermute | solution.py:263
  113.9 16.2 %collective-permute-start.27 = (bf16[2,24,64,256]{3,2,1,0:T(8,128)(2,1)S(1)}, bf16[2,24,64,256]{3,2,1,0:T(8,128)(2,1)S(1)}, u32[]{:S(2)}, u32[]{:S(2)}) collective-permute-start(bf16[2,24,64,256]{3,2,1,0:T(8,128)(2,1)S(1)} %pad_maximum_fusion.1), channel_id=1, source_target_pairs={{0,4},{4,0},{8,12},{12,8},{16,20},{20,16},{24,28},{28,24},{1,5},{5... | collective-permute-start | bytes 4718600 | tf_op jit(solution)/shard_map/ppermute | solution.py:263
  119.1 20.8 %collective-permute-start.31 = (bf16[8,64,256]{2,1,0:T(8,128)(2,1)S(1)}, bf16[8,64,256]{2,1,0:T(8,128)(2,1)S(1)}, u32[]{:S(2)}, u32[]{:S(2)}) collective-permute-start(bf16[8,64,256]{2,1,0:T(8,128)(2,1)S(1)} %constant_dynamic-update-slice_fusion.13.refs_3_.refs_4_), channel_id=1, source_target_pairs={{0,16},{4,20},{8,24},{12,28},{16,0},{20,4},{24,8},{28,12},{1,17},{... | collective-permute-start | bytes 786440 | tf_op jit(solution)/shard_map/ppermute | solution.py:263
  120.0 10.1 %collective-permute-start.25 = (bf16[4,64,256]{2,1,0:T(8,128)(2,1)S(1)}, bf16[4,64,256]{2,1,0:T(8,128)(2,1)S(1)}, u32[]{:S(2)}, u32[]{:S(2)}) collective-permute-start(bf16[4,64,256]{2,1,0:T(8,128)(2,1)S(1)} %get-tuple-element.148), channel_id=1, source_target_pairs={{0,3},{1,2},{2,1},{3,0},{4,7},{5,6},{6,5},{7,4},{8,11},{9,10},{10,... | collective-permute-start | bytes 393224 | tf_op jit(solution)/shard_map/ppermute | solution.py:263
  128.1 11.8 %collective-permute-start.32 = (bf16[12,64,256]{2,1,0:T(8,128)(2,1)S(1)}, bf16[12,64,256]{2,1,0:T(8,128)(2,1)S(1)}, u32[]{:S(2)}, u32[]{:S(2)}) collective-permute-start(bf16[12,64,256]{2,1,0:T(8,128)(2,1)S(1)} %broadcast_select_fusion.5), channel_id=1, source_target_pairs={{0,8},{4,12},{8,0},{12,4},{16,24},{20,28},{24,16},{28,20},{1,9},{5... | collective-permute-start | bytes 1179656 | tf_op jit(solution)/shard_map/ppermute | solution.py:263
  139.9 10.2 %collective-permute-start.33 = (bf16[8,64,256]{2,1,0:T(8,128)(2,1)S(1)}, bf16[8,64,256]{2,1,0:T(8,128)(2,1)S(1)}, u32[]{:S(2)}, u32[]{:S(2)}) collective-permute-start(bf16[8,64,256]{2,1,0:T(8,128)(2,1)S(1)} %broadcast_select_fusion.7), channel_id=1, source_target_pairs={{0,8},{4,12},{8,0},{12,4},{16,24},{20,28},{24,16},{28,20},{1,9},{5... | collective-permute-start | bytes 786440 | tf_op jit(solution)/shard_map/ppermute | solution.py:263
  141.4 8.8 %collective-permute-start.34 = (bf16[8,64,256]{2,1,0:T(8,128)(2,1)S(1)}, bf16[8,64,256]{2,1,0:T(8,128)(2,1)S(1)}, u32[]{:S(2)}, u32[]{:S(2)}) collective-permute-start(bf16[8,64,256]{2,1,0:T(8,128)(2,1)S(1)} %constant_dynamic-update-slice_fusion.9.refs_3_.refs_4_), channel_id=1, source_target_pairs={{0,16},{4,20},{8,24},{12,28},{16,0},{20,4},{24,8},{28,12},{1,17},{... | collective-permute-start | bytes 786440 | tf_op jit(solution)/shard_map/ppermute | solution.py:263
  150.2 9.8 %collective-permute-start.36 = (bf16[8,64,256]{2,1,0:T(8,128)(2,1)S(1)}, bf16[8,64,256]{2,1,0:T(8,128)(2,1)S(1)}, u32[]{:S(2)}, u32[]{:S(2)}) collective-permute-start(bf16[8,64,256]{2,1,0:T(8,128)(2,1)S(1)} %broadcast_select_fusion.6), channel_id=1, source_target_pairs={{0,8},{4,12},{8,0},{12,4},{16,24},{20,28},{24,16},{28,20},{1,9},{5... | collective-permute-start | bytes 786440 | tf_op jit(solution)/shard_map/ppermute | solution.py:263
  (10 other events, 55.1 us)

commit v2 on v1

--- a/solution.py
+++ b/solution.py
@@ -163,52 +163,63 @@
     )(*operands)
 
 
-def pairs_kernel(scale, half, count, step, *refs):
-    out = refs[-1]
-    per_block = [refs[n * count : (n + 1) * count] for n in range(half + 1)]
-    for channel in range(step):
-
-        def pieces(block):
-            got = []
-            for ref in per_block[block]:
-                if ref.ndim == 3:
-                    got.append(ref[channel])
-                else:
-                    got += [ref[m, channel] for m in range(ref.shape[0])]
-            return got
-
-        mine = pieces(0)
-        turned = []
-        for value in mine:
-            size = 2 * PART_FRAMES
-            for first in range(0, value.shape[0], size):
-                turned.append(value[first + PART_FRAMES : first + size])
-                turned.append(-value[first : first + PART_FRAMES])
-        left = jnp.concatenate(mine, axis=0).T
-        left_turned = jnp.concatenate(turned, axis=0).T
-        width = left.shape[0]
-        for block in range(half + 1):
-            right = jnp.concatenate(pieces(block), axis=0)
-            columns = slice(block * width, (block + 1) * width)
-            out[channel, 0, :, columns] = (
-                jnp.dot(left, right, preferred_element_type=jnp.float32) * scale
-            )
-            out[channel, 1, :, columns] = (
-                jnp.dot(left_turned, right, preferred_element_type=jnp.float32) * scale
-            )
+def pairs_kernel(scale, count, step, wanted, *refs):
+    out, lefts = refs[-2:]
+    mine = refs[:count]
+    per_block = [refs[n * count : (n + 1) * count] for n in range(1, len(refs) // count)]
+
+    def pieces(block, channel):
+        got = []
+        for ref in block:
+            if len(ref.shape) == 3:
+                got.append(ref[channel])
+            else:
+                got += [ref[m, channel] for m in range(ref.shape[0])]
+        return got
+
+    @pl.when(pl.program_id(1) == 0)
+    def _():
+        for channel in range(step):
+            values = pieces(mine, channel)
+            turned = []
+            for value in values:
+                size = 2 * PART_FRAMES
+                for first in range(0, value.shape[0], size):
+                    turned.append(value[first + PART_FRAMES : first + size])
+                    turned.append(-value[first : first + PART_FRAMES])
+            lefts[channel, 0] = jnp.concatenate(values, axis=0).T
+            lefts[channel, 1] = jnp.concatenate(turned, axis=0).T
+
+    width = lefts.shape[2]
+    together = out.shape[-1] // width
+    for j in range(len(wanted) // together):
+
+        @pl.when(pl.program_id(1) == j)
+        def _(j=j):
+            for channel in range(step):
+                for k in range(together):
+                    right = jnp.concatenate(pieces(per_block[j * together + k], channel), axis=0)
+                    for part in range(2):
+                        out[channel, part, :, k * width : (k + 1) * width] = (
+                            jnp.dot(
+                                lefts[channel, part], right, preferred_element_type=jnp.float32
+                            )
+                            * scale
+                        )
 
 
 PART_FRAMES = 16
-
-
-def pairs(blocks, total, first, size, kept, scale):
-    half = len(blocks) - 1
+NO_COST = pl.CostEstimate(flops=0, bytes_accessed=0, transcendentals=0)
+
+
+def pairs(blocks, total, first, size, kept, scale, wanted):
     inputs = blocks[0][0][0].shape[-1]
     operands, in_specs = [], []
     count = len(blocks[0])
-    offsets = [offset for block in blocks for _, _, offset in block]
+    used = [blocks[0]] + [blocks[n] for n in wanted]
+    offsets = [offset for block in used for _, _, offset in block]
     step = 2 if all(x % 2 == 0 for x in [size, first, *offsets]) else 1
-    for block in blocks:
+    for block in used:
         for array, stack, offset in block:
             operands.append(array)
             rows = array.shape[-2]
@@ -216,13 +227,29 @@
             lead = array.shape[:-3] if stack is None else array.shape[1:-3]
             zeros = (0,) * len(lead)
             if stack is None:
-                shape, index = (*lead, step, rows, inputs), lambda i, a=at, z=zeros: (*z, a + i, 0, 0)
+                shape = (*lead, step, rows, inputs)
+                index = lambda i, j, a=at, z=zeros: (*z, a + i, 0, 0)
             else:
                 shape = (None, *lead, step, rows, inputs)
-                index = lambda i, a=at, s=stack, z=zeros: (s, *z, a + i, 0, 0)
+                index = lambda i, j, a=at, s=stack, z=zeros: (s, *z, a + i, 0, 0)
             in_specs.append(pl.BlockSpec(shape, index))
-    depth = sum(math.prod(x.shape[:-3] if st is None else x.shape[1:-3]) * x.shape[-2] for x, st, _ in blocks[0])
-    slots = (half + 1) * inputs
+    depth = sum(
+        math.prod(x.shape[:-3] if st is None else x.shape[1:-3]) * x.shape[-2]
+        for x, st, _ in blocks[0]
+    )
+    start = wanted[0]
+    apart = wanted[1] - start if len(wanted) > 1 else 1
+    if apart == 1:
+        steps = 1
+        out_spec = pl.BlockSpec(
+            tuple(map(pl.Element, (step, 2, inputs, len(wanted) * inputs))),
+            lambda i, j: (first + i * step, 0, 0, start * inputs),
+        )
+    else:
+        steps = len(wanted)
+        out_spec = pl.BlockSpec(
+            (step, 2, inputs, inputs), lambda i, j: (first // step + i, 0, 0, start + apart * j)
+        )
     aliases = {}
     if total is not None:
         aliases = {len(operands): 0}
@@ -232,24 +259,21 @@
     def body(*refs):
         refs = list(refs)
         if total is not None:
-            refs.pop(-2)
-        pairs_kernel(scale, half, count, step, *refs)
+            refs.pop(-3)
+        pairs_kernel(scale, count, step, wanted, *refs)
 
     return pl.pallas_call(
         body,
-        grid=(size // step,),
-        out_shape=jax.ShapeDtypeStruct((kept, 2, inputs, slots), jnp.float32),
+        grid=(size // step, steps),
+        out_shape=jax.ShapeDtypeStruct((kept, 2, inputs, len(blocks) * inputs), jnp.float32),
         in_specs=in_specs,
-        out_specs=pl.BlockSpec((step, 2, inputs, slots), lambda i: (first // step + i, 0, 0, 0)),
+        out_specs=out_spec,
+        scratch_shapes=[pltpu.VMEM((step, 2, inputs, depth), jnp.bfloat16)],
         input_output_aliases=aliases,
         compiler_params=pltpu.CompilerParams(
-            vmem_limit_bytes=32 * 1024 * 1024, dimension_semantics=("arbitrary",)
+            vmem_limit_bytes=32 * 1024 * 1024, dimension_semantics=("arbitrary", "arbitrary")
         ),
-        cost_estimate=pl.CostEstimate(
-            flops=2 * size * 2 * inputs * slots * depth,
-            bytes_accessed=size * 2 * inputs * slots * 4,
-            transcendentals=0,
-        ),
+        cost_estimate=NO_COST,
     )(*operands)
 
 
@@ -314,6 +338,9 @@
     def core(self, *earlier):
         sent = jnp.stack(self.for_core(*earlier))
         self.over_core, self.slots = swapped(sent, self.axis, 1), (0, 1)
+
+    over_x = over_core = None
+    slots = (0, 1)
 
     def blocks(self):
         return [
@@ -362,17 +389,20 @@
     far = [pieces[len(nears) + q :: count] for q in range(count)]
     scale = 1.0 / math.sqrt(frames_dev * devices)
 
-    def run_pairs(total, q, *groups_):
+    def run_pairs(total, q, wanted, *groups_):
         blocks = [
             [(*entry, at) for entry, (_, at) in zip(entries, groups_)]
             for entries in zip(*[g for g, _ in groups_])
         ]
-        return pairs(blocks, total, firsts[q], sizes[q], kept, scale)
+        return pairs(blocks, total, firsts[q], sizes[q], kept, scale, wanted)
 
     if not planned:
         near = swapped(near[0], "tf", 1)
         far = jnp.stack([swapped(x, "tf", hop + 2) for hop, x in enumerate(far[0])])
-        return run_pairs(None, 0, *[(partners(x, "inp"), 0) for x in (own_a, own_b, near, far)])
+        wanted = tuple(range(lax.axis_size("inp") // 2 + 1))
+        return run_pairs(
+            None, 0, wanted, *[(partners(x, "inp"), 0) for x in (own_a, own_b, near, far)]
+        )
 
     def over_z(q, *earlier):
         sent = lax.optimization_barrier((*far[q], *earlier))
@@ -383,12 +413,13 @@
     a, b = Exchange(own_a, "inp"), Exchange(own_b, "inp")
     t = jnp.zeros((8, 128), jnp.float32)
 
-    def chunk(q):
+    def chunk(q, wanted):
         h = max(i for i, first in enumerate(near_firsts) if first <= firsts[q])
         at = nears[q] if q < len(nears) else 0
         return run_pairs(
             total,
             q,
+            wanted,
             (a.blocks(), firsts[q]),
             (b.blocks(), firsts[q]),
             (lines[h].blocks(), firsts[q] - near_firsts[h]),
@@ -414,40 +445,44 @@
     lines.append(exchange(n[1], *z[1]))
     lines[1].y(lines[0].over_y, t)
     lines[0].x(b.over_x, t)
+    early, late, full = (0, 4), (1, 2, 3), (0, 1, 2, 3, 4)
     t = tick(t, *z[2], lines[0].over_y, b.over_x)
     z.append(over_z(3, t))
     lines.append(exchange(n[2], *z[2]))
     lines[2].y(lines[1].over_y, t)
     lines[1].x(lines[0].over_x, t)
     core_of_both(a, b, t)
-    t = tick(t, *z[3], lines[1].over_y, lines[0].over_x)
+    total = chunk(0, early)
+    t = tick(t, *z[3], lines[1].over_y, lines[0].over_x, total)
     z.append(over_z(4, t))
     lines.append(exchange(*z[3]))
     lines[3].y(lines[2].over_y, t)
     lines[2].x(lines[1].over_x, t)
     lines[0].core(a.over_core, t)
-    t = tick(t, *z[4], lines[2].over_y, lines[1].over_x, a.over_core)
+    total = chunk(1, early)
+    t = tick(t, *z[4], lines[2].over_y, lines[1].over_x, a.over_core, total)
     z.append(over_z(5, t))
     lines.append(exchange(*z[4]))
     lines[4].y(lines[3].over_y, t)
     lines[3].x(lines[2].over_x, t)
-    total = chunk(0)
+    total = chunk(2, early)
+    total = chunk(0, late)
     lines[1].core(lines[0].over_core, t, total)
     t = tick(t, *z[5], lines[3].over_y, lines[2].over_x, lines[0].over_core)
     lines.append(exchange(*z[5]))
     lines[5].y(lines[4].over_y, t)
     lines[4].x(lines[3].over_x, t)
     lines[2].core(lines[1].over_core, t)
-    total = chunk(1)
+    total = chunk(1, late)
     t = tick(t, lines[4].over_y, lines[3].over_x, lines[1].over_core, total)
     lines[5].x(lines[4].over_x, t)
     lines[3].core(lines[2].over_core, t)
-    total = chunk(2)
+    total = chunk(2, late)
     t = tick(t, lines[5].over_y, lines[4].over_x, lines[2].over_core, total)
     core_of_both(lines[4], lines[5], t, lines[3].over_core)
-    total = chunk(3)
-    total = chunk(4)
-    total = chunk(5)
+    total = chunk(3, full)
+    total = chunk(4, full)
+    total = chunk(5, full)
     return total
 
 

time: 179 us -> 175 us (0.978)
  waiting for transfers between devices: 84.9 us -> 62.4 us
  starting transfers between devices: 38.3 us -> 49.1 us
  Pallas kernels: 47.7 us -> 54.7 us
    ppermute x37, waiting for transfers between devices: 83.5 us -> 61 us  [swapped(): return lax.ppermute(x, axis, [(i, i ^ bit) for i in range(devices)])]
    ppermute x37, starting transfers between devices: 36.2 us -> 47 us  [swapped(): return lax.ppermute(x, axis, [(i, i ^ bit) for i in range(devices)])]
    pallas_call x6 -> x9, Pallas kernels: 36.2 us -> 43.2 us  [pairs(): pl.pallas_call(body, grid=(size // step, steps), out_shape=jax.ShapeDtype...]
  transfers between devices with their start and end apart: 38 -> 38, of which waited for: 20 -> 20; matrix products, arithmetic and copies ran while one was open for 1% -> 1% of each run, Pallas kernels for 21% -> 26%
where the time goes in v2:
time: 175 us; the launch traced here: 172 us
  waiting for transfers between devices  62.4 us (36%)
  Pallas kernels  54.7 us (31%)
  starting transfers between devices  49.1 us (28%)
  local copies, waits for them, and re-layouts  3.64 us (2%)
  other arithmetic  2.11 us (1%)
    ppermute x37, waiting for transfers between devices, swapped(): return lax.ppermute(x, axis, [(i, i ^ bit) for i in range(devices)])  61 us
    ppermute x37, starting transfers between devices, swapped(): return lax.ppermute(x, axis, [(i, i ^ bit) for i in range(devices)])  47 us
    pallas_call x9, Pallas kernels, pairs(): pl.pallas_call(body, grid=(size // step, steps), out_shape=jax.ShapeDtype...  43.2 us
    pallas_call x2, Pallas kernels, spectra_part(): pl.pallas_call(functools.partial(spectra_kernel, {'halo': halo is not Non...  11.5 us
  transfers between devices with their start and end apart: 38, of which 20 were waited for; matrix products, arithmetic and copies ran while one was open for 1% of the time, Pallas kernels for 26%

profile of v2, /device:TPU:17, one launch (start us, length us, event | category | flops | bytes accessed | tf_op | source)
XLA Modules:
  0.0 172.2 jit_solution(12615091122275821641)
XLA Ops:
  0.0 1.8 %slice.4 = bf16[2,256,384]{2,1,0:T(8,128)(2,1)} slice(bf16[2,256,4096]{2,1,0:T(8,128)(2,1)} %refs_2_.3), slice={[0:2], [0:256], [0:384]} | slice | bytes 786432 | tf_op jit(solution)/shard_map/slice | solution.py:377
  1.8 2.1 %collective-permute-start = (bf16[2,256,384]{2,1,0:T(8,128)(2,1)}, bf16[2,256,384]{2,1,0:T(8,128)(2,1)S(1)}, u32[]{:S(2)}, u32[]{:S(2)}) collective-permute-start(bf16[2,256,384]{2,1,0:T(8,128)(2,1)} %slice.4), channel_id=1, source_target_pairs={{1,0},{2,1},{3,2},{5,4},{6,5},{7,6},{9,8},{10,9},{11,10},{13,12},{... | collective-permute-start | bytes 1179656 | tf_op jit(solution)/shard_map/ppermute | solution.py:378
  5.5 5.7 %shard_map.37 = (bf16[32,32,256]{2,1,0:T(8,128)(2,1)S(1)}, bf16[96,32,256]{2,1,0:T(8,128)(2,1)S(1)}) custom-call(s32[1]{0:T(128)} %bitcast.refs_0_, bf16[2,256,4096]{2,1,0:T(8,128)(2,1)} %refs_2_.3, bf16[2,256,4096]{2,1,0:T(8,128)(2,1)} %refs_2_.3, f32[4,128]{1,0:T(4,128)S(1)} %copy-done.2, bf16[2,256,256]{2,1,0:T(8,128)(2,1)S(1)} %copy-done), custom_call_target="tpu_custom_call" | custom-call | flops 1610612736 | bytes 4194304 | tf_op jit(solution)/shard_map/pallas_call | solution.py:146
  12.5 1.4 collective-permute-done.refs_3_
  13.9 5.8 %shard_map.38 = (bf16[32,32,256]{2,1,0:T(8,128)(2,1)S(1)}, bf16[12,64,256]{2,1,0:T(8,128)(2,1)S(1)}, bf16[12,64,256]{2,1,0:T(8,128)(2,1)S(1)}, bf16[8,64,256]{2,...) custom-call(s32[1]{0:T(128)} %bitcast.refs_0_, ...), custom_call_target="tpu_custom_call" | custom-call | flops 1610612736 | bytes 4194304 | tf_op jit(solution)/shard_map/pallas_call | solution.py:146
  25.1 2.5 %collective-permute-done.2 = bf16[6,64,256]{2,1,0:T(8,128)(2,1)S(1)} collective-permute-done((bf16[6,64,256]{2,1,0:T(8,128)(2,1)S(1)}, bf16[6,64,256]{2,1,0:T(8,128)(2,1)S(1)}, u32[]{:S(2)}, u32[]{:S(2)}) %collective-permute-start.2) | collective-permute-done | bytes 196640 | tf_op jit(solution)/shard_map/ppermute | solution.py:287
  27.6 5.8 %collective-permute-done.3 = bf16[6,64,256]{2,1,0:T(8,128)(2,1)S(1)} collective-permute-done((bf16[6,64,256]{2,1,0:T(8,128)(2,1)S(1)}, bf16[6,64,256]{2,1,0:T(8,128)(2,1)S(1)}, u32[]{:S(2)}, u32[]{:S(2)}) %collective-permute-start.3) | collective-permute-done | bytes 196640 | tf_op jit(solution)/shard_map/ppermute | solution.py:287
  33.4 5.9 %collective-permute-start.5 = (bf16[6,64,256]{2,1,0:T(8,128)(2,1)S(1)}, bf16[6,64,256]{2,1,0:T(8,128)(2,1)S(1)}, u32[]{:S(2)}, u32[]{:S(2)}) collective-permute-start(bf16[6,64,256]{2,1,0:T(8,128)(2,1)S(1)} %get-tuple-element.108), channel_id=1, source_target_pairs={{0,2},{1,3},{2,0},{3,1},{4,6},{5,7},{6,4},{7,5},{8,10},{9,11},{10,... | collective-permute-start | bytes 589832 | tf_op jit(solution)/shard_map/ppermute | solution.py:287
  43.3 8.8 %collective-permute-done.5 = bf16[6,64,256]{2,1,0:T(8,128)(2,1)S(1)} collective-permute-done((bf16[6,64,256]{2,1,0:T(8,128)(2,1)S(1)}, bf16[6,64,256]{2,1,0:T(8,128)(2,1)S(1)}, u32[]{:S(2)}, u32[]{:S(2)}) %collective-permute-start.5) | collective-permute-done | bytes 196640 | tf_op jit(solution)/shard_map/ppermute | solution.py:287
  52.1 5.1 %collective-permute-done.6 = bf16[6,64,256]{2,1,0:T(8,128)(2,1)S(1)} collective-permute-done((bf16[6,64,256]{2,1,0:T(8,128)(2,1)S(1)}, bf16[6,64,256]{2,1,0:T(8,128)(2,1)S(1)}, u32[]{:S(2)}, u32[]{:S(2)}) %collective-permute-start.6) | collective-permute-done | bytes 196640 | tf_op jit(solution)/shard_map/ppermute | solution.py:287
  58.6 2.3 %collective-permute-start.10 = (bf16[8,64,256]{2,1,0:T(8,128)(2,1)S(1)}, bf16[8,64,256]{2,1,0:T(8,128)(2,1)S(1)}, u32[]{:S(2)}, u32[]{:S(2)}) collective-permute-start(bf16[8,64,256]{2,1,0:T(8,128)(2,1)S(1)} %get-tuple-element.114), channel_id=1, source_target_pairs={{0,1},{1,0},{2,3},{3,2},{4,5},{5,4},{6,7},{7,6},{8,9},{9,8},{10,11... | collective-permute-start | bytes 786440 | tf_op jit(solution)/shard_map/ppermute | solution.py:287
  60.9 13.3 %collective-permute-done.10 = bf16[8,64,256]{2,1,0:T(8,128)(2,1)S(1)} collective-permute-done((bf16[8,64,256]{2,1,0:T(8,128)(2,1)S(1)}, bf16[8,64,256]{2,1,0:T(8,128)(2,1)S(1)}, u32[]{:S(2)}, u32[]{:S(2)}) %collective-permute-start.10) | collective-permute-done | bytes 262176 | tf_op jit(solution)/shard_map/ppermute | solution.py:287
  74.2 1.8 %collective-permute-done.12 = bf16[6,64,256]{2,1,0:T(8,128)(2,1)S(1)} collective-permute-done((bf16[6,64,256]{2,1,0:T(8,128)(2,1)S(1)}, bf16[6,64,256]{2,1,0:T(8,128)(2,1)S(1)}, u32[]{:S(2)}, u32[]{:S(2)}) %collective-permute-start.12) | collective-permute-done | bytes 196640 | tf_op jit(solution)/shard_map/ppermute | solution.py:287
  79.4 3.0 %collective-permute-start.23 = (bf16[4,32,32,256]{3,2,1,0:T(8,128)(2,1)S(1)}, bf16[4,32,32,256]{3,2,1,0:T(8,128)(2,1)S(1)}, u32[]{:S(2)}, u32[]{:S(2)}) collective-permute-start(bf16[4,32,32,256]{3,2,1,0:T(8,128)(2,1)S(1)} %pad_maximum_fusion), channel_id=1, source_target_pairs={{0,4},{4,0},{8,12},{12,8},{16,20},{20,16},{24,28},{28,24},{1,5},{5... | collective-permute-start | bytes 6291464 | tf_op jit(solution)/shard_map/ppermute | solution.py:287
  82.4 4.3 %shard_map.39.refs_15_ = f32[32,2,256,1280]{3,2,1,0:T(8,128)} custom-call(bf16[32,32,256]{2,1,0:T(8,128)(2,1)S(1)} %get-tuple-element.140.refs_0_.refs_5_, bf16[32,32,256]{2,1,0:T(8,128)(2,1)S(1)} %get-tuple-element.143.refs_1_.refs_6_, bf16[24,64,256]{2,1,0:T(8,128)(2,1)S(1)} %constant_dynamic-update-slice_fusion.3.refs_2_.refs_3_.refs_4_.refs_7_.refs_8_.refs_9_, ...), custom_call_target="tpu_custom_call" | custom-call | tf_op jit(solution)/shard_map/pallas_call | solution.py:265
  86.7 3.9 %collective-permute-done.15 = bf16[6,64,256]{2,1,0:T(8,128)(2,1)S(1)} collective-permute-done((bf16[6,64,256]{2,1,0:T(8,128)(2,1)S(1)}, bf16[6,64,256]{2,1,0:T(8,128)(2,1)S(1)}, u32[]{:S(2)}, u32[]{:S(2)}) %collective-permute-start.15) | collective-permute-done | bytes 196640 | tf_op jit(solution)/shard_map/ppermute | solution.py:287
  90.6 4.2 %collective-permute-done.16 = bf16[6,64,256]{2,1,0:T(8,128)(2,1)S(1)} collective-permute-done((bf16[6,64,256]{2,1,0:T(8,128)(2,1)S(1)}, bf16[6,64,256]{2,1,0:T(8,128)(2,1)S(1)}, u32[]{:S(2)}, u32[]{:S(2)}) %collective-permute-start.16) | collective-permute-done | bytes 196640 | tf_op jit(solution)/shard_map/ppermute | solution.py:287
  97.8 4.4 %shard_map.40.refs_15_ = f32[32,2,256,1280]{3,2,1,0:T(8,128)} custom-call(bf16[32,32,256]{2,1,0:T(8,128)(2,1)S(1)} %get-tuple-element.140.refs_0_.refs_5_, bf16[32,32,256]{2,1,0:T(8,128)(2,1)S(1)} %get-tuple-element.143.refs_1_.refs_6_, ...), custom_call_target="tpu_custom_call", output_to_operand_aliasing={{}: (15, {})} | custom-call | tf_op jit(solution)/shard_map/pallas_call | solution.py:265
  102.2 6.3 %collective-permute-done.20 = bf16[4,64,256]{2,1,0:T(8,128)(2,1)S(1)} collective-permute-done((bf16[4,64,256]{2,1,0:T(8,128)(2,1)S(1)}, bf16[4,64,256]{2,1,0:T(8,128)(2,1)S(1)}, u32[]{:S(2)}, u32[]{:S(2)}) %collective-permute-start.20) | collective-permute-done | bytes 131104 | tf_op jit(solution)/shard_map/ppermute | solution.py:287
  110.6 1.6 collective-permute-done.22.refs_13_.refs_14_.refs_12_.refs_17_
  112.9 3.6 %collective-permute-start.27 = (bf16[2,24,64,256]{3,2,1,0:T(8,128)(2,1)S(1)}, bf16[2,24,64,256]{3,2,1,0:T(8,128)(2,1)S(1)}, u32[]{:S(2)}, u32[]{:S(2)}) collective-permute-start(bf16[2,24,64,256]{3,2,1,0:T(8,128)(2,1)S(1)} %pad_maximum_fusion.1), channel_id=1, source_target_pairs={{0,4},{4,0},{8,12},{12,8},{16,20},{20,16},{24,28},{28,24},{1,5},{5... | collective-permute-start | bytes 4718600 | tf_op jit(solution)/shard_map/ppermute | solution.py:287
  118.2 1.6 collective-permute-start.25
  119.8 4.3 %shard_map.41.refs_20_ = f32[32,2,256,1280]{3,2,1,0:T(8,128)} custom-call(bf16[32,32,256]{2,1,0:T(8,128)(2,1)S(1)} %get-tuple-element.140.refs_0_.refs_5_, bf16[32,32,256]{2,1,0:T(8,128)(2,1)S(1)} %get-tuple-element.143.refs_1_.refs_6_, ...), custom_call_target="tpu_custom_call", output_to_operand_aliasing={{}: (15, {})} | custom-call | tf_op jit(solution)/shard_map/pallas_call | solution.py:265
  125.7 1.7 collective-permute-done.25
  127.4 4.6 %shard_map.42.refs_20_ = f32[32,2,256,1280]{3,2,1,0:T(8,128)} custom-call(bf16[32,32,256]{2,1,0:T(8,128)(2,1)S(1)} %get-tuple-element.140.refs_0_.refs_5_, bf16[32,32,256]{2,1,0:T(8,128)(2,1)S(1)} %get-tuple-element.143.refs_1_.refs_6_, ...), custom_call_target="tpu_custom_call", output_to_operand_aliasing={{}: (20, {})} | custom-call | tf_op jit(solution)/shard_map/pallas_call | solution.py:265
  132.3 5.3 %collective-permute-start.28 = (bf16[2,24,64,256]{3,2,1,0:T(8,128)(2,1)S(1)}, bf16[2,24,64,256]{3,2,1,0:T(8,128)(2,1)S(1)}, u32[]{:S(2)}, u32[]{:S(2)}) collective-permute-start(bf16[2,24,64,256]{3,2,1,0:T(8,128)(2,1)S(1)} %pad_maximum_fusion.2), channel_id=1, source_target_pairs={{0,4},{4,0},{8,12},{12,8},{16,20},{20,16},{24,28},{28,24},{1,5},{5... | collective-permute-start | bytes 4718600 | tf_op jit(solution)/shard_map/ppermute | solution.py:287
  140.7 4.6 %shard_map.43.refs_20_ = f32[32,2,256,1280]{3,2,1,0:T(8,128)} custom-call(bf16[32,32,256]{2,1,0:T(8,128)(2,1)S(1)} %get-tuple-element.140.refs_0_.refs_5_, bf16[32,32,256]{2,1,0:T(8,128)(2,1)S(1)} %get-tuple-element.143.refs_1_.refs_6_, ...), custom_call_target="tpu_custom_call", output_to_operand_aliasing={{}: (20, {})} | custom-call | tf_op jit(solution)/shard_map/pallas_call | solution.py:265
  149.2 4.6 %shard_map.44.refs_30_ = f32[32,2,256,1280]{3,2,1,0:T(8,128)} custom-call(bf16[32,32,256]{2,1,0:T(8,128)(2,1)S(1)} %get-tuple-element.140.refs_0_.refs_5_, bf16[32,32,256]{2,1,0:T(8,128)(2,1)S(1)} %get-tuple-element.143.refs_1_.refs_6_, ...), custom_call_target="tpu_custom_call", output_to_operand_aliasing={{}: (20, {})} | custom-call | tf_op jit(solution)/shard_map/pallas_call | solution.py:265
  154.0 1.7 collective-permute-start.37
  155.7 6.6 %shard_map.45.refs_30_ = f32[32,2,256,1280]{3,2,1,0:T(8,128)} custom-call(bf16[32,32,256]{2,1,0:T(8,128)(2,1)S(1)} %get-tuple-element.140.refs_0_.refs_5_, bf16[32,32,256]{2,1,0:T(8,128)(2,1)S(1)} %get-tuple-element.143.refs_1_.refs_6_, ...), custom_call_target="tpu_custom_call", output_to_operand_aliasing={{}: (30, {})} | custom-call | tf_op jit(solution)/shard_map/pallas_call | solution.py:265
  162.3 5.0 %shard_map.46.refs_30_ = f32[32,2,256,1280]{3,2,1,0:T(8,128)} custom-call(bf16[32,32,256]{2,1,0:T(8,128)(2,1)S(1)} %get-tuple-element.140.refs_0_.refs_5_, bf16[32,32,256]{2,1,0:T(8,128)(2,1)S(1)} %get-tuple-element.143.refs_1_.refs_6_, ...), custom_call_target="tpu_custom_call", output_to_operand_aliasing={{}: (30, {})} | custom-call | tf_op jit(solution)/shard_map/pallas_call | solution.py:265
  167.2 5.0 %shard_map.47 = f32[32,2,256,1280]{3,2,1,0:T(8,128)} custom-call(bf16[32,32,256]{2,1,0:T(8,128)(2,1)S(1)} %get-tuple-element.140.refs_0_.refs_5_, bf16[32,32,256]{2,1,0:T(8,128)(2,1)S(1)} %get-tuple-element.143.refs_1_.refs_6_, ...), custom_call_target="tpu_custom_call", output_to_operand_aliasing={{}: (30, {})} | custom-call | tf_op jit(solution)/shard_map/pallas_call | solution.py:265
  (100 shorter events, 33.6 us)
Async XLA Ops:
  1.8 12.1 %collective-permute-start = (bf16[2,256,384]{2,1,0:T(8,128)(2,1)}, bf16[2,256,384]{2,1,0:T(8,128)(2,1)S(1)}, u32[]{:S(2)}, u32[]{:S(2)}) collective-permute-start(bf16[2,256,384]{2,1,0:T(8,128)(2,1)} %slice.4), channel_id=1, source_target_pairs={{1,0},{2,1},{3,2},{5,4},{6,5},{7,6},{9,8},{10,9},{11,10},{13,12},{... | collective-permute-start | bytes 1179656 | tf_op jit(solution)/shard_map/ppermute | solution.py:378
  11.2 12.5 %collective-permute-start.8 = (bf16[32,32,256]{2,1,0:T(8,128)(2,1)S(1)}, bf16[32,32,256]{2,1,0:T(8,128)(2,1)S(1)}, u32[]{:S(2)}, u32[]{:S(2)}) collective-permute-start(bf16[32,32,256]{2,1,0:T(8,128)(2,1)S(1)} %get-tuple-element.140.refs_0_.refs_5_), channel_id=1, source_target_pairs={{0,16},{4,20},{8,24},{12,28},{16,0},{20,4},{24,8},{28,12},{1,17},{... | collective-permute-start | bytes 1572872 | tf_op jit(solution)/shard_map/ppermute | solution.py:287
  19.6 8.0 %collective-permute-start.2 = (bf16[6,64,256]{2,1,0:T(8,128)(2,1)S(1)}, bf16[6,64,256]{2,1,0:T(8,128)(2,1)S(1)}, u32[]{:S(2)}, u32[]{:S(2)}) collective-permute-start(bf16[6,64,256]{2,1,0:T(8,128)(2,1)S(1)} %get-tuple-element.102), channel_id=1, source_target_pairs={{0,2},{1,3},{2,0},{3,1},{4,6},{5,7},{6,4},{7,5},{8,10},{9,11},{10,... | collective-permute-start | bytes 589832 | tf_op jit(solution)/shard_map/ppermute | solution.py:287
  19.9 20.6 %collective-permute-start.1 = (bf16[12,64,256]{2,1,0:T(8,128)(2,1)S(1)}, bf16[12,64,256]{2,1,0:T(8,128)(2,1)S(1)}, u32[]{:S(2)}, u32[]{:S(2)}) collective-permute-start(bf16[12,64,256]{2,1,0:T(8,128)(2,1)S(1)} %get-tuple-element.99), channel_id=1, source_target_pairs={{0,1},{1,0},{2,3},{3,2},{4,5},{5,4},{6,7},{7,6},{8,9},{9,8},{10,11... | collective-permute-start | bytes 1179656 | tf_op jit(solution)/shard_map/ppermute | solution.py:287
  21.1 12.3 %collective-permute-start.3 = (bf16[6,64,256]{2,1,0:T(8,128)(2,1)S(1)}, bf16[6,64,256]{2,1,0:T(8,128)(2,1)S(1)}, u32[]{:S(2)}, u32[]{:S(2)}) collective-permute-start(bf16[6,64,256]{2,1,0:T(8,128)(2,1)S(1)} %get-tuple-element.103), channel_id=1, source_target_pairs={{0,3},{1,2},{2,1},{3,0},{4,7},{5,6},{6,5},{7,4},{8,11},{9,10},{10,... | collective-permute-start | bytes 589832 | tf_op jit(solution)/shard_map/ppermute | solution.py:287
  22.4 18.3 %collective-permute-start.7 = (bf16[32,32,256]{2,1,0:T(8,128)(2,1)S(1)}, bf16[32,32,256]{2,1,0:T(8,128)(2,1)S(1)}, u32[]{:S(2)}, u32[]{:S(2)}) collective-permute-start(bf16[32,32,256]{2,1,0:T(8,128)(2,1)S(1)} %get-tuple-element.143.refs_1_.refs_6_), channel_id=1, source_target_pairs={{0,16},{4,20},{8,24},{12,28},{16,0},{20,4},{24,8},{28,12},{1,17},{... | collective-permute-start | bytes 1572872 | tf_op jit(solution)/shard_map/ppermute | solution.py:287
  23.8 18.2 %collective-permute-start.9 = (bf16[32,32,256]{2,1,0:T(8,128)(2,1)S(1)}, bf16[32,32,256]{2,1,0:T(8,128)(2,1)S(1)}, u32[]{:S(2)}, u32[]{:S(2)}) collective-permute-start(bf16[32,32,256]{2,1,0:T(8,128)(2,1)S(1)} %broadcast_select_fusion.4), channel_id=1, source_target_pairs={{0,8},{4,12},{8,0},{12,4},{16,24},{20,28},{24,16},{28,20},{1,9},{5... | collective-permute-start | bytes 1572872 | tf_op jit(solution)/shard_map/ppermute | solution.py:287
  33.4 18.7 %collective-permute-start.5 = (bf16[6,64,256]{2,1,0:T(8,128)(2,1)S(1)}, bf16[6,64,256]{2,1,0:T(8,128)(2,1)S(1)}, u32[]{:S(2)}, u32[]{:S(2)}) collective-permute-start(bf16[6,64,256]{2,1,0:T(8,128)(2,1)S(1)} %get-tuple-element.108), channel_id=1, source_target_pairs={{0,2},{1,3},{2,0},{3,1},{4,6},{5,7},{6,4},{7,5},{8,10},{9,11},{10,... | collective-permute-start | bytes 589832 | tf_op jit(solution)/shard_map/ppermute | solution.py:287
  39.3 18.0 %collective-permute-start.6 = (bf16[6,64,256]{2,1,0:T(8,128)(2,1)S(1)}, bf16[6,64,256]{2,1,0:T(8,128)(2,1)S(1)}, u32[]{:S(2)}, u32[]{:S(2)}) collective-permute-start(bf16[6,64,256]{2,1,0:T(8,128)(2,1)S(1)} %get-tuple-element.109), channel_id=1, source_target_pairs={{0,3},{1,2},{2,1},{3,0},{4,7},{5,6},{6,5},{7,4},{8,11},{9,10},{10,... | collective-permute-start | bytes 589832 | tf_op jit(solution)/shard_map/ppermute | solution.py:287
  40.6 18.0 %collective-permute-start.4 = (bf16[12,64,256]{2,1,0:T(8,128)(2,1)S(1)}, bf16[12,64,256]{2,1,0:T(8,128)(2,1)S(1)}, u32[]{:S(2)}, u32[]{:S(2)}) collective-permute-start(bf16[12,64,256]{2,1,0:T(8,128)(2,1)S(1)} %get-tuple-element.105), channel_id=1, source_target_pairs={{0,1},{1,0},{2,3},{3,2},{4,5},{5,4},{6,7},{7,6},{8,9},{9,8},{10,11... | collective-permute-start | bytes 1179656 | tf_op jit(solution)/shard_map/ppermute | solution.py:287
  40.6 35.5 %collective-permute-start.13 = (bf16[24,64,256]{2,1,0:T(8,128)(2,1)S(1)}, bf16[24,64,256]{2,1,0:T(8,128)(2,1)S(1)}, u32[]{:S(2)}, u32[]{:S(2)}) collective-permute-start(bf16[24,64,256]{2,1,0:T(8,128)(2,1)S(1)} %constant_dynamic-update-slice_fusion.3.refs_2_.refs_3_.refs_4_.refs_7_.refs_8_.refs_9_), channel_id=1, source_target_pairs={{0,16},{4,20},{8,24},{12,28},{16,0},{20,4},{24,8},{28,12},{1,17},{... | collective-permute-start | bytes 2359304 | tf_op jit(solution)/shard_map/ppermute | solution.py:287
  42.0 34.1 %collective-permute-start.14 = (bf16[32,32,256]{2,1,0:T(8,128)(2,1)S(1)}, bf16[32,32,256]{2,1,0:T(8,128)(2,1)S(1)}, u32[]{:S(2)}, u32[]{:S(2)}) collective-permute-start(bf16[32,32,256]{2,1,0:T(8,128)(2,1)S(1)} %broadcast_select_fusion.3), channel_id=1, source_target_pairs={{0,8},{4,12},{8,0},{12,4},{16,24},{20,28},{24,16},{28,20},{1,9},{5... | collective-permute-start | bytes 1572872 | tf_op jit(solution)/shard_map/ppermute | solution.py:287
  57.3 16.9 %collective-permute-start.11 = (bf16[6,64,256]{2,1,0:T(8,128)(2,1)S(1)}, bf16[6,64,256]{2,1,0:T(8,128)(2,1)S(1)}, u32[]{:S(2)}, u32[]{:S(2)}) collective-permute-start(bf16[6,64,256]{2,1,0:T(8,128)(2,1)S(1)} %get-tuple-element.117), channel_id=1, source_target_pairs={{0,2},{1,3},{2,0},{3,1},{4,6},{5,7},{6,4},{7,5},{8,10},{9,11},{10,... | collective-permute-start | bytes 589832 | tf_op jit(solution)/shard_map/ppermute | solution.py:287
  57.3 18.8 %collective-permute-start.12 = (bf16[6,64,256]{2,1,0:T(8,128)(2,1)S(1)}, bf16[6,64,256]{2,1,0:T(8,128)(2,1)S(1)}, u32[]{:S(2)}, u32[]{:S(2)}) collective-permute-start(bf16[6,64,256]{2,1,0:T(8,128)(2,1)S(1)} %get-tuple-element.118), channel_id=1, source_target_pairs={{0,3},{1,2},{2,1},{3,0},{4,7},{5,6},{6,5},{7,4},{8,11},{9,10},{10,... | collective-permute-start | bytes 589832 | tf_op jit(solution)/shard_map/ppermute | solution.py:287
  58.6 15.6 %collective-permute-start.10 = (bf16[8,64,256]{2,1,0:T(8,128)(2,1)S(1)}, bf16[8,64,256]{2,1,0:T(8,128)(2,1)S(1)}, u32[]{:S(2)}, u32[]{:S(2)}) collective-permute-start(bf16[8,64,256]{2,1,0:T(8,128)(2,1)S(1)} %get-tuple-element.114), channel_id=1, source_target_pairs={{0,1},{1,0},{2,3},{3,2},{4,5},{5,4},{6,7},{7,6},{8,9},{9,8},{10,11... | collective-permute-start | bytes 786440 | tf_op jit(solution)/shard_map/ppermute | solution.py:287
  76.2 18.6 %collective-permute-start.18 = (bf16[24,64,256]{2,1,0:T(8,128)(2,1)S(1)}, bf16[24,64,256]{2,1,0:T(8,128)(2,1)S(1)}, u32[]{:S(2)}, u32[]{:S(2)}) collective-permute-start(bf16[24,64,256]{2,1,0:T(8,128)(2,1)S(1)} %broadcast_select_fusion.1), channel_id=1, source_target_pairs={{0,8},{4,12},{8,0},{12,4},{16,24},{20,28},{24,16},{28,20},{1,9},{5... | collective-permute-start | bytes 2359304 | tf_op jit(solution)/shard_map/ppermute | solution.py:287
  77.5 17.7 %collective-permute-start.17 = (bf16[24,64,256]{2,1,0:T(8,128)(2,1)S(1)}, bf16[24,64,256]{2,1,0:T(8,128)(2,1)S(1)}, u32[]{:S(2)}, u32[]{:S(2)}) collective-permute-start(bf16[24,64,256]{2,1,0:T(8,128)(2,1)S(1)} %constant_dynamic-update-slice_fusion.6.refs_3_.refs_4_.refs_8_.refs_9_.refs_2_.refs_7_), channel_id=1, source_target_pairs={{0,16},{4,20},{8,24},{12,28},{16,0},{20,4},{24,8},{28,12},{1,17},{... | collective-permute-start | bytes 2359304 | tf_op jit(solution)/shard_map/ppermute | solution.py:287
  78.7 11.9 %collective-permute-start.15 = (bf16[6,64,256]{2,1,0:T(8,128)(2,1)S(1)}, bf16[6,64,256]{2,1,0:T(8,128)(2,1)S(1)}, u32[]{:S(2)}, u32[]{:S(2)}) collective-permute-start(bf16[6,64,256]{2,1,0:T(8,128)(2,1)S(1)} %get-tuple-element.127), channel_id=1, source_target_pairs={{0,2},{1,3},{2,0},{3,1},{4,6},{5,7},{6,4},{7,5},{8,10},{9,11},{10,... | collective-permute-start | bytes 589832 | tf_op jit(solution)/shard_map/ppermute | solution.py:287
  78.7 16.1 %collective-permute-start.16 = (bf16[6,64,256]{2,1,0:T(8,128)(2,1)S(1)}, bf16[6,64,256]{2,1,0:T(8,128)(2,1)S(1)}, u32[]{:S(2)}, u32[]{:S(2)}) collective-permute-start(bf16[6,64,256]{2,1,0:T(8,128)(2,1)S(1)} %get-tuple-element.128), channel_id=1, source_target_pairs={{0,3},{1,2},{2,1},{3,0},{4,7},{5,6},{6,5},{7,4},{8,11},{9,10},{10,... | collective-permute-start | bytes 589832 | tf_op jit(solution)/shard_map/ppermute | solution.py:287
  79.4 33.2 %collective-permute-start.23 = (bf16[4,32,32,256]{3,2,1,0:T(8,128)(2,1)S(1)}, bf16[4,32,32,256]{3,2,1,0:T(8,128)(2,1)S(1)}, u32[]{:S(2)}, u32[]{:S(2)}) collective-permute-start(bf16[4,32,32,256]{3,2,1,0:T(8,128)(2,1)S(1)} %pad_maximum_fusion), channel_id=1, source_target_pairs={{0,4},{4,0},{8,12},{12,8},{16,20},{20,16},{24,28},{28,24},{1,5},{5... | collective-permute-start | bytes 6291464 | tf_op jit(solution)/shard_map/ppermute | solution.py:287
  95.3 16.9 %collective-permute-start.22 = (bf16[24,64,256]{2,1,0:T(8,128)(2,1)S(1)}, bf16[24,64,256]{2,1,0:T(8,128)(2,1)S(1)}, u32[]{:S(2)}, u32[]{:S(2)}) collective-permute-start(bf16[24,64,256]{2,1,0:T(8,128)(2,1)S(1)} %broadcast_select_fusion), channel_id=1, source_target_pairs={{0,8},{4,12},{8,0},{12,4},{16,24},{20,28},{24,16},{28,20},{1,9},{5... | collective-permute-start | bytes 2359304 | tf_op jit(solution)/shard_map/ppermute | solution.py:287
  95.6 13.8 %collective-permute-start.21 = (bf16[20,64,256]{2,1,0:T(8,128)(2,1)S(1)}, bf16[20,64,256]{2,1,0:T(8,128)(2,1)S(1)}, u32[]{:S(2)}, u32[]{:S(2)}) collective-permute-start(bf16[20,64,256]{2,1,0:T(8,128)(2,1)S(1)} %constant_dynamic-update-slice_fusion.refs_3_.refs_4_.refs_8_.refs_9_.refs_2_.refs_7_), channel_id=1, source_target_pairs={{0,16},{4,20},{8,24},{12,28},{16,0},{20,4},{24,8},{28,12},{1,17},{... | collective-permute-start | bytes 1966088 | tf_op jit(solution)/shard_map/ppermute | solution.py:287
  96.9 11.6 %collective-permute-start.20 = (bf16[4,64,256]{2,1,0:T(8,128)(2,1)S(1)}, bf16[4,64,256]{2,1,0:T(8,128)(2,1)S(1)}, u32[]{:S(2)}, u32[]{:S(2)}) collective-permute-start(bf16[4,64,256]{2,1,0:T(8,128)(2,1)S(1)} %get-tuple-element.136), channel_id=1, source_target_pairs={{0,3},{1,2},{2,1},{3,0},{4,7},{5,6},{6,5},{7,4},{8,11},{9,10},{10,... | collective-permute-start | bytes 393224 | tf_op jit(solution)/shard_map/ppermute | solution.py:287
  112.2 13.1 %collective-permute-start.26 = (bf16[20,64,256]{2,1,0:T(8,128)(2,1)S(1)}, bf16[20,64,256]{2,1,0:T(8,128)(2,1)S(1)}, u32[]{:S(2)}, u32[]{:S(2)}) collective-permute-start(bf16[20,64,256]{2,1,0:T(8,128)(2,1)S(1)} %broadcast_select_fusion.2), channel_id=1, source_target_pairs={{0,8},{4,12},{8,0},{12,4},{16,24},{20,28},{24,16},{28,20},{1,9},{5... | collective-permute-start | bytes 1966088 | tf_op jit(solution)/shard_map/ppermute | solution.py:287
  112.9 14.5 %collective-permute-start.27 = (bf16[2,24,64,256]{3,2,1,0:T(8,128)(2,1)S(1)}, bf16[2,24,64,256]{3,2,1,0:T(8,128)(2,1)S(1)}, u32[]{:S(2)}, u32[]{:S(2)}) collective-permute-start(bf16[2,24,64,256]{3,2,1,0:T(8,128)(2,1)S(1)} %pad_maximum_fusion.1), channel_id=1, source_target_pairs={{0,4},{4,0},{8,12},{12,8},{16,20},{20,16},{24,28},{28,24},{1,5},{5... | collective-permute-start | bytes 4718600 | tf_op jit(solution)/shard_map/ppermute | solution.py:287
  117.0 20.7 %collective-permute-start.31 = (bf16[8,64,256]{2,1,0:T(8,128)(2,1)S(1)}, bf16[8,64,256]{2,1,0:T(8,128)(2,1)S(1)}, u32[]{:S(2)}, u32[]{:S(2)}) collective-permute-start(bf16[8,64,256]{2,1,0:T(8,128)(2,1)S(1)} %constant_dynamic-update-slice_fusion.13.refs_3_.refs_4_.refs_8_.refs_9_), channel_id=1, source_target_pairs={{0,16},{4,20},{8,24},{12,28},{16,0},{20,4},{24,8},{28,12},{1,17},{... | collective-permute-start | bytes 786440 | tf_op jit(solution)/shard_map/ppermute | solution.py:287
  118.2 9.2 %collective-permute-start.25 = (bf16[4,64,256]{2,1,0:T(8,128)(2,1)S(1)}, bf16[4,64,256]{2,1,0:T(8,128)(2,1)S(1)}, u32[]{:S(2)}, u32[]{:S(2)}) collective-permute-start(bf16[4,64,256]{2,1,0:T(8,128)(2,1)S(1)} %get-tuple-element.148), channel_id=1, source_target_pairs={{0,3},{1,2},{2,1},{3,0},{4,7},{5,6},{6,5},{7,4},{8,11},{9,10},{10,... | collective-permute-start | bytes 393224 | tf_op jit(solution)/shard_map/ppermute | solution.py:287
  125.4 12.2 %collective-permute-start.32 = (bf16[12,64,256]{2,1,0:T(8,128)(2,1)S(1)}, bf16[12,64,256]{2,1,0:T(8,128)(2,1)S(1)}, u32[]{:S(2)}, u32[]{:S(2)}) collective-permute-start(bf16[12,64,256]{2,1,0:T(8,128)(2,1)S(1)} %broadcast_select_fusion.5), channel_id=1, source_target_pairs={{0,8},{4,12},{8,0},{12,4},{16,24},{20,28},{24,16},{28,20},{1,9},{5... | collective-permute-start | bytes 1179656 | tf_op jit(solution)/shard_map/ppermute | solution.py:287
  132.3 8.4 %collective-permute-start.28 = (bf16[2,24,64,256]{3,2,1,0:T(8,128)(2,1)S(1)}, bf16[2,24,64,256]{3,2,1,0:T(8,128)(2,1)S(1)}, u32[]{:S(2)}, u32[]{:S(2)}) collective-permute-start(bf16[2,24,64,256]{3,2,1,0:T(8,128)(2,1)S(1)} %pad_maximum_fusion.2), channel_id=1, source_target_pairs={{0,4},{4,0},{8,12},{12,8},{16,20},{20,16},{24,28},{28,24},{1,5},{5... | collective-permute-start | bytes 4718600 | tf_op jit(solution)/shard_map/ppermute | solution.py:287
  137.7 8.2 %collective-permute-start.33 = (bf16[8,64,256]{2,1,0:T(8,128)(2,1)S(1)}, bf16[8,64,256]{2,1,0:T(8,128)(2,1)S(1)}, u32[]{:S(2)}, u32[]{:S(2)}) collective-permute-start(bf16[8,64,256]{2,1,0:T(8,128)(2,1)S(1)} %broadcast_select_fusion.7), channel_id=1, source_target_pairs={{0,8},{4,12},{8,0},{12,4},{16,24},{20,28},{24,16},{28,20},{1,9},{5... | collective-permute-start | bytes 786440 | tf_op jit(solution)/shard_map/ppermute | solution.py:287
  139.0 7.6 %collective-permute-start.34 = (bf16[8,64,256]{2,1,0:T(8,128)(2,1)S(1)}, bf16[8,64,256]{2,1,0:T(8,128)(2,1)S(1)}, u32[]{:S(2)}, u32[]{:S(2)}) collective-permute-start(bf16[8,64,256]{2,1,0:T(8,128)(2,1)S(1)} %constant_dynamic-update-slice_fusion.9.refs_3_.refs_4_.refs_8_.refs_9_), channel_id=1, source_target_pairs={{0,16},{4,20},{8,24},{12,28},{16,0},{20,4},{24,8},{28,12},{1,17},{... | collective-permute-start | bytes 786440 | tf_op jit(solution)/shard_map/ppermute | solution.py:287
  154.0 8.2 %collective-permute-start.37 = (bf16[4,8,64,256]{3,2,1,0:T(8,128)(2,1)S(1)}, bf16[4,8,64,256]{3,2,1,0:T(8,128)(2,1)S(1)}, u32[]{:S(2)}, u32[]{:S(2)}) collective-permute-start(bf16[4,8,64,256]{3,2,1,0:T(8,128)(2,1)S(1)} %pad_maximum_fusion.4), channel_id=1, source_target_pairs={{0,4},{4,0},{8,12},{12,8},{16,20},{20,16},{24,28},{28,24},{1,5},{5... | collective-permute-start | bytes 3145736 | tf_op jit(solution)/shard_map/ppermute | solution.py:287
  (10 other events, 54.0 us)

commit v3 on v2

--- a/solution.py
+++ b/solution.py
@@ -463,9 +463,9 @@
     t = tick(t, *z[4], lines[2].over_y, lines[1].over_x, a.over_core, total)
     z.append(over_z(5, t))
     lines.append(exchange(*z[4]))
-    lines[4].y(lines[3].over_y, t)
+    total = chunk(2, early)
+    lines[4].y(lines[3].over_y, t, total)
     lines[3].x(lines[2].over_x, t)
-    total = chunk(2, early)
     total = chunk(0, late)
     lines[1].core(lines[0].over_core, t, total)
     t = tick(t, *z[5], lines[3].over_y, lines[2].over_x, lines[0].over_core)

time: 175 us -> 174 us (level)
  starting transfers between devices: 49.1 us -> 37.8 us
  waiting for transfers between devices: 62.4 us -> 73.1 us
    ppermute x37, starting transfers between devices: 47 us -> 35.7 us  [swapped(): return lax.ppermute(x, axis, [(i, i ^ bit) for i in range(devices)])]
    ppermute x37, waiting for transfers between devices: 61 us -> 71.8 us  [swapped(): return lax.ppermute(x, axis, [(i, i ^ bit) for i in range(devices)])]
  transfers between devices with their start and end apart: 38 -> 38, of which waited for: 20 -> 18; matrix products, arithmetic and copies ran while one was open for 1% -> 1% of each run, Pallas kernels for 26% -> 26%
where the time goes in v3:
time: 174 us; the launch traced here: 172 us
  waiting for transfers between devices  73.1 us (42%)
  Pallas kernels  54.7 us (31%)
  starting transfers between devices  37.8 us (22%)
  local copies, waits for them, and re-layouts  3.64 us (2%)
  other arithmetic  2.11 us (1%)
    ppermute x37, waiting for transfers between devices, swapped(): return lax.ppermute(x, axis, [(i, i ^ bit) for i in range(devices)])  71.8 us
    pallas_call x9, Pallas kernels, pairs(): pl.pallas_call(body, grid=(size // step, steps), out_shape=jax.ShapeDtype...  43.3 us
    ppermute x37, starting transfers between devices, swapped(): return lax.ppermute(x, axis, [(i, i ^ bit) for i in range(devices)])  35.7 us
    pallas_call x2, Pallas kernels, spectra_part(): pl.pallas_call(functools.partial(spectra_kernel, {'halo': halo is not Non...  11.5 us
  transfers between devices with their start and end apart: 38, of which 18 were waited for; matrix products, arithmetic and copies ran while one was open for 1% of the time, Pallas kernels for 26%

profile of v3, /device:TPU:17, one launch (start us, length us, event | category | flops | bytes accessed | tf_op | source)
XLA Modules:
  0.0 171.7 jit_solution(14257069275665809508)
XLA Ops:
  1.8 2.1 %collective-permute-start = (bf16[2,256,384]{2,1,0:T(8,128)(2,1)}, bf16[2,256,384]{2,1,0:T(8,128)(2,1)S(1)}, u32[]{:S(2)}, u32[]{:S(2)}) collective-permute-start(bf16[2,256,384]{2,1,0:T(8,128)(2,1)} %slice.4), channel_id=1, source_target_pairs={{1,0},{2,1},{3,2},{5,4},{6,5},{7,6},{9,8},{10,9},{11,10},{13,12},{... | collective-permute-start | bytes 1179656 | tf_op jit(solution)/shard_map/ppermute | solution.py:378
  5.5 5.7 %shard_map.37 = (bf16[32,32,256]{2,1,0:T(8,128)(2,1)S(1)}, bf16[96,32,256]{2,1,0:T(8,128)(2,1)S(1)}) custom-call(s32[1]{0:T(128)} %bitcast.refs_0_, bf16[2,256,4096]{2,1,0:T(8,128)(2,1)} %refs_2_.3, bf16[2,256,4096]{2,1,0:T(8,128)(2,1)} %refs_2_.3, f32[4,128]{1,0:T(4,128)S(1)} %copy-done.2, bf16[2,256,256]{2,1,0:T(8,128)(2,1)S(1)} %copy-done), custom_call_target="tpu_custom_call" | custom-call | flops 1610612736 | bytes 4194304 | tf_op jit(solution)/shard_map/pallas_call | solution.py:146
  13.9 5.8 %shard_map.38 = (bf16[32,32,256]{2,1,0:T(8,128)(2,1)S(1)}, bf16[12,64,256]{2,1,0:T(8,128)(2,1)S(1)}, bf16[12,64,256]{2,1,0:T(8,128)(2,1)S(1)}, bf16[8,64,256]{2,...) custom-call(s32[1]{0:T(128)} %bitcast.refs_0_, ...), custom_call_target="tpu_custom_call" | custom-call | flops 1610612736 | bytes 4194304 | tf_op jit(solution)/shard_map/pallas_call | solution.py:146
  21.5 3.0 %collective-permute-start.1 = (bf16[12,64,256]{2,1,0:T(8,128)(2,1)S(1)}, bf16[12,64,256]{2,1,0:T(8,128)(2,1)S(1)}, u32[]{:S(2)}, u32[]{:S(2)}) collective-permute-start(bf16[12,64,256]{2,1,0:T(8,128)(2,1)S(1)} %get-tuple-element.99), channel_id=1, source_target_pairs={{0,1},{1,0},{2,3},{3,2},{4,5},{5,4},{6,7},{7,6},{8,9},{9,8},{10,11... | collective-permute-start | bytes 1179656 | tf_op jit(solution)/shard_map/ppermute | solution.py:287
  25.8 6.1 %collective-permute-done.2 = bf16[6,64,256]{2,1,0:T(8,128)(2,1)S(1)} collective-permute-done((bf16[6,64,256]{2,1,0:T(8,128)(2,1)S(1)}, bf16[6,64,256]{2,1,0:T(8,128)(2,1)S(1)}, u32[]{:S(2)}, u32[]{:S(2)}) %collective-permute-start.2) | collective-permute-done | bytes 196640 | tf_op jit(solution)/shard_map/ppermute | solution.py:287
  31.9 5.7 %collective-permute-done.3 = bf16[6,64,256]{2,1,0:T(8,128)(2,1)S(1)} collective-permute-done((bf16[6,64,256]{2,1,0:T(8,128)(2,1)S(1)}, bf16[6,64,256]{2,1,0:T(8,128)(2,1)S(1)}, u32[]{:S(2)}, u32[]{:S(2)}) %collective-permute-start.3) | collective-permute-done | bytes 196640 | tf_op jit(solution)/shard_map/ppermute | solution.py:287
  38.9 3.7 %collective-permute-start.4 = (bf16[12,64,256]{2,1,0:T(8,128)(2,1)S(1)}, bf16[12,64,256]{2,1,0:T(8,128)(2,1)S(1)}, u32[]{:S(2)}, u32[]{:S(2)}) collective-permute-start(bf16[12,64,256]{2,1,0:T(8,128)(2,1)S(1)} %get-tuple-element.105), channel_id=1, source_target_pairs={{0,1},{1,0},{2,3},{3,2},{4,5},{5,4},{6,7},{7,6},{8,9},{9,8},{10,11... | collective-permute-start | bytes 1179656 | tf_op jit(solution)/shard_map/ppermute | solution.py:287
  44.5 2.7 %collective-permute-done.5 = bf16[6,64,256]{2,1,0:T(8,128)(2,1)S(1)} collective-permute-done((bf16[6,64,256]{2,1,0:T(8,128)(2,1)S(1)}, bf16[6,64,256]{2,1,0:T(8,128)(2,1)S(1)}, u32[]{:S(2)}, u32[]{:S(2)}) %collective-permute-start.5) | collective-permute-done | bytes 196640 | tf_op jit(solution)/shard_map/ppermute | solution.py:287
  47.1 8.0 %collective-permute-done.6 = bf16[6,64,256]{2,1,0:T(8,128)(2,1)S(1)} collective-permute-done((bf16[6,64,256]{2,1,0:T(8,128)(2,1)S(1)}, bf16[6,64,256]{2,1,0:T(8,128)(2,1)S(1)}, u32[]{:S(2)}, u32[]{:S(2)}) %collective-permute-start.6) | collective-permute-done | bytes 196640 | tf_op jit(solution)/shard_map/ppermute | solution.py:287
  55.4 3.4 %collective-permute-done.4 = bf16[12,64,256]{2,1,0:T(8,128)(2,1)S(1)} collective-permute-done((bf16[12,64,256]{2,1,0:T(8,128)(2,1)S(1)}, bf16[12,64,256]{2,1,0:T(8,128)(2,1)S(1)}, u32[]{:S(2)}, u32[]{:S(2)}) %collective-permute-start.4) | collective-permute-done | bytes 393248 | tf_op jit(solution)/shard_map/ppermute | solution.py:287
  58.8 2.2 %collective-permute-start.10 = (bf16[8,64,256]{2,1,0:T(8,128)(2,1)S(1)}, bf16[8,64,256]{2,1,0:T(8,128)(2,1)S(1)}, u32[]{:S(2)}, u32[]{:S(2)}) collective-permute-start(bf16[8,64,256]{2,1,0:T(8,128)(2,1)S(1)} %get-tuple-element.114), channel_id=1, source_target_pairs={{0,1},{1,0},{2,3},{3,2},{4,5},{5,4},{6,7},{7,6},{8,9},{9,8},{10,11... | collective-permute-start | bytes 786440 | tf_op jit(solution)/shard_map/ppermute | solution.py:287
  61.1 9.8 %collective-permute-done.10 = bf16[8,64,256]{2,1,0:T(8,128)(2,1)S(1)} collective-permute-done((bf16[8,64,256]{2,1,0:T(8,128)(2,1)S(1)}, bf16[8,64,256]{2,1,0:T(8,128)(2,1)S(1)}, u32[]{:S(2)}, u32[]{:S(2)}) %collective-permute-start.10) | collective-permute-done | bytes 262176 | tf_op jit(solution)/shard_map/ppermute | solution.py:287
  71.6 2.5 %collective-permute-start.18 = (bf16[24,64,256]{2,1,0:T(8,128)(2,1)S(1)}, bf16[24,64,256]{2,1,0:T(8,128)(2,1)S(1)}, u32[]{:S(2)}, u32[]{:S(2)}) collective-permute-start(bf16[24,64,256]{2,1,0:T(8,128)(2,1)S(1)} %broadcast_select_fusion.1), channel_id=1, source_target_pairs={{0,8},{4,12},{8,0},{12,4},{16,24},{20,28},{24,16},{28,20},{1,9},{5... | collective-permute-start | bytes 2359304 | tf_op jit(solution)/shard_map/ppermute | solution.py:287
  74.6 2.2 %collective-permute-start.16 = (bf16[6,64,256]{2,1,0:T(8,128)(2,1)S(1)}, bf16[6,64,256]{2,1,0:T(8,128)(2,1)S(1)}, u32[]{:S(2)}, u32[]{:S(2)}) collective-permute-start(bf16[6,64,256]{2,1,0:T(8,128)(2,1)S(1)} %get-tuple-element.128), channel_id=1, source_target_pairs={{0,3},{1,2},{2,1},{3,0},{4,7},{5,6},{6,5},{7,4},{8,11},{9,10},{10,... | collective-permute-start | bytes 589832 | tf_op jit(solution)/shard_map/ppermute | solution.py:287
  77.3 2.1 %collective-permute-start.23 = (bf16[4,32,32,256]{3,2,1,0:T(8,128)(2,1)S(1)}, bf16[4,32,32,256]{3,2,1,0:T(8,128)(2,1)S(1)}, u32[]{:S(2)}, u32[]{:S(2)}) collective-permute-start(bf16[4,32,32,256]{3,2,1,0:T(8,128)(2,1)S(1)} %pad_maximum_fusion), channel_id=1, source_target_pairs={{0,4},{4,0},{8,12},{12,8},{16,20},{20,16},{24,28},{28,24},{1,5},{5... | collective-permute-start | bytes 6291464 | tf_op jit(solution)/shard_map/ppermute | solution.py:287
  79.4 4.3 %shard_map.39.refs_15_ = f32[32,2,256,1280]{3,2,1,0:T(8,128)} custom-call(bf16[32,32,256]{2,1,0:T(8,128)(2,1)S(1)} %get-tuple-element.140.refs_0_.refs_5_, bf16[32,32,256]{2,1,0:T(8,128)(2,1)S(1)} %get-tuple-element.143.refs_1_.refs_6_, bf16[24,64,256]{2,1,0:T(8,128)(2,1)S(1)} %constant_dynamic-update-slice_fusion.3.refs_2_.refs_3_.refs_4_.refs_7_.refs_8_.refs_9_, ...), custom_call_target="tpu_custom_call" | custom-call | tf_op jit(solution)/shard_map/pallas_call | solution.py:265
  83.7 10.9 %collective-permute-done.16 = bf16[6,64,256]{2,1,0:T(8,128)(2,1)S(1)} collective-permute-done((bf16[6,64,256]{2,1,0:T(8,128)(2,1)S(1)}, bf16[6,64,256]{2,1,0:T(8,128)(2,1)S(1)}, u32[]{:S(2)}, u32[]{:S(2)}) %collective-permute-start.16) | collective-permute-done | bytes 196640 | tf_op jit(solution)/shard_map/ppermute | solution.py:287
  95.9 4.4 %shard_map.40.refs_15_ = f32[32,2,256,1280]{3,2,1,0:T(8,128)} custom-call(bf16[32,32,256]{2,1,0:T(8,128)(2,1)S(1)} %get-tuple-element.140.refs_0_.refs_5_, bf16[32,32,256]{2,1,0:T(8,128)(2,1)S(1)} %get-tuple-element.143.refs_1_.refs_6_, ...), custom_call_target="tpu_custom_call", output_to_operand_aliasing={{}: (15, {})} | custom-call | tf_op jit(solution)/shard_map/pallas_call | solution.py:265
  100.3 4.0 %collective-permute-done.19 = bf16[4,64,256]{2,1,0:T(8,128)(2,1)S(1)} collective-permute-done((bf16[4,64,256]{2,1,0:T(8,128)(2,1)S(1)}, bf16[4,64,256]{2,1,0:T(8,128)(2,1)S(1)}, u32[]{:S(2)}, u32[]{:S(2)}) %collective-permute-start.19) | collective-permute-done | bytes 131104 | tf_op jit(solution)/shard_map/ppermute | solution.py:287
  104.3 2.9 %collective-permute-done.20 = bf16[4,64,256]{2,1,0:T(8,128)(2,1)S(1)} collective-permute-done((bf16[4,64,256]{2,1,0:T(8,128)(2,1)S(1)}, bf16[4,64,256]{2,1,0:T(8,128)(2,1)S(1)}, u32[]{:S(2)}, u32[]{:S(2)}) %collective-permute-start.20) | collective-permute-done | bytes 131104 | tf_op jit(solution)/shard_map/ppermute | solution.py:287
  107.3 3.0 %collective-permute-done.21.refs_13_.refs_14_.refs_27_ = bf16[20,64,256]{2,1,0:T(8,128)(2,1)S(1)} collective-permute-done((bf16[20,64,256]{2,1,0:T(8,128)(2,1)S(1)}, bf16[20,64,256]{2,1,0:T(8,128)(2,1)S(1)}, u32[]{:S(2)}, u32[]{:S(2)}) %collective-permute-start.21) | collective-permute-done | bytes 655392 | tf_op jit(solution)/shard_map/ppermute | solution.py:287
  111.0 2.2 %collective-permute-done.22.refs_13_.refs_14_.refs_12_.refs_17_ = bf16[24,64,256]{2,1,0:T(8,128)(2,1)S(1)} collective-permute-done((bf16[24,64,256]{2,1,0:T(8,128)(2,1)S(1)}, bf16[24,64,256]{2,1,0:T(8,128)(2,1)S(1)}, u32[]{:S(2)}, u32[]{:S(2)}) %collective-permute-start.22) | collective-permute-done | bytes 786464 | tf_op jit(solution)/shard_map/ppermute | solution.py:287
  113.9 1.9 %collective-permute-start.27 = (bf16[2,24,64,256]{3,2,1,0:T(8,128)(2,1)S(1)}, bf16[2,24,64,256]{3,2,1,0:T(8,128)(2,1)S(1)}, u32[]{:S(2)}, u32[]{:S(2)}) collective-permute-start(bf16[2,24,64,256]{3,2,1,0:T(8,128)(2,1)S(1)} %pad_maximum_fusion.1), channel_id=1, source_target_pairs={{0,4},{4,0},{8,12},{12,8},{16,20},{20,16},{24,28},{28,24},{1,5},{5... | collective-permute-start | bytes 4718600 | tf_op jit(solution)/shard_map/ppermute | solution.py:287
  115.7 4.3 %shard_map.41.refs_20_ = f32[32,2,256,1280]{3,2,1,0:T(8,128)} custom-call(bf16[32,32,256]{2,1,0:T(8,128)(2,1)S(1)} %get-tuple-element.140.refs_0_.refs_5_, bf16[32,32,256]{2,1,0:T(8,128)(2,1)S(1)} %get-tuple-element.143.refs_1_.refs_6_, ...), custom_call_target="tpu_custom_call", output_to_operand_aliasing={{}: (15, {})} | custom-call | tf_op jit(solution)/shard_map/pallas_call | solution.py:265
  120.8 7.2 %collective-permute-done.26.refs_13_.refs_14_.refs_17_ = bf16[20,64,256]{2,1,0:T(8,128)(2,1)S(1)} collective-permute-done((bf16[20,64,256]{2,1,0:T(8,128)(2,1)S(1)}, bf16[20,64,256]{2,1,0:T(8,128)(2,1)S(1)}, u32[]{:S(2)}, u32[]{:S(2)}) %collective-permute-start.26) | collective-permute-done | bytes 655392 | tf_op jit(solution)/shard_map/ppermute | solution.py:287
  128.4 2.8 %collective-permute-done.25 = bf16[4,64,256]{2,1,0:T(8,128)(2,1)S(1)} collective-permute-done((bf16[4,64,256]{2,1,0:T(8,128)(2,1)S(1)}, bf16[4,64,256]{2,1,0:T(8,128)(2,1)S(1)}, u32[]{:S(2)}, u32[]{:S(2)}) %collective-permute-start.25) | collective-permute-done | bytes 131104 | tf_op jit(solution)/shard_map/ppermute | solution.py:287
  131.2 4.6 %shard_map.42.refs_20_ = f32[32,2,256,1280]{3,2,1,0:T(8,128)} custom-call(bf16[32,32,256]{2,1,0:T(8,128)(2,1)S(1)} %get-tuple-element.140.refs_0_.refs_5_, bf16[32,32,256]{2,1,0:T(8,128)(2,1)S(1)} %get-tuple-element.143.refs_1_.refs_6_, ...), custom_call_target="tpu_custom_call", output_to_operand_aliasing={{}: (20, {})} | custom-call | tf_op jit(solution)/shard_map/pallas_call | solution.py:265
  140.7 4.6 %shard_map.43.refs_20_ = f32[32,2,256,1280]{3,2,1,0:T(8,128)} custom-call(bf16[32,32,256]{2,1,0:T(8,128)(2,1)S(1)} %get-tuple-element.140.refs_0_.refs_5_, bf16[32,32,256]{2,1,0:T(8,128)(2,1)S(1)} %get-tuple-element.143.refs_1_.refs_6_, ...), custom_call_target="tpu_custom_call", output_to_operand_aliasing={{}: (20, {})} | custom-call | tf_op jit(solution)/shard_map/pallas_call | solution.py:265
  149.3 4.6 %shard_map.44.refs_30_ = f32[32,2,256,1280]{3,2,1,0:T(8,128)} custom-call(bf16[32,32,256]{2,1,0:T(8,128)(2,1)S(1)} %get-tuple-element.140.refs_0_.refs_5_, bf16[32,32,256]{2,1,0:T(8,128)(2,1)S(1)} %get-tuple-element.143.refs_1_.refs_6_, ...), custom_call_target="tpu_custom_call", output_to_operand_aliasing={{}: (20, {})} | custom-call | tf_op jit(solution)/shard_map/pallas_call | solution.py:265
  155.2 6.6 %shard_map.45.refs_30_ = f32[32,2,256,1280]{3,2,1,0:T(8,128)} custom-call(bf16[32,32,256]{2,1,0:T(8,128)(2,1)S(1)} %get-tuple-element.140.refs_0_.refs_5_, bf16[32,32,256]{2,1,0:T(8,128)(2,1)S(1)} %get-tuple-element.143.refs_1_.refs_6_, ...), custom_call_target="tpu_custom_call", output_to_operand_aliasing={{}: (30, {})} | custom-call | tf_op jit(solution)/shard_map/pallas_call | solution.py:265
  161.8 5.0 %shard_map.46.refs_30_ = f32[32,2,256,1280]{3,2,1,0:T(8,128)} custom-call(bf16[32,32,256]{2,1,0:T(8,128)(2,1)S(1)} %get-tuple-element.140.refs_0_.refs_5_, bf16[32,32,256]{2,1,0:T(8,128)(2,1)S(1)} %get-tuple-element.143.refs_1_.refs_6_, ...), custom_call_target="tpu_custom_call", output_to_operand_aliasing={{}: (30, {})} | custom-call | tf_op jit(solution)/shard_map/pallas_call | solution.py:265
  166.7 5.0 %shard_map.47 = f32[32,2,256,1280]{3,2,1,0:T(8,128)} custom-call(bf16[32,32,256]{2,1,0:T(8,128)(2,1)S(1)} %get-tuple-element.140.refs_0_.refs_5_, bf16[32,32,256]{2,1,0:T(8,128)(2,1)S(1)} %get-tuple-element.143.refs_1_.refs_6_, ...), custom_call_target="tpu_custom_call", output_to_operand_aliasing={{}: (30, {})} | custom-call | tf_op jit(solution)/shard_map/pallas_call | solution.py:265
  (100 shorter events, 28.3 us)
Async XLA Ops:
  1.8 12.1 %collective-permute-start = (bf16[2,256,384]{2,1,0:T(8,128)(2,1)}, bf16[2,256,384]{2,1,0:T(8,128)(2,1)S(1)}, u32[]{:S(2)}, u32[]{:S(2)}) collective-permute-start(bf16[2,256,384]{2,1,0:T(8,128)(2,1)} %slice.4), channel_id=1, source_target_pairs={{1,0},{2,1},{3,2},{5,4},{6,5},{7,6},{9,8},{10,9},{11,10},{13,12},{... | collective-permute-start | bytes 1179656 | tf_op jit(solution)/shard_map/ppermute | solution.py:378
  11.2 13.3 %collective-permute-start.8 = (bf16[32,32,256]{2,1,0:T(8,128)(2,1)S(1)}, bf16[32,32,256]{2,1,0:T(8,128)(2,1)S(1)}, u32[]{:S(2)}, u32[]{:S(2)}) collective-permute-start(bf16[32,32,256]{2,1,0:T(8,128)(2,1)S(1)} %get-tuple-element.140.refs_0_.refs_5_), channel_id=1, source_target_pairs={{0,16},{4,20},{8,24},{12,28},{16,0},{20,4},{24,8},{28,12},{1,17},{... | collective-permute-start | bytes 1572872 | tf_op jit(solution)/shard_map/ppermute | solution.py:287
  19.6 12.3 %collective-permute-start.2 = (bf16[6,64,256]{2,1,0:T(8,128)(2,1)S(1)}, bf16[6,64,256]{2,1,0:T(8,128)(2,1)S(1)}, u32[]{:S(2)}, u32[]{:S(2)}) collective-permute-start(bf16[6,64,256]{2,1,0:T(8,128)(2,1)S(1)} %get-tuple-element.102), channel_id=1, source_target_pairs={{0,2},{1,3},{2,0},{3,1},{4,6},{5,7},{6,4},{7,5},{8,10},{9,11},{10,... | collective-permute-start | bytes 589832 | tf_op jit(solution)/shard_map/ppermute | solution.py:287
  19.9 17.7 %collective-permute-start.3 = (bf16[6,64,256]{2,1,0:T(8,128)(2,1)S(1)}, bf16[6,64,256]{2,1,0:T(8,128)(2,1)S(1)}, u32[]{:S(2)}, u32[]{:S(2)}) collective-permute-start(bf16[6,64,256]{2,1,0:T(8,128)(2,1)S(1)} %get-tuple-element.103), channel_id=1, source_target_pairs={{0,3},{1,2},{2,1},{3,0},{4,7},{5,6},{6,5},{7,4},{8,11},{9,10},{10,... | collective-permute-start | bytes 589832 | tf_op jit(solution)/shard_map/ppermute | solution.py:287
  20.9 21.8 %collective-permute-start.7 = (bf16[32,32,256]{2,1,0:T(8,128)(2,1)S(1)}, bf16[32,32,256]{2,1,0:T(8,128)(2,1)S(1)}, u32[]{:S(2)}, u32[]{:S(2)}) collective-permute-start(bf16[32,32,256]{2,1,0:T(8,128)(2,1)S(1)} %get-tuple-element.143.refs_1_.refs_6_), channel_id=1, source_target_pairs={{0,16},{4,20},{8,24},{12,28},{16,0},{20,4},{24,8},{28,12},{1,17},{... | collective-permute-start | bytes 1572872 | tf_op jit(solution)/shard_map/ppermute | solution.py:287
  21.5 17.4 %collective-permute-start.1 = (bf16[12,64,256]{2,1,0:T(8,128)(2,1)S(1)}, bf16[12,64,256]{2,1,0:T(8,128)(2,1)S(1)}, u32[]{:S(2)}, u32[]{:S(2)}) collective-permute-start(bf16[12,64,256]{2,1,0:T(8,128)(2,1)S(1)} %get-tuple-element.99), channel_id=1, source_target_pairs={{0,1},{1,0},{2,3},{3,2},{4,5},{5,4},{6,7},{7,6},{8,9},{9,8},{10,11... | collective-permute-start | bytes 1179656 | tf_op jit(solution)/shard_map/ppermute | solution.py:287
  24.6 18.2 %collective-permute-start.9 = (bf16[32,32,256]{2,1,0:T(8,128)(2,1)S(1)}, bf16[32,32,256]{2,1,0:T(8,128)(2,1)S(1)}, u32[]{:S(2)}, u32[]{:S(2)}) collective-permute-start(bf16[32,32,256]{2,1,0:T(8,128)(2,1)S(1)} %broadcast_select_fusion.4), channel_id=1, source_target_pairs={{0,8},{4,12},{8,0},{12,4},{16,24},{20,28},{24,16},{28,20},{1,9},{5... | collective-permute-start | bytes 1572872 | tf_op jit(solution)/shard_map/ppermute | solution.py:287
  37.6 9.5 %collective-permute-start.5 = (bf16[6,64,256]{2,1,0:T(8,128)(2,1)S(1)}, bf16[6,64,256]{2,1,0:T(8,128)(2,1)S(1)}, u32[]{:S(2)}, u32[]{:S(2)}) collective-permute-start(bf16[6,64,256]{2,1,0:T(8,128)(2,1)S(1)} %get-tuple-element.108), channel_id=1, source_target_pairs={{0,2},{1,3},{2,0},{3,1},{4,6},{5,7},{6,4},{7,5},{8,10},{9,11},{10,... | collective-permute-start | bytes 589832 | tf_op jit(solution)/shard_map/ppermute | solution.py:287
  37.6 17.4 %collective-permute-start.6 = (bf16[6,64,256]{2,1,0:T(8,128)(2,1)S(1)}, bf16[6,64,256]{2,1,0:T(8,128)(2,1)S(1)}, u32[]{:S(2)}, u32[]{:S(2)}) collective-permute-start(bf16[6,64,256]{2,1,0:T(8,128)(2,1)S(1)} %get-tuple-element.109), channel_id=1, source_target_pairs={{0,3},{1,2},{2,1},{3,0},{4,7},{5,6},{6,5},{7,4},{8,11},{9,10},{10,... | collective-permute-start | bytes 589832 | tf_op jit(solution)/shard_map/ppermute | solution.py:287
  38.9 20.0 %collective-permute-start.4 = (bf16[12,64,256]{2,1,0:T(8,128)(2,1)S(1)}, bf16[12,64,256]{2,1,0:T(8,128)(2,1)S(1)}, u32[]{:S(2)}, u32[]{:S(2)}) collective-permute-start(bf16[12,64,256]{2,1,0:T(8,128)(2,1)S(1)} %get-tuple-element.105), channel_id=1, source_target_pairs={{0,1},{1,0},{2,3},{3,2},{4,5},{5,4},{6,7},{7,6},{8,9},{9,8},{10,11... | collective-permute-start | bytes 1179656 | tf_op jit(solution)/shard_map/ppermute | solution.py:287
  42.7 28.8 %collective-permute-start.13 = (bf16[24,64,256]{2,1,0:T(8,128)(2,1)S(1)}, bf16[24,64,256]{2,1,0:T(8,128)(2,1)S(1)}, u32[]{:S(2)}, u32[]{:S(2)}) collective-permute-start(bf16[24,64,256]{2,1,0:T(8,128)(2,1)S(1)} %constant_dynamic-update-slice_fusion.3.refs_2_.refs_3_.refs_4_.refs_7_.refs_8_.refs_9_), channel_id=1, source_target_pairs={{0,16},{4,20},{8,24},{12,28},{16,0},{20,4},{24,8},{28,12},{1,17},{... | collective-permute-start | bytes 2359304 | tf_op jit(solution)/shard_map/ppermute | solution.py:287
  42.8 28.7 %collective-permute-start.14 = (bf16[32,32,256]{2,1,0:T(8,128)(2,1)S(1)}, bf16[32,32,256]{2,1,0:T(8,128)(2,1)S(1)}, u32[]{:S(2)}, u32[]{:S(2)}) collective-permute-start(bf16[32,32,256]{2,1,0:T(8,128)(2,1)S(1)} %broadcast_select_fusion.3), channel_id=1, source_target_pairs={{0,8},{4,12},{8,0},{12,4},{16,24},{20,28},{24,16},{28,20},{1,9},{5... | collective-permute-start | bytes 1572872 | tf_op jit(solution)/shard_map/ppermute | solution.py:287
  55.1 15.8 %collective-permute-start.11 = (bf16[6,64,256]{2,1,0:T(8,128)(2,1)S(1)}, bf16[6,64,256]{2,1,0:T(8,128)(2,1)S(1)}, u32[]{:S(2)}, u32[]{:S(2)}) collective-permute-start(bf16[6,64,256]{2,1,0:T(8,128)(2,1)S(1)} %get-tuple-element.117), channel_id=1, source_target_pairs={{0,2},{1,3},{2,0},{3,1},{4,6},{5,7},{6,4},{7,5},{8,10},{9,11},{10,... | collective-permute-start | bytes 589832 | tf_op jit(solution)/shard_map/ppermute | solution.py:287
  55.1 16.4 %collective-permute-start.12 = (bf16[6,64,256]{2,1,0:T(8,128)(2,1)S(1)}, bf16[6,64,256]{2,1,0:T(8,128)(2,1)S(1)}, u32[]{:S(2)}, u32[]{:S(2)}) collective-permute-start(bf16[6,64,256]{2,1,0:T(8,128)(2,1)S(1)} %get-tuple-element.118), channel_id=1, source_target_pairs={{0,3},{1,2},{2,1},{3,0},{4,7},{5,6},{6,5},{7,4},{8,11},{9,10},{10,... | collective-permute-start | bytes 589832 | tf_op jit(solution)/shard_map/ppermute | solution.py:287
  58.8 12.0 %collective-permute-start.10 = (bf16[8,64,256]{2,1,0:T(8,128)(2,1)S(1)}, bf16[8,64,256]{2,1,0:T(8,128)(2,1)S(1)}, u32[]{:S(2)}, u32[]{:S(2)}) collective-permute-start(bf16[8,64,256]{2,1,0:T(8,128)(2,1)S(1)} %get-tuple-element.114), channel_id=1, source_target_pairs={{0,1},{1,0},{2,3},{3,2},{4,5},{5,4},{6,7},{7,6},{8,9},{9,8},{10,11... | collective-permute-start | bytes 786440 | tf_op jit(solution)/shard_map/ppermute | solution.py:287
  71.6 23.0 %collective-permute-start.18 = (bf16[24,64,256]{2,1,0:T(8,128)(2,1)S(1)}, bf16[24,64,256]{2,1,0:T(8,128)(2,1)S(1)}, u32[]{:S(2)}, u32[]{:S(2)}) collective-permute-start(bf16[24,64,256]{2,1,0:T(8,128)(2,1)S(1)} %broadcast_select_fusion.1), channel_id=1, source_target_pairs={{0,8},{4,12},{8,0},{12,4},{16,24},{20,28},{24,16},{28,20},{1,9},{5... | collective-permute-start | bytes 2359304 | tf_op jit(solution)/shard_map/ppermute | solution.py:287
  74.1 20.5 %collective-permute-start.17 = (bf16[24,64,256]{2,1,0:T(8,128)(2,1)S(1)}, bf16[24,64,256]{2,1,0:T(8,128)(2,1)S(1)}, u32[]{:S(2)}, u32[]{:S(2)}) collective-permute-start(bf16[24,64,256]{2,1,0:T(8,128)(2,1)S(1)} %constant_dynamic-update-slice_fusion.6.refs_3_.refs_4_.refs_8_.refs_9_.refs_2_.refs_7_), channel_id=1, source_target_pairs={{0,16},{4,20},{8,24},{12,28},{16,0},{20,4},{24,8},{28,12},{1,17},{... | collective-permute-start | bytes 2359304 | tf_op jit(solution)/shard_map/ppermute | solution.py:287
  74.6 9.1 %collective-permute-start.15 = (bf16[6,64,256]{2,1,0:T(8,128)(2,1)S(1)}, bf16[6,64,256]{2,1,0:T(8,128)(2,1)S(1)}, u32[]{:S(2)}, u32[]{:S(2)}) collective-permute-start(bf16[6,64,256]{2,1,0:T(8,128)(2,1)S(1)} %get-tuple-element.127), channel_id=1, source_target_pairs={{0,2},{1,3},{2,0},{3,1},{4,6},{5,7},{6,4},{7,5},{8,10},{9,11},{10,... | collective-permute-start | bytes 589832 | tf_op jit(solution)/shard_map/ppermute | solution.py:287
  74.6 20.0 %collective-permute-start.16 = (bf16[6,64,256]{2,1,0:T(8,128)(2,1)S(1)}, bf16[6,64,256]{2,1,0:T(8,128)(2,1)S(1)}, u32[]{:S(2)}, u32[]{:S(2)}) collective-permute-start(bf16[6,64,256]{2,1,0:T(8,128)(2,1)S(1)} %get-tuple-element.128), channel_id=1, source_target_pairs={{0,3},{1,2},{2,1},{3,0},{4,7},{5,6},{6,5},{7,4},{8,11},{9,10},{10,... | collective-permute-start | bytes 589832 | tf_op jit(solution)/shard_map/ppermute | solution.py:287
  77.3 36.3 %collective-permute-start.23 = (bf16[4,32,32,256]{3,2,1,0:T(8,128)(2,1)S(1)}, bf16[4,32,32,256]{3,2,1,0:T(8,128)(2,1)S(1)}, u32[]{:S(2)}, u32[]{:S(2)}) collective-permute-start(bf16[4,32,32,256]{3,2,1,0:T(8,128)(2,1)S(1)} %pad_maximum_fusion), channel_id=1, source_target_pairs={{0,4},{4,0},{8,12},{12,8},{16,20},{20,16},{24,28},{28,24},{1,5},{5... | collective-permute-start | bytes 6291464 | tf_op jit(solution)/shard_map/ppermute | solution.py:287
  94.7 18.5 %collective-permute-start.22 = (bf16[24,64,256]{2,1,0:T(8,128)(2,1)S(1)}, bf16[24,64,256]{2,1,0:T(8,128)(2,1)S(1)}, u32[]{:S(2)}, u32[]{:S(2)}) collective-permute-start(bf16[24,64,256]{2,1,0:T(8,128)(2,1)S(1)} %broadcast_select_fusion), channel_id=1, source_target_pairs={{0,8},{4,12},{8,0},{12,4},{16,24},{20,28},{24,16},{28,20},{1,9},{5... | collective-permute-start | bytes 2359304 | tf_op jit(solution)/shard_map/ppermute | solution.py:287
  95.0 15.3 %collective-permute-start.21 = (bf16[20,64,256]{2,1,0:T(8,128)(2,1)S(1)}, bf16[20,64,256]{2,1,0:T(8,128)(2,1)S(1)}, u32[]{:S(2)}, u32[]{:S(2)}) collective-permute-start(bf16[20,64,256]{2,1,0:T(8,128)(2,1)S(1)} %constant_dynamic-update-slice_fusion.refs_3_.refs_4_.refs_8_.refs_9_.refs_2_.refs_7_), channel_id=1, source_target_pairs={{0,16},{4,20},{8,24},{12,28},{16,0},{20,4},{24,8},{28,12},{1,17},{... | collective-permute-start | bytes 1966088 | tf_op jit(solution)/shard_map/ppermute | solution.py:287
  95.8 8.5 %collective-permute-start.19 = (bf16[4,64,256]{2,1,0:T(8,128)(2,1)S(1)}, bf16[4,64,256]{2,1,0:T(8,128)(2,1)S(1)}, u32[]{:S(2)}, u32[]{:S(2)}) collective-permute-start(bf16[4,64,256]{2,1,0:T(8,128)(2,1)S(1)} %get-tuple-element.135), channel_id=1, source_target_pairs={{0,2},{1,3},{2,0},{3,1},{4,6},{5,7},{6,4},{7,5},{8,10},{9,11},{10,... | collective-permute-start | bytes 393224 | tf_op jit(solution)/shard_map/ppermute | solution.py:287
  95.8 11.5 %collective-permute-start.20 = (bf16[4,64,256]{2,1,0:T(8,128)(2,1)S(1)}, bf16[4,64,256]{2,1,0:T(8,128)(2,1)S(1)}, u32[]{:S(2)}, u32[]{:S(2)}) collective-permute-start(bf16[4,64,256]{2,1,0:T(8,128)(2,1)S(1)} %get-tuple-element.136), channel_id=1, source_target_pairs={{0,3},{1,2},{2,1},{3,0},{4,7},{5,6},{6,5},{7,4},{8,11},{9,10},{10,... | collective-permute-start | bytes 393224 | tf_op jit(solution)/shard_map/ppermute | solution.py:287
  110.3 9.7 %collective-permute-start.29 = (bf16[12,64,256]{2,1,0:T(8,128)(2,1)S(1)}, bf16[12,64,256]{2,1,0:T(8,128)(2,1)S(1)}, u32[]{:S(2)}, u32[]{:S(2)}) collective-permute-start(bf16[12,64,256]{2,1,0:T(8,128)(2,1)S(1)} %constant_dynamic-update-slice_fusion.11.refs_3_.refs_4_.refs_8_.refs_9_), channel_id=1, source_target_pairs={{0,16},{4,20},{8,24},{12,28},{16,0},{20,4},{24,8},{28,12},{1,17},{... | collective-permute-start | bytes 1179656 | tf_op jit(solution)/shard_map/ppermute | solution.py:287
  113.3 14.8 %collective-permute-start.26 = (bf16[20,64,256]{2,1,0:T(8,128)(2,1)S(1)}, bf16[20,64,256]{2,1,0:T(8,128)(2,1)S(1)}, u32[]{:S(2)}, u32[]{:S(2)}) collective-permute-start(bf16[20,64,256]{2,1,0:T(8,128)(2,1)S(1)} %broadcast_select_fusion.2), channel_id=1, source_target_pairs={{0,8},{4,12},{8,0},{12,4},{16,24},{20,28},{24,16},{28,20},{1,9},{5... | collective-permute-start | bytes 1966088 | tf_op jit(solution)/shard_map/ppermute | solution.py:287
  113.9 17.3 %collective-permute-start.27 = (bf16[2,24,64,256]{3,2,1,0:T(8,128)(2,1)S(1)}, bf16[2,24,64,256]{3,2,1,0:T(8,128)(2,1)S(1)}, u32[]{:S(2)}, u32[]{:S(2)}) collective-permute-start(bf16[2,24,64,256]{3,2,1,0:T(8,128)(2,1)S(1)} %pad_maximum_fusion.1), channel_id=1, source_target_pairs={{0,4},{4,0},{8,12},{12,8},{16,20},{20,16},{24,28},{28,24},{1,5},{5... | collective-permute-start | bytes 4718600 | tf_op jit(solution)/shard_map/ppermute | solution.py:287
  120.0 8.3 %collective-permute-start.24 = (bf16[4,64,256]{2,1,0:T(8,128)(2,1)S(1)}, bf16[4,64,256]{2,1,0:T(8,128)(2,1)S(1)}, u32[]{:S(2)}, u32[]{:S(2)}) collective-permute-start(bf16[4,64,256]{2,1,0:T(8,128)(2,1)S(1)} %get-tuple-element.147), channel_id=1, source_target_pairs={{0,2},{1,3},{2,0},{3,1},{4,6},{5,7},{6,4},{7,5},{8,10},{9,11},{10,... | collective-permute-start | bytes 393224 | tf_op jit(solution)/shard_map/ppermute | solution.py:287
  120.0 11.1 %collective-permute-start.25 = (bf16[4,64,256]{2,1,0:T(8,128)(2,1)S(1)}, bf16[4,64,256]{2,1,0:T(8,128)(2,1)S(1)}, u32[]{:S(2)}, u32[]{:S(2)}) collective-permute-start(bf16[4,64,256]{2,1,0:T(8,128)(2,1)S(1)} %get-tuple-element.148), channel_id=1, source_target_pairs={{0,3},{1,2},{2,1},{3,0},{4,7},{5,6},{6,5},{7,4},{8,11},{9,10},{10,... | collective-permute-start | bytes 393224 | tf_op jit(solution)/shard_map/ppermute | solution.py:287
  120.1 17.7 %collective-permute-start.31 = (bf16[8,64,256]{2,1,0:T(8,128)(2,1)S(1)}, bf16[8,64,256]{2,1,0:T(8,128)(2,1)S(1)}, u32[]{:S(2)}, u32[]{:S(2)}) collective-permute-start(bf16[8,64,256]{2,1,0:T(8,128)(2,1)S(1)} %constant_dynamic-update-slice_fusion.13.refs_3_.refs_4_.refs_8_.refs_9_), channel_id=1, source_target_pairs={{0,16},{4,20},{8,24},{12,28},{16,0},{20,4},{24,8},{28,12},{1,17},{... | collective-permute-start | bytes 786440 | tf_op jit(solution)/shard_map/ppermute | solution.py:287
  128.1 9.6 %collective-permute-start.32 = (bf16[12,64,256]{2,1,0:T(8,128)(2,1)S(1)}, bf16[12,64,256]{2,1,0:T(8,128)(2,1)S(1)}, u32[]{:S(2)}, u32[]{:S(2)}) collective-permute-start(bf16[12,64,256]{2,1,0:T(8,128)(2,1)S(1)} %broadcast_select_fusion.5), channel_id=1, source_target_pairs={{0,8},{4,12},{8,0},{12,4},{16,24},{20,28},{24,16},{28,20},{1,9},{5... | collective-permute-start | bytes 1179656 | tf_op jit(solution)/shard_map/ppermute | solution.py:287
  137.8 8.3 %collective-permute-start.33 = (bf16[8,64,256]{2,1,0:T(8,128)(2,1)S(1)}, bf16[8,64,256]{2,1,0:T(8,128)(2,1)S(1)}, u32[]{:S(2)}, u32[]{:S(2)}) collective-permute-start(bf16[8,64,256]{2,1,0:T(8,128)(2,1)S(1)} %broadcast_select_fusion.7), channel_id=1, source_target_pairs={{0,8},{4,12},{8,0},{12,4},{16,24},{20,28},{24,16},{28,20},{1,9},{5... | collective-permute-start | bytes 786440 | tf_op jit(solution)/shard_map/ppermute | solution.py:287
  (10 other events, 53.5 us)

commit v4 on v3

--- a/solution.py
+++ b/solution.py
@@ -376,7 +376,8 @@
     groups = frames_dev // GROUP // 2
     leading = voltages[:, :, : (tap_count - 1) * channels]
     halo = lax.ppermute(leading, "tf", [(i, i - 1) for i in range(1, devices)])
-    table = jnp.asarray(dft_tables(channels))
+    table = pltpu.with_memory_space_constraint(jnp.asarray(dft_tables(channels)), pltpu.HBM)
+    window = pltpu.with_memory_space_constraint(window, pltpu.HBM)
     me = lax.axis_index("tf").astype(jnp.int32).reshape(1)
     own_a, rest = spectra_part(
         voltages, None, window, table, me, devices, 0, groups, rest_cuts, None

time: 174 us -> 173 us (level)
  local copies, waits for them, and re-layouts: 3.64 us -> 1.26 us
  waiting for transfers between devices: 73.1 us -> 75.1 us
  transfers between devices with their start and end apart: 38 -> 38, of which waited for: 18 -> 15; matrix products, arithmetic and copies ran while one was open for 1% -> 1% of each run, Pallas kernels for 26% -> 26%
where the time goes in v4:
time: 173 us; the launch traced here: 172 us
  waiting for transfers between devices  75.1 us (43%)
  Pallas kernels  54.8 us (32%)
  starting transfers between devices  38 us (22%)
  other arithmetic  2.06 us (1%)
    ppermute x37, waiting for transfers between devices, swapped(): return lax.ppermute(x, axis, [(i, i ^ bit) for i in range(devices)])  72.3 us
    pallas_call x9, Pallas kernels, pairs(): pl.pallas_call(body, grid=(size // step, steps), out_shape=jax.ShapeDtype...  43.3 us
    ppermute x37, starting transfers between devices, swapped(): return lax.ppermute(x, axis, [(i, i ^ bit) for i in range(devices)])  35.9 us
    pallas_call x2, Pallas kernels, spectra_part(): pl.pallas_call(functools.partial(spectra_kernel, {'halo': halo is not Non...  11.6 us
  transfers between devices with their start and end apart: 38, of which 15 were waited for; matrix products, arithmetic and copies ran while one was open for 1% of the time, Pallas kernels for 26%

profile of v4, /device:TPU:17, one launch (start us, length us, event | category | flops | bytes accessed | tf_op | source)
XLA Modules:
  0.0 171.5 jit_solution(2813172963727488865)
XLA Ops:
  1.0 2.1 %collective-permute-start = (bf16[2,256,384]{2,1,0:T(8,128)(2,1)S(1)}, bf16[2,256,384]{2,1,0:T(8,128)(2,1)S(1)}, u32[]{:S(2)}, u32[]{:S(2)}) collective-permute-start(bf16[2,256,384]{2,1,0:T(8,128)(2,1)S(1)} %slice.4), channel_id=1, source_target_pairs={{1,0},{2,1},{3,2},{5,4},{6,5},{7,6},{9,8},{10,9},{11,10},{13,12},{... | collective-permute-start | bytes 1179656 | tf_op jit(solution)/shard_map/ppermute | solution.py:378
  3.1 5.7 %shard_map.37 = (bf16[32,32,256]{2,1,0:T(8,128)(2,1)S(1)}, bf16[96,32,256]{2,1,0:T(8,128)(2,1)S(1)}) custom-call(s32[1]{0:T(128)} %bitcast.refs_0_, bf16[2,256,4096]{2,1,0:T(8,128)(2,1)} %refs_2_.3, bf16[2,256,4096]{2,1,0:T(8,128)(2,1)} %refs_2_.3, f32[4,128]{1,0:T(4,128)} %refs_4_.2, bf16[2,256,256]{2,1,0:T(8,128)(2,1)} %constant.17.clone.refs_4_.refs_5_), custom_call_target="tpu_custom_call" | custom-call | flops 1610612736 | bytes 4194304 | tf_op jit(solution)/shard_map/pallas_call | solution.py:146
  10.2 2.7 %collective-permute-done.refs_3_ = bf16[2,256,384]{2,1,0:T(8,128)(2,1)S(1)} collective-permute-done((bf16[2,256,384]{2,1,0:T(8,128)(2,1)S(1)}, bf16[2,256,384]{2,1,0:T(8,128)(2,1)S(1)}, u32[]{:S(2)}, u32[]{:S(2)}) %collective-permute-start) | collective-permute-done | bytes 393248 | tf_op jit(solution)/shard_map/ppermute | solution.py:378
  12.9 5.8 %shard_map.38 = (bf16[32,32,256]{2,1,0:T(8,128)(2,1)S(1)}, bf16[12,64,256]{2,1,0:T(8,128)(2,1)S(1)}, bf16[12,64,256]{2,1,0:T(8,128)(2,1)S(1)}, bf16[8,64,256]{2,...) custom-call(s32[1]{0:T(128)} %bitcast.refs_0_, ...), custom_call_target="tpu_custom_call" | custom-call | flops 1610612736 | bytes 4194304 | tf_op jit(solution)/shard_map/pallas_call | solution.py:146
  20.5 3.1 %collective-permute-start.1 = (bf16[12,64,256]{2,1,0:T(8,128)(2,1)S(1)}, bf16[12,64,256]{2,1,0:T(8,128)(2,1)S(1)}, u32[]{:S(2)}, u32[]{:S(2)}) collective-permute-start(bf16[12,64,256]{2,1,0:T(8,128)(2,1)S(1)} %get-tuple-element.99), channel_id=1, source_target_pairs={{0,1},{1,0},{2,3},{3,2},{4,5},{5,4},{6,7},{7,6},{8,9},{9,8},{10,11... | collective-permute-start | bytes 1179656 | tf_op jit(solution)/shard_map/ppermute | solution.py:287
  25.0 6.1 %collective-permute-done.2 = bf16[6,64,256]{2,1,0:T(8,128)(2,1)S(1)} collective-permute-done((bf16[6,64,256]{2,1,0:T(8,128)(2,1)S(1)}, bf16[6,64,256]{2,1,0:T(8,128)(2,1)S(1)}, u32[]{:S(2)}, u32[]{:S(2)}) %collective-permute-start.2) | collective-permute-done | bytes 196640 | tf_op jit(solution)/shard_map/ppermute | solution.py:287
  31.0 4.4 %collective-permute-done.3 = bf16[6,64,256]{2,1,0:T(8,128)(2,1)S(1)} collective-permute-done((bf16[6,64,256]{2,1,0:T(8,128)(2,1)S(1)}, bf16[6,64,256]{2,1,0:T(8,128)(2,1)S(1)}, u32[]{:S(2)}, u32[]{:S(2)}) %collective-permute-start.3) | collective-permute-done | bytes 196640 | tf_op jit(solution)/shard_map/ppermute | solution.py:287
  35.4 2.2 %collective-permute-start.6 = (bf16[6,64,256]{2,1,0:T(8,128)(2,1)S(1)}, bf16[6,64,256]{2,1,0:T(8,128)(2,1)S(1)}, u32[]{:S(2)}, u32[]{:S(2)}) collective-permute-start(bf16[6,64,256]{2,1,0:T(8,128)(2,1)S(1)} %get-tuple-element.109), channel_id=1, source_target_pairs={{0,3},{1,2},{2,1},{3,0},{4,7},{5,6},{6,5},{7,4},{8,11},{9,10},{10,... | collective-permute-start | bytes 589832 | tf_op jit(solution)/shard_map/ppermute | solution.py:287
  41.6 13.5 %collective-permute-done.6 = bf16[6,64,256]{2,1,0:T(8,128)(2,1)S(1)} collective-permute-done((bf16[6,64,256]{2,1,0:T(8,128)(2,1)S(1)}, bf16[6,64,256]{2,1,0:T(8,128)(2,1)S(1)}, u32[]{:S(2)}, u32[]{:S(2)}) %collective-permute-start.6) | collective-permute-done | bytes 196640 | tf_op jit(solution)/shard_map/ppermute | solution.py:287
  55.1 3.5 %collective-permute-start.10 = (bf16[8,64,256]{2,1,0:T(8,128)(2,1)S(1)}, bf16[8,64,256]{2,1,0:T(8,128)(2,1)S(1)}, u32[]{:S(2)}, u32[]{:S(2)}) collective-permute-start(bf16[8,64,256]{2,1,0:T(8,128)(2,1)S(1)} %get-tuple-element.114), channel_id=1, source_target_pairs={{0,1},{1,0},{2,3},{3,2},{4,5},{5,4},{6,7},{7,6},{8,9},{9,8},{10,11... | collective-permute-start | bytes 786440 | tf_op jit(solution)/shard_map/ppermute | solution.py:287
  58.8 11.0 %collective-permute-done.10 = bf16[8,64,256]{2,1,0:T(8,128)(2,1)S(1)} collective-permute-done((bf16[8,64,256]{2,1,0:T(8,128)(2,1)S(1)}, bf16[8,64,256]{2,1,0:T(8,128)(2,1)S(1)}, u32[]{:S(2)}, u32[]{:S(2)}) %collective-permute-start.10) | collective-permute-done | bytes 262176 | tf_op jit(solution)/shard_map/ppermute | solution.py:287
  69.8 2.3 %collective-permute-done.12 = bf16[6,64,256]{2,1,0:T(8,128)(2,1)S(1)} collective-permute-done((bf16[6,64,256]{2,1,0:T(8,128)(2,1)S(1)}, bf16[6,64,256]{2,1,0:T(8,128)(2,1)S(1)}, u32[]{:S(2)}, u32[]{:S(2)}) %collective-permute-start.12) | collective-permute-done | bytes 196640 | tf_op jit(solution)/shard_map/ppermute | solution.py:287
  73.7 2.2 %collective-permute-start.16 = (bf16[6,64,256]{2,1,0:T(8,128)(2,1)S(1)}, bf16[6,64,256]{2,1,0:T(8,128)(2,1)S(1)}, u32[]{:S(2)}, u32[]{:S(2)}) collective-permute-start(bf16[6,64,256]{2,1,0:T(8,128)(2,1)S(1)} %get-tuple-element.128), channel_id=1, source_target_pairs={{0,3},{1,2},{2,1},{3,0},{4,7},{5,6},{6,5},{7,4},{8,11},{9,10},{10,... | collective-permute-start | bytes 589832 | tf_op jit(solution)/shard_map/ppermute | solution.py:287
  76.3 2.1 %collective-permute-start.23 = (bf16[4,32,32,256]{3,2,1,0:T(8,128)(2,1)S(1)}, bf16[4,32,32,256]{3,2,1,0:T(8,128)(2,1)S(1)}, u32[]{:S(2)}, u32[]{:S(2)}) collective-permute-start(bf16[4,32,32,256]{3,2,1,0:T(8,128)(2,1)S(1)} %pad_maximum_fusion), channel_id=1, source_target_pairs={{0,4},{4,0},{8,12},{12,8},{16,20},{20,16},{24,28},{28,24},{1,5},{5... | collective-permute-start | bytes 6291464 | tf_op jit(solution)/shard_map/ppermute | solution.py:287
  78.4 4.3 %shard_map.39.refs_15_ = f32[32,2,256,1280]{3,2,1,0:T(8,128)} custom-call(bf16[32,32,256]{2,1,0:T(8,128)(2,1)S(1)} %get-tuple-element.140.refs_0_.refs_5_, bf16[32,32,256]{2,1,0:T(8,128)(2,1)S(1)} %get-tuple-element.143.refs_1_.refs_6_, bf16[24,64,256]{2,1,0:T(8,128)(2,1)S(1)} %constant_dynamic-update-slice_fusion.3.refs_2_.refs_3_.refs_4_.refs_7_.refs_8_.refs_9_, ...), custom_call_target="tpu_custom_call" | custom-call | tf_op jit(solution)/shard_map/pallas_call | solution.py:265
  82.7 11.0 %collective-permute-done.16 = bf16[6,64,256]{2,1,0:T(8,128)(2,1)S(1)} collective-permute-done((bf16[6,64,256]{2,1,0:T(8,128)(2,1)S(1)}, bf16[6,64,256]{2,1,0:T(8,128)(2,1)S(1)}, u32[]{:S(2)}, u32[]{:S(2)}) %collective-permute-start.16) | collective-permute-done | bytes 196640 | tf_op jit(solution)/shard_map/ppermute | solution.py:287
  95.5 4.4 %shard_map.40.refs_15_ = f32[32,2,256,1280]{3,2,1,0:T(8,128)} custom-call(bf16[32,32,256]{2,1,0:T(8,128)(2,1)S(1)} %get-tuple-element.140.refs_0_.refs_5_, bf16[32,32,256]{2,1,0:T(8,128)(2,1)S(1)} %get-tuple-element.143.refs_1_.refs_6_, ...), custom_call_target="tpu_custom_call", output_to_operand_aliasing={{}: (15, {})} | custom-call | tf_op jit(solution)/shard_map/pallas_call | solution.py:265
  99.9 4.2 %collective-permute-done.19 = bf16[4,64,256]{2,1,0:T(8,128)(2,1)S(1)} collective-permute-done((bf16[4,64,256]{2,1,0:T(8,128)(2,1)S(1)}, bf16[4,64,256]{2,1,0:T(8,128)(2,1)S(1)}, u32[]{:S(2)}, u32[]{:S(2)}) %collective-permute-start.19) | collective-permute-done | bytes 131104 | tf_op jit(solution)/shard_map/ppermute | solution.py:287
  104.1 2.8 %collective-permute-done.20 = bf16[4,64,256]{2,1,0:T(8,128)(2,1)S(1)} collective-permute-done((bf16[4,64,256]{2,1,0:T(8,128)(2,1)S(1)}, bf16[4,64,256]{2,1,0:T(8,128)(2,1)S(1)}, u32[]{:S(2)}, u32[]{:S(2)}) %collective-permute-start.20) | collective-permute-done | bytes 131104 | tf_op jit(solution)/shard_map/ppermute | solution.py:287
  106.9 2.5 %collective-permute-done.21.refs_13_.refs_14_.refs_27_ = bf16[20,64,256]{2,1,0:T(8,128)(2,1)S(1)} collective-permute-done((bf16[20,64,256]{2,1,0:T(8,128)(2,1)S(1)}, bf16[20,64,256]{2,1,0:T(8,128)(2,1)S(1)}, u32[]{:S(2)}, u32[]{:S(2)}) %collective-permute-start.21) | collective-permute-done | bytes 655392 | tf_op jit(solution)/shard_map/ppermute | solution.py:287
  113.0 1.9 %collective-permute-start.27 = (bf16[2,24,64,256]{3,2,1,0:T(8,128)(2,1)S(1)}, bf16[2,24,64,256]{3,2,1,0:T(8,128)(2,1)S(1)}, u32[]{:S(2)}, u32[]{:S(2)}) collective-permute-start(bf16[2,24,64,256]{3,2,1,0:T(8,128)(2,1)S(1)} %pad_maximum_fusion.1), channel_id=1, source_target_pairs={{0,4},{4,0},{8,12},{12,8},{16,20},{20,16},{24,28},{28,24},{1,5},{5... | collective-permute-start | bytes 4718600 | tf_op jit(solution)/shard_map/ppermute | solution.py:287
  114.9 4.3 %shard_map.41.refs_20_ = f32[32,2,256,1280]{3,2,1,0:T(8,128)} custom-call(bf16[32,32,256]{2,1,0:T(8,128)(2,1)S(1)} %get-tuple-element.140.refs_0_.refs_5_, bf16[32,32,256]{2,1,0:T(8,128)(2,1)S(1)} %get-tuple-element.143.refs_1_.refs_6_, ...), custom_call_target="tpu_custom_call", output_to_operand_aliasing={{}: (15, {})} | custom-call | tf_op jit(solution)/shard_map/pallas_call | solution.py:265
  120.5 6.6 %collective-permute-done.26.refs_13_.refs_14_.refs_17_ = bf16[20,64,256]{2,1,0:T(8,128)(2,1)S(1)} collective-permute-done((bf16[20,64,256]{2,1,0:T(8,128)(2,1)S(1)}, bf16[20,64,256]{2,1,0:T(8,128)(2,1)S(1)}, u32[]{:S(2)}, u32[]{:S(2)}) %collective-permute-start.26) | collective-permute-done | bytes 655392 | tf_op jit(solution)/shard_map/ppermute | solution.py:287
  127.5 2.4 %collective-permute-done.25 = bf16[4,64,256]{2,1,0:T(8,128)(2,1)S(1)} collective-permute-done((bf16[4,64,256]{2,1,0:T(8,128)(2,1)S(1)}, bf16[4,64,256]{2,1,0:T(8,128)(2,1)S(1)}, u32[]{:S(2)}, u32[]{:S(2)}) %collective-permute-start.25) | collective-permute-done | bytes 131104 | tf_op jit(solution)/shard_map/ppermute | solution.py:287
  130.0 4.6 %shard_map.42.refs_20_ = f32[32,2,256,1280]{3,2,1,0:T(8,128)} custom-call(bf16[32,32,256]{2,1,0:T(8,128)(2,1)S(1)} %get-tuple-element.140.refs_0_.refs_5_, bf16[32,32,256]{2,1,0:T(8,128)(2,1)S(1)} %get-tuple-element.143.refs_1_.refs_6_, ...), custom_call_target="tpu_custom_call", output_to_operand_aliasing={{}: (20, {})} | custom-call | tf_op jit(solution)/shard_map/pallas_call | solution.py:265
  134.9 2.2 %collective-permute-start.28 = (bf16[2,24,64,256]{3,2,1,0:T(8,128)(2,1)S(1)}, bf16[2,24,64,256]{3,2,1,0:T(8,128)(2,1)S(1)}, u32[]{:S(2)}, u32[]{:S(2)}) collective-permute-start(bf16[2,24,64,256]{3,2,1,0:T(8,128)(2,1)S(1)} %pad_maximum_fusion.2), channel_id=1, source_target_pairs={{0,4},{4,0},{8,12},{12,8},{16,20},{20,16},{24,28},{28,24},{1,5},{5... | collective-permute-start | bytes 4718600 | tf_op jit(solution)/shard_map/ppermute | solution.py:287
  140.2 4.6 %shard_map.43.refs_20_ = f32[32,2,256,1280]{3,2,1,0:T(8,128)} custom-call(bf16[32,32,256]{2,1,0:T(8,128)(2,1)S(1)} %get-tuple-element.140.refs_0_.refs_5_, bf16[32,32,256]{2,1,0:T(8,128)(2,1)S(1)} %get-tuple-element.143.refs_1_.refs_6_, ...), custom_call_target="tpu_custom_call", output_to_operand_aliasing={{}: (20, {})} | custom-call | tf_op jit(solution)/shard_map/pallas_call | solution.py:265
  146.1 2.4 %collective-permute-done.30.refs_8_.refs_9_.refs_18_.refs_19_.refs_12_.refs_22_ = bf16[2,20,64,256]{3,2,1,0:T(8,128)(2,1)S(1)} collective-permute-done((bf16[2,20,64,256]{3,2,1,0:T(8,128)(2,1)S(1)}, bf16[2,20,64,256]{3,2,1,0:T(8,128)(2,1)S(1)}, u32[]{:S(2)}, u32[]{:S(2)}) %collective-permute-start.30) | collective-permute-done | bytes 1310752 | tf_op jit(solution)/shard_map/ppermute | solution.py:287
  149.1 4.6 %shard_map.44.refs_30_ = f32[32,2,256,1280]{3,2,1,0:T(8,128)} custom-call(bf16[32,32,256]{2,1,0:T(8,128)(2,1)S(1)} %get-tuple-element.140.refs_0_.refs_5_, bf16[32,32,256]{2,1,0:T(8,128)(2,1)S(1)} %get-tuple-element.143.refs_1_.refs_6_, ...), custom_call_target="tpu_custom_call", output_to_operand_aliasing={{}: (20, {})} | custom-call | tf_op jit(solution)/shard_map/pallas_call | solution.py:265
  155.0 6.5 %shard_map.45.refs_30_ = f32[32,2,256,1280]{3,2,1,0:T(8,128)} custom-call(bf16[32,32,256]{2,1,0:T(8,128)(2,1)S(1)} %get-tuple-element.140.refs_0_.refs_5_, bf16[32,32,256]{2,1,0:T(8,128)(2,1)S(1)} %get-tuple-element.143.refs_1_.refs_6_, ...), custom_call_target="tpu_custom_call", output_to_operand_aliasing={{}: (30, {})} | custom-call | tf_op jit(solution)/shard_map/pallas_call | solution.py:265
  161.6 5.0 %shard_map.46.refs_30_ = f32[32,2,256,1280]{3,2,1,0:T(8,128)} custom-call(bf16[32,32,256]{2,1,0:T(8,128)(2,1)S(1)} %get-tuple-element.140.refs_0_.refs_5_, bf16[32,32,256]{2,1,0:T(8,128)(2,1)S(1)} %get-tuple-element.143.refs_1_.refs_6_, ...), custom_call_target="tpu_custom_call", output_to_operand_aliasing={{}: (30, {})} | custom-call | tf_op jit(solution)/shard_map/pallas_call | solution.py:265
  166.5 5.0 %shard_map.47 = f32[32,2,256,1280]{3,2,1,0:T(8,128)} custom-call(bf16[32,32,256]{2,1,0:T(8,128)(2,1)S(1)} %get-tuple-element.140.refs_0_.refs_5_, bf16[32,32,256]{2,1,0:T(8,128)(2,1)S(1)} %get-tuple-element.143.refs_1_.refs_6_, ...), custom_call_target="tpu_custom_call", output_to_operand_aliasing={{}: (30, {})} | custom-call | tf_op jit(solution)/shard_map/pallas_call | solution.py:265
  (92 shorter events, 25.1 us)
Async XLA Ops:
  1.0 11.9 %collective-permute-start = (bf16[2,256,384]{2,1,0:T(8,128)(2,1)S(1)}, bf16[2,256,384]{2,1,0:T(8,128)(2,1)S(1)}, u32[]{:S(2)}, u32[]{:S(2)}) collective-permute-start(bf16[2,256,384]{2,1,0:T(8,128)(2,1)S(1)} %slice.4), channel_id=1, source_target_pairs={{1,0},{2,1},{3,2},{5,4},{6,5},{7,6},{9,8},{10,9},{11,10},{13,12},{... | collective-permute-start | bytes 1179656 | tf_op jit(solution)/shard_map/ppermute | solution.py:378
  8.9 14.7 %collective-permute-start.8 = (bf16[32,32,256]{2,1,0:T(8,128)(2,1)S(1)}, bf16[32,32,256]{2,1,0:T(8,128)(2,1)S(1)}, u32[]{:S(2)}, u32[]{:S(2)}) collective-permute-start(bf16[32,32,256]{2,1,0:T(8,128)(2,1)S(1)} %get-tuple-element.140.refs_0_.refs_5_), channel_id=1, source_target_pairs={{0,16},{4,20},{8,24},{12,28},{16,0},{20,4},{24,8},{28,12},{1,17},{... | collective-permute-start | bytes 1572872 | tf_op jit(solution)/shard_map/ppermute | solution.py:287
  18.8 12.3 %collective-permute-start.2 = (bf16[6,64,256]{2,1,0:T(8,128)(2,1)S(1)}, bf16[6,64,256]{2,1,0:T(8,128)(2,1)S(1)}, u32[]{:S(2)}, u32[]{:S(2)}) collective-permute-start(bf16[6,64,256]{2,1,0:T(8,128)(2,1)S(1)} %get-tuple-element.102), channel_id=1, source_target_pairs={{0,2},{1,3},{2,0},{3,1},{4,6},{5,7},{6,4},{7,5},{8,10},{9,11},{10,... | collective-permute-start | bytes 589832 | tf_op jit(solution)/shard_map/ppermute | solution.py:287
  19.0 16.4 %collective-permute-start.3 = (bf16[6,64,256]{2,1,0:T(8,128)(2,1)S(1)}, bf16[6,64,256]{2,1,0:T(8,128)(2,1)S(1)}, u32[]{:S(2)}, u32[]{:S(2)}) collective-permute-start(bf16[6,64,256]{2,1,0:T(8,128)(2,1)S(1)} %get-tuple-element.103), channel_id=1, source_target_pairs={{0,3},{1,2},{2,1},{3,0},{4,7},{5,6},{6,5},{7,4},{8,11},{9,10},{10,... | collective-permute-start | bytes 589832 | tf_op jit(solution)/shard_map/ppermute | solution.py:287
  19.3 20.3 %collective-permute-start.7 = (bf16[32,32,256]{2,1,0:T(8,128)(2,1)S(1)}, bf16[32,32,256]{2,1,0:T(8,128)(2,1)S(1)}, u32[]{:S(2)}, u32[]{:S(2)}) collective-permute-start(bf16[32,32,256]{2,1,0:T(8,128)(2,1)S(1)} %get-tuple-element.143.refs_1_.refs_6_), channel_id=1, source_target_pairs={{0,16},{4,20},{8,24},{12,28},{16,0},{20,4},{24,8},{28,12},{1,17},{... | collective-permute-start | bytes 1572872 | tf_op jit(solution)/shard_map/ppermute | solution.py:287
  20.5 17.1 %collective-permute-start.1 = (bf16[12,64,256]{2,1,0:T(8,128)(2,1)S(1)}, bf16[12,64,256]{2,1,0:T(8,128)(2,1)S(1)}, u32[]{:S(2)}, u32[]{:S(2)}) collective-permute-start(bf16[12,64,256]{2,1,0:T(8,128)(2,1)S(1)} %get-tuple-element.99), channel_id=1, source_target_pairs={{0,1},{1,0},{2,3},{3,2},{4,5},{5,4},{6,7},{7,6},{8,9},{9,8},{10,11... | collective-permute-start | bytes 1179656 | tf_op jit(solution)/shard_map/ppermute | solution.py:287
  23.7 16.6 %collective-permute-start.9 = (bf16[32,32,256]{2,1,0:T(8,128)(2,1)S(1)}, bf16[32,32,256]{2,1,0:T(8,128)(2,1)S(1)}, u32[]{:S(2)}, u32[]{:S(2)}) collective-permute-start(bf16[32,32,256]{2,1,0:T(8,128)(2,1)S(1)} %broadcast_select_fusion.4), channel_id=1, source_target_pairs={{0,8},{4,12},{8,0},{12,4},{16,24},{20,28},{24,16},{28,20},{1,9},{5... | collective-permute-start | bytes 1572872 | tf_op jit(solution)/shard_map/ppermute | solution.py:287
  35.4 19.7 %collective-permute-start.6 = (bf16[6,64,256]{2,1,0:T(8,128)(2,1)S(1)}, bf16[6,64,256]{2,1,0:T(8,128)(2,1)S(1)}, u32[]{:S(2)}, u32[]{:S(2)}) collective-permute-start(bf16[6,64,256]{2,1,0:T(8,128)(2,1)S(1)} %get-tuple-element.109), channel_id=1, source_target_pairs={{0,3},{1,2},{2,1},{3,0},{4,7},{5,6},{6,5},{7,4},{8,11},{9,10},{10,... | collective-permute-start | bytes 589832 | tf_op jit(solution)/shard_map/ppermute | solution.py:287
  37.6 17.5 %collective-permute-start.4 = (bf16[12,64,256]{2,1,0:T(8,128)(2,1)S(1)}, bf16[12,64,256]{2,1,0:T(8,128)(2,1)S(1)}, u32[]{:S(2)}, u32[]{:S(2)}) collective-permute-start(bf16[12,64,256]{2,1,0:T(8,128)(2,1)S(1)} %get-tuple-element.105), channel_id=1, source_target_pairs={{0,1},{1,0},{2,3},{3,2},{4,5},{5,4},{6,7},{7,6},{8,9},{9,8},{10,11... | collective-permute-start | bytes 1179656 | tf_op jit(solution)/shard_map/ppermute | solution.py:287
  39.5 32.6 %collective-permute-start.13 = (bf16[24,64,256]{2,1,0:T(8,128)(2,1)S(1)}, bf16[24,64,256]{2,1,0:T(8,128)(2,1)S(1)}, u32[]{:S(2)}, u32[]{:S(2)}) collective-permute-start(bf16[24,64,256]{2,1,0:T(8,128)(2,1)S(1)} %constant_dynamic-update-slice_fusion.3.refs_2_.refs_3_.refs_4_.refs_7_.refs_8_.refs_9_), channel_id=1, source_target_pairs={{0,16},{4,20},{8,24},{12,28},{16,0},{20,4},{24,8},{28,12},{1,17},{... | collective-permute-start | bytes 2359304 | tf_op jit(solution)/shard_map/ppermute | solution.py:287
  40.3 31.8 %collective-permute-start.14 = (bf16[32,32,256]{2,1,0:T(8,128)(2,1)S(1)}, bf16[32,32,256]{2,1,0:T(8,128)(2,1)S(1)}, u32[]{:S(2)}, u32[]{:S(2)}) collective-permute-start(bf16[32,32,256]{2,1,0:T(8,128)(2,1)S(1)} %broadcast_select_fusion.3), channel_id=1, source_target_pairs={{0,8},{4,12},{8,0},{12,4},{16,24},{20,28},{24,16},{28,20},{1,9},{5... | collective-permute-start | bytes 1572872 | tf_op jit(solution)/shard_map/ppermute | solution.py:287
  55.1 14.7 %collective-permute-start.11 = (bf16[6,64,256]{2,1,0:T(8,128)(2,1)S(1)}, bf16[6,64,256]{2,1,0:T(8,128)(2,1)S(1)}, u32[]{:S(2)}, u32[]{:S(2)}) collective-permute-start(bf16[6,64,256]{2,1,0:T(8,128)(2,1)S(1)} %get-tuple-element.117), channel_id=1, source_target_pairs={{0,2},{1,3},{2,0},{3,1},{4,6},{5,7},{6,4},{7,5},{8,10},{9,11},{10,... | collective-permute-start | bytes 589832 | tf_op jit(solution)/shard_map/ppermute | solution.py:287
  55.1 17.0 %collective-permute-start.12 = (bf16[6,64,256]{2,1,0:T(8,128)(2,1)S(1)}, bf16[6,64,256]{2,1,0:T(8,128)(2,1)S(1)}, u32[]{:S(2)}, u32[]{:S(2)}) collective-permute-start(bf16[6,64,256]{2,1,0:T(8,128)(2,1)S(1)} %get-tuple-element.118), channel_id=1, source_target_pairs={{0,3},{1,2},{2,1},{3,0},{4,7},{5,6},{6,5},{7,4},{8,11},{9,10},{10,... | collective-permute-start | bytes 589832 | tf_op jit(solution)/shard_map/ppermute | solution.py:287
  55.1 14.6 %collective-permute-start.10 = (bf16[8,64,256]{2,1,0:T(8,128)(2,1)S(1)}, bf16[8,64,256]{2,1,0:T(8,128)(2,1)S(1)}, u32[]{:S(2)}, u32[]{:S(2)}) collective-permute-start(bf16[8,64,256]{2,1,0:T(8,128)(2,1)S(1)} %get-tuple-element.114), channel_id=1, source_target_pairs={{0,1},{1,0},{2,3},{3,2},{4,5},{5,4},{6,7},{7,6},{8,9},{9,8},{10,11... | collective-permute-start | bytes 786440 | tf_op jit(solution)/shard_map/ppermute | solution.py:287
  72.2 21.5 %collective-permute-start.18 = (bf16[24,64,256]{2,1,0:T(8,128)(2,1)S(1)}, bf16[24,64,256]{2,1,0:T(8,128)(2,1)S(1)}, u32[]{:S(2)}, u32[]{:S(2)}) collective-permute-start(bf16[24,64,256]{2,1,0:T(8,128)(2,1)S(1)} %broadcast_select_fusion.1), channel_id=1, source_target_pairs={{0,8},{4,12},{8,0},{12,4},{16,24},{20,28},{24,16},{28,20},{1,9},{5... | collective-permute-start | bytes 2359304 | tf_op jit(solution)/shard_map/ppermute | solution.py:287
  72.4 21.3 %collective-permute-start.17 = (bf16[24,64,256]{2,1,0:T(8,128)(2,1)S(1)}, bf16[24,64,256]{2,1,0:T(8,128)(2,1)S(1)}, u32[]{:S(2)}, u32[]{:S(2)}) collective-permute-start(bf16[24,64,256]{2,1,0:T(8,128)(2,1)S(1)} %constant_dynamic-update-slice_fusion.6.refs_3_.refs_4_.refs_8_.refs_9_.refs_2_.refs_7_), channel_id=1, source_target_pairs={{0,16},{4,20},{8,24},{12,28},{16,0},{20,4},{24,8},{28,12},{1,17},{... | collective-permute-start | bytes 2359304 | tf_op jit(solution)/shard_map/ppermute | solution.py:287
  73.7 9.1 %collective-permute-start.15 = (bf16[6,64,256]{2,1,0:T(8,128)(2,1)S(1)}, bf16[6,64,256]{2,1,0:T(8,128)(2,1)S(1)}, u32[]{:S(2)}, u32[]{:S(2)}) collective-permute-start(bf16[6,64,256]{2,1,0:T(8,128)(2,1)S(1)} %get-tuple-element.127), channel_id=1, source_target_pairs={{0,2},{1,3},{2,0},{3,1},{4,6},{5,7},{6,4},{7,5},{8,10},{9,11},{10,... | collective-permute-start | bytes 589832 | tf_op jit(solution)/shard_map/ppermute | solution.py:287
  73.7 20.0 %collective-permute-start.16 = (bf16[6,64,256]{2,1,0:T(8,128)(2,1)S(1)}, bf16[6,64,256]{2,1,0:T(8,128)(2,1)S(1)}, u32[]{:S(2)}, u32[]{:S(2)}) collective-permute-start(bf16[6,64,256]{2,1,0:T(8,128)(2,1)S(1)} %get-tuple-element.128), channel_id=1, source_target_pairs={{0,3},{1,2},{2,1},{3,0},{4,7},{5,6},{6,5},{7,4},{8,11},{9,10},{10,... | collective-permute-start | bytes 589832 | tf_op jit(solution)/shard_map/ppermute | solution.py:287
  76.3 36.4 %collective-permute-start.23 = (bf16[4,32,32,256]{3,2,1,0:T(8,128)(2,1)S(1)}, bf16[4,32,32,256]{3,2,1,0:T(8,128)(2,1)S(1)}, u32[]{:S(2)}, u32[]{:S(2)}) collective-permute-start(bf16[4,32,32,256]{3,2,1,0:T(8,128)(2,1)S(1)} %pad_maximum_fusion), channel_id=1, source_target_pairs={{0,4},{4,0},{8,12},{12,8},{16,20},{20,16},{24,28},{28,24},{1,5},{5... | collective-permute-start | bytes 6291464 | tf_op jit(solution)/shard_map/ppermute | solution.py:287
  93.8 18.5 %collective-permute-start.22 = (bf16[24,64,256]{2,1,0:T(8,128)(2,1)S(1)}, bf16[24,64,256]{2,1,0:T(8,128)(2,1)S(1)}, u32[]{:S(2)}, u32[]{:S(2)}) collective-permute-start(bf16[24,64,256]{2,1,0:T(8,128)(2,1)S(1)} %broadcast_select_fusion), channel_id=1, source_target_pairs={{0,8},{4,12},{8,0},{12,4},{16,24},{20,28},{24,16},{28,20},{1,9},{5... | collective-permute-start | bytes 2359304 | tf_op jit(solution)/shard_map/ppermute | solution.py:287
  94.1 15.3 %collective-permute-start.21 = (bf16[20,64,256]{2,1,0:T(8,128)(2,1)S(1)}, bf16[20,64,256]{2,1,0:T(8,128)(2,1)S(1)}, u32[]{:S(2)}, u32[]{:S(2)}) collective-permute-start(bf16[20,64,256]{2,1,0:T(8,128)(2,1)S(1)} %constant_dynamic-update-slice_fusion.refs_3_.refs_4_.refs_8_.refs_9_.refs_2_.refs_7_), channel_id=1, source_target_pairs={{0,16},{4,20},{8,24},{12,28},{16,0},{20,4},{24,8},{28,12},{1,17},{... | collective-permute-start | bytes 1966088 | tf_op jit(solution)/shard_map/ppermute | solution.py:287
  95.4 8.7 %collective-permute-start.19 = (bf16[4,64,256]{2,1,0:T(8,128)(2,1)S(1)}, bf16[4,64,256]{2,1,0:T(8,128)(2,1)S(1)}, u32[]{:S(2)}, u32[]{:S(2)}) collective-permute-start(bf16[4,64,256]{2,1,0:T(8,128)(2,1)S(1)} %get-tuple-element.135), channel_id=1, source_target_pairs={{0,2},{1,3},{2,0},{3,1},{4,6},{5,7},{6,4},{7,5},{8,10},{9,11},{10,... | collective-permute-start | bytes 393224 | tf_op jit(solution)/shard_map/ppermute | solution.py:287
  95.4 11.5 %collective-permute-start.20 = (bf16[4,64,256]{2,1,0:T(8,128)(2,1)S(1)}, bf16[4,64,256]{2,1,0:T(8,128)(2,1)S(1)}, u32[]{:S(2)}, u32[]{:S(2)}) collective-permute-start(bf16[4,64,256]{2,1,0:T(8,128)(2,1)S(1)} %get-tuple-element.136), channel_id=1, source_target_pairs={{0,3},{1,2},{2,1},{3,0},{4,7},{5,6},{6,5},{7,4},{8,11},{9,10},{10,... | collective-permute-start | bytes 393224 | tf_op jit(solution)/shard_map/ppermute | solution.py:287
  109.4 9.7 %collective-permute-start.29 = (bf16[12,64,256]{2,1,0:T(8,128)(2,1)S(1)}, bf16[12,64,256]{2,1,0:T(8,128)(2,1)S(1)}, u32[]{:S(2)}, u32[]{:S(2)}) collective-permute-start(bf16[12,64,256]{2,1,0:T(8,128)(2,1)S(1)} %constant_dynamic-update-slice_fusion.11.refs_3_.refs_4_.refs_8_.refs_9_), channel_id=1, source_target_pairs={{0,16},{4,20},{8,24},{12,28},{16,0},{20,4},{24,8},{28,12},{1,17},{... | collective-permute-start | bytes 1179656 | tf_op jit(solution)/shard_map/ppermute | solution.py:287
  112.4 14.8 %collective-permute-start.26 = (bf16[20,64,256]{2,1,0:T(8,128)(2,1)S(1)}, bf16[20,64,256]{2,1,0:T(8,128)(2,1)S(1)}, u32[]{:S(2)}, u32[]{:S(2)}) collective-permute-start(bf16[20,64,256]{2,1,0:T(8,128)(2,1)S(1)} %broadcast_select_fusion.2), channel_id=1, source_target_pairs={{0,8},{4,12},{8,0},{12,4},{16,24},{20,28},{24,16},{28,20},{1,9},{5... | collective-permute-start | bytes 1966088 | tf_op jit(solution)/shard_map/ppermute | solution.py:287
  113.0 17.0 %collective-permute-start.27 = (bf16[2,24,64,256]{3,2,1,0:T(8,128)(2,1)S(1)}, bf16[2,24,64,256]{3,2,1,0:T(8,128)(2,1)S(1)}, u32[]{:S(2)}, u32[]{:S(2)}) collective-permute-start(bf16[2,24,64,256]{3,2,1,0:T(8,128)(2,1)S(1)} %pad_maximum_fusion.1), channel_id=1, source_target_pairs={{0,4},{4,0},{8,12},{12,8},{16,20},{20,16},{24,28},{28,24},{1,5},{5... | collective-permute-start | bytes 4718600 | tf_op jit(solution)/shard_map/ppermute | solution.py:287
  119.2 8.3 %collective-permute-start.24 = (bf16[4,64,256]{2,1,0:T(8,128)(2,1)S(1)}, bf16[4,64,256]{2,1,0:T(8,128)(2,1)S(1)}, u32[]{:S(2)}, u32[]{:S(2)}) collective-permute-start(bf16[4,64,256]{2,1,0:T(8,128)(2,1)S(1)} %get-tuple-element.147), channel_id=1, source_target_pairs={{0,2},{1,3},{2,0},{3,1},{4,6},{5,7},{6,4},{7,5},{8,10},{9,11},{10,... | collective-permute-start | bytes 393224 | tf_op jit(solution)/shard_map/ppermute | solution.py:287
  119.2 10.8 %collective-permute-start.25 = (bf16[4,64,256]{2,1,0:T(8,128)(2,1)S(1)}, bf16[4,64,256]{2,1,0:T(8,128)(2,1)S(1)}, u32[]{:S(2)}, u32[]{:S(2)}) collective-permute-start(bf16[4,64,256]{2,1,0:T(8,128)(2,1)S(1)} %get-tuple-element.148), channel_id=1, source_target_pairs={{0,3},{1,2},{2,1},{3,0},{4,7},{5,6},{6,5},{7,4},{8,11},{9,10},{10,... | collective-permute-start | bytes 393224 | tf_op jit(solution)/shard_map/ppermute | solution.py:287
  119.2 17.9 %collective-permute-start.31 = (bf16[8,64,256]{2,1,0:T(8,128)(2,1)S(1)}, bf16[8,64,256]{2,1,0:T(8,128)(2,1)S(1)}, u32[]{:S(2)}, u32[]{:S(2)}) collective-permute-start(bf16[8,64,256]{2,1,0:T(8,128)(2,1)S(1)} %constant_dynamic-update-slice_fusion.13.refs_3_.refs_4_.refs_8_.refs_9_), channel_id=1, source_target_pairs={{0,16},{4,20},{8,24},{12,28},{16,0},{20,4},{24,8},{28,12},{1,17},{... | collective-permute-start | bytes 786440 | tf_op jit(solution)/shard_map/ppermute | solution.py:287
  127.2 9.9 %collective-permute-start.32 = (bf16[12,64,256]{2,1,0:T(8,128)(2,1)S(1)}, bf16[12,64,256]{2,1,0:T(8,128)(2,1)S(1)}, u32[]{:S(2)}, u32[]{:S(2)}) collective-permute-start(bf16[12,64,256]{2,1,0:T(8,128)(2,1)S(1)} %broadcast_select_fusion.5), channel_id=1, source_target_pairs={{0,8},{4,12},{8,0},{12,4},{16,24},{20,28},{24,16},{28,20},{1,9},{5... | collective-permute-start | bytes 1179656 | tf_op jit(solution)/shard_map/ppermute | solution.py:287
  137.2 8.7 %collective-permute-start.33 = (bf16[8,64,256]{2,1,0:T(8,128)(2,1)S(1)}, bf16[8,64,256]{2,1,0:T(8,128)(2,1)S(1)}, u32[]{:S(2)}, u32[]{:S(2)}) collective-permute-start(bf16[8,64,256]{2,1,0:T(8,128)(2,1)S(1)} %broadcast_select_fusion.7), channel_id=1, source_target_pairs={{0,8},{4,12},{8,0},{12,4},{16,24},{20,28},{24,16},{28,20},{1,9},{5... | collective-permute-start | bytes 786440 | tf_op jit(solution)/shard_map/ppermute | solution.py:287
  137.6 8.2 %collective-permute-start.34 = (bf16[8,64,256]{2,1,0:T(8,128)(2,1)S(1)}, bf16[8,64,256]{2,1,0:T(8,128)(2,1)S(1)}, u32[]{:S(2)}, u32[]{:S(2)}) collective-permute-start(bf16[8,64,256]{2,1,0:T(8,128)(2,1)S(1)} %constant_dynamic-update-slice_fusion.9.refs_3_.refs_4_.refs_8_.refs_9_), channel_id=1, source_target_pairs={{0,16},{4,20},{8,24},{12,28},{16,0},{20,4},{24,8},{28,12},{1,17},{... | collective-permute-start | bytes 786440 | tf_op jit(solution)/shard_map/ppermute | solution.py:287
  (6 other events, 35.4 us)

commit v5 on v4

--- a/solution.py
+++ b/solution.py
@@ -177,35 +177,43 @@
                 got += [ref[m, channel] for m in range(ref.shape[0])]
         return got
 
+    def rows_of(channel):
+        values = pieces(mine, channel)
+        turned = []
+        for value in values:
+            size = 2 * PART_FRAMES
+            for first in range(0, value.shape[0], size):
+                turned.append(value[first + PART_FRAMES : first + size])
+                turned.append(-value[first : first + PART_FRAMES])
+        return jnp.concatenate(values, axis=0).T, jnp.concatenate(turned, axis=0).T
+
+    width = lefts.shape[2]
+    together = out.shape[-1] // width
+
+    def products(channel, j, left):
+        for k in range(together):
+            right = jnp.concatenate(pieces(per_block[j * together + k], channel), axis=0)
+            for part in range(2):
+                out[channel, part, :, k * width : (k + 1) * width] = (
+                    jnp.dot(left[part], right, preferred_element_type=jnp.float32) * scale
+                )
+
+    if together == len(wanted):
+        for channel in range(step):
+            products(channel, 0, rows_of(channel))
+        return
+
     @pl.when(pl.program_id(1) == 0)
     def _():
         for channel in range(step):
-            values = pieces(mine, channel)
-            turned = []
-            for value in values:
-                size = 2 * PART_FRAMES
-                for first in range(0, value.shape[0], size):
-                    turned.append(value[first + PART_FRAMES : first + size])
-                    turned.append(-value[first : first + PART_FRAMES])
-            lefts[channel, 0] = jnp.concatenate(values, axis=0).T
-            lefts[channel, 1] = jnp.concatenate(turned, axis=0).T
-
-    width = lefts.shape[2]
-    together = out.shape[-1] // width
+            lefts[channel, 0], lefts[channel, 1] = rows_of(channel)
+
     for j in range(len(wanted) // together):
 
         @pl.when(pl.program_id(1) == j)
         def _(j=j):
             for channel in range(step):
-                for k in range(together):
-                    right = jnp.concatenate(pieces(per_block[j * together + k], channel), axis=0)
-                    for part in range(2):
-                        out[channel, part, :, k * width : (k + 1) * width] = (
-                            jnp.dot(
-                                lefts[channel, part], right, preferred_element_type=jnp.float32
-                            )
-                            * scale
-                        )
+                products(channel, j, (lefts[channel, 0], lefts[channel, 1]))
 
 
 PART_FRAMES = 16

time: 173 us -> 173 us (level)
  no operation moved by 1% of the time
where the time goes in v5:
time: 173 us; the launch traced here: 172 us
  waiting for transfers between devices  75.1 us (43%)
  Pallas kernels  54.8 us (32%)
  starting transfers between devices  38 us (22%)
  other arithmetic  2.06 us (1%)
    ppermute x37, waiting for transfers between devices, swapped(): return lax.ppermute(x, axis, [(i, i ^ bit) for i in range(devices)])  72.3 us
    pallas_call x9, Pallas kernels, pairs(): pl.pallas_call(body, grid=(size // step, steps), out_shape=jax.ShapeDtype...  43.3 us
    ppermute x37, starting transfers between devices, swapped(): return lax.ppermute(x, axis, [(i, i ^ bit) for i in range(devices)])  35.9 us
    pallas_call x2, Pallas kernels, spectra_part(): pl.pallas_call(functools.partial(spectra_kernel, {'halo': halo is not Non...  11.6 us
  transfers between devices with their start and end apart: 38, of which 15 were waited for; matrix products, arithmetic and copies ran while one was open for 1% of the time, Pallas kernels for 26%

profile of v5, /device:TPU:17, one launch (start us, length us, event | category | flops | bytes accessed | tf_op | source)
XLA Modules:
  0.0 171.5 jit_solution(2813172963727488865)
XLA Ops:
  1.0 2.1 %collective-permute-start = (bf16[2,256,384]{2,1,0:T(8,128)(2,1)S(1)}, bf16[2,256,384]{2,1,0:T(8,128)(2,1)S(1)}, u32[]{:S(2)}, u32[]{:S(2)}) collective-permute-start(bf16[2,256,384]{2,1,0:T(8,128)(2,1)S(1)} %slice.4), channel_id=1, source_target_pairs={{1,0},{2,1},{3,2},{5,4},{6,5},{7,6},{9,8},{10,9},{11,10},{13,12},{... | collective-permute-start | bytes 1179656 | tf_op jit(solution)/shard_map/ppermute | solution.py:386
  3.1 5.7 %shard_map.37 = (bf16[32,32,256]{2,1,0:T(8,128)(2,1)S(1)}, bf16[96,32,256]{2,1,0:T(8,128)(2,1)S(1)}) custom-call(s32[1]{0:T(128)} %bitcast.refs_0_, bf16[2,256,4096]{2,1,0:T(8,128)(2,1)} %refs_2_.3, bf16[2,256,4096]{2,1,0:T(8,128)(2,1)} %refs_2_.3, f32[4,128]{1,0:T(4,128)} %refs_4_.2, bf16[2,256,256]{2,1,0:T(8,128)(2,1)} %constant.17.clone.refs_4_.refs_5_), custom_call_target="tpu_custom_call" | custom-call | flops 1610612736 | bytes 4194304 | tf_op jit(solution)/shard_map/pallas_call | solution.py:146
  10.2 2.7 %collective-permute-done.refs_3_ = bf16[2,256,384]{2,1,0:T(8,128)(2,1)S(1)} collective-permute-done((bf16[2,256,384]{2,1,0:T(8,128)(2,1)S(1)}, bf16[2,256,384]{2,1,0:T(8,128)(2,1)S(1)}, u32[]{:S(2)}, u32[]{:S(2)}) %collective-permute-start) | collective-permute-done | bytes 393248 | tf_op jit(solution)/shard_map/ppermute | solution.py:386
  12.9 5.8 %shard_map.38 = (bf16[32,32,256]{2,1,0:T(8,128)(2,1)S(1)}, bf16[12,64,256]{2,1,0:T(8,128)(2,1)S(1)}, bf16[12,64,256]{2,1,0:T(8,128)(2,1)S(1)}, bf16[8,64,256]{2,...) custom-call(s32[1]{0:T(128)} %bitcast.refs_0_, ...), custom_call_target="tpu_custom_call" | custom-call | flops 1610612736 | bytes 4194304 | tf_op jit(solution)/shard_map/pallas_call | solution.py:146
  20.5 3.1 %collective-permute-start.1 = (bf16[12,64,256]{2,1,0:T(8,128)(2,1)S(1)}, bf16[12,64,256]{2,1,0:T(8,128)(2,1)S(1)}, u32[]{:S(2)}, u32[]{:S(2)}) collective-permute-start(bf16[12,64,256]{2,1,0:T(8,128)(2,1)S(1)} %get-tuple-element.99), channel_id=1, source_target_pairs={{0,1},{1,0},{2,3},{3,2},{4,5},{5,4},{6,7},{7,6},{8,9},{9,8},{10,11... | collective-permute-start | bytes 1179656 | tf_op jit(solution)/shard_map/ppermute | solution.py:295
  25.0 6.1 %collective-permute-done.2 = bf16[6,64,256]{2,1,0:T(8,128)(2,1)S(1)} collective-permute-done((bf16[6,64,256]{2,1,0:T(8,128)(2,1)S(1)}, bf16[6,64,256]{2,1,0:T(8,128)(2,1)S(1)}, u32[]{:S(2)}, u32[]{:S(2)}) %collective-permute-start.2) | collective-permute-done | bytes 196640 | tf_op jit(solution)/shard_map/ppermute | solution.py:295
  31.0 4.4 %collective-permute-done.3 = bf16[6,64,256]{2,1,0:T(8,128)(2,1)S(1)} collective-permute-done((bf16[6,64,256]{2,1,0:T(8,128)(2,1)S(1)}, bf16[6,64,256]{2,1,0:T(8,128)(2,1)S(1)}, u32[]{:S(2)}, u32[]{:S(2)}) %collective-permute-start.3) | collective-permute-done | bytes 196640 | tf_op jit(solution)/shard_map/ppermute | solution.py:295
  35.4 2.2 %collective-permute-start.6 = (bf16[6,64,256]{2,1,0:T(8,128)(2,1)S(1)}, bf16[6,64,256]{2,1,0:T(8,128)(2,1)S(1)}, u32[]{:S(2)}, u32[]{:S(2)}) collective-permute-start(bf16[6,64,256]{2,1,0:T(8,128)(2,1)S(1)} %get-tuple-element.109), channel_id=1, source_target_pairs={{0,3},{1,2},{2,1},{3,0},{4,7},{5,6},{6,5},{7,4},{8,11},{9,10},{10,... | collective-permute-start | bytes 589832 | tf_op jit(solution)/shard_map/ppermute | solution.py:295
  41.6 13.5 %collective-permute-done.6 = bf16[6,64,256]{2,1,0:T(8,128)(2,1)S(1)} collective-permute-done((bf16[6,64,256]{2,1,0:T(8,128)(2,1)S(1)}, bf16[6,64,256]{2,1,0:T(8,128)(2,1)S(1)}, u32[]{:S(2)}, u32[]{:S(2)}) %collective-permute-start.6) | collective-permute-done | bytes 196640 | tf_op jit(solution)/shard_map/ppermute | solution.py:295
  55.1 3.5 %collective-permute-start.10 = (bf16[8,64,256]{2,1,0:T(8,128)(2,1)S(1)}, bf16[8,64,256]{2,1,0:T(8,128)(2,1)S(1)}, u32[]{:S(2)}, u32[]{:S(2)}) collective-permute-start(bf16[8,64,256]{2,1,0:T(8,128)(2,1)S(1)} %get-tuple-element.114), channel_id=1, source_target_pairs={{0,1},{1,0},{2,3},{3,2},{4,5},{5,4},{6,7},{7,6},{8,9},{9,8},{10,11... | collective-permute-start | bytes 786440 | tf_op jit(solution)/shard_map/ppermute | solution.py:295
  58.8 11.0 %collective-permute-done.10 = bf16[8,64,256]{2,1,0:T(8,128)(2,1)S(1)} collective-permute-done((bf16[8,64,256]{2,1,0:T(8,128)(2,1)S(1)}, bf16[8,64,256]{2,1,0:T(8,128)(2,1)S(1)}, u32[]{:S(2)}, u32[]{:S(2)}) %collective-permute-start.10) | collective-permute-done | bytes 262176 | tf_op jit(solution)/shard_map/ppermute | solution.py:295
  69.8 2.3 %collective-permute-done.12 = bf16[6,64,256]{2,1,0:T(8,128)(2,1)S(1)} collective-permute-done((bf16[6,64,256]{2,1,0:T(8,128)(2,1)S(1)}, bf16[6,64,256]{2,1,0:T(8,128)(2,1)S(1)}, u32[]{:S(2)}, u32[]{:S(2)}) %collective-permute-start.12) | collective-permute-done | bytes 196640 | tf_op jit(solution)/shard_map/ppermute | solution.py:295
  73.7 2.2 %collective-permute-start.16 = (bf16[6,64,256]{2,1,0:T(8,128)(2,1)S(1)}, bf16[6,64,256]{2,1,0:T(8,128)(2,1)S(1)}, u32[]{:S(2)}, u32[]{:S(2)}) collective-permute-start(bf16[6,64,256]{2,1,0:T(8,128)(2,1)S(1)} %get-tuple-element.128), channel_id=1, source_target_pairs={{0,3},{1,2},{2,1},{3,0},{4,7},{5,6},{6,5},{7,4},{8,11},{9,10},{10,... | collective-permute-start | bytes 589832 | tf_op jit(solution)/shard_map/ppermute | solution.py:295
  76.3 2.1 %collective-permute-start.23 = (bf16[4,32,32,256]{3,2,1,0:T(8,128)(2,1)S(1)}, bf16[4,32,32,256]{3,2,1,0:T(8,128)(2,1)S(1)}, u32[]{:S(2)}, u32[]{:S(2)}) collective-permute-start(bf16[4,32,32,256]{3,2,1,0:T(8,128)(2,1)S(1)} %pad_maximum_fusion), channel_id=1, source_target_pairs={{0,4},{4,0},{8,12},{12,8},{16,20},{20,16},{24,28},{28,24},{1,5},{5... | collective-permute-start | bytes 6291464 | tf_op jit(solution)/shard_map/ppermute | solution.py:295
  78.4 4.3 %shard_map.39.refs_15_ = f32[32,2,256,1280]{3,2,1,0:T(8,128)} custom-call(bf16[32,32,256]{2,1,0:T(8,128)(2,1)S(1)} %get-tuple-element.140.refs_0_.refs_5_, bf16[32,32,256]{2,1,0:T(8,128)(2,1)S(1)} %get-tuple-element.143.refs_1_.refs_6_, bf16[24,64,256]{2,1,0:T(8,128)(2,1)S(1)} %constant_dynamic-update-slice_fusion.3.refs_2_.refs_3_.refs_4_.refs_7_.refs_8_.refs_9_, ...), custom_call_target="tpu_custom_call" | custom-call | tf_op jit(solution)/shard_map/pallas_call | solution.py:273
  82.7 11.0 %collective-permute-done.16 = bf16[6,64,256]{2,1,0:T(8,128)(2,1)S(1)} collective-permute-done((bf16[6,64,256]{2,1,0:T(8,128)(2,1)S(1)}, bf16[6,64,256]{2,1,0:T(8,128)(2,1)S(1)}, u32[]{:S(2)}, u32[]{:S(2)}) %collective-permute-start.16) | collective-permute-done | bytes 196640 | tf_op jit(solution)/shard_map/ppermute | solution.py:295
  95.5 4.4 %shard_map.40.refs_15_ = f32[32,2,256,1280]{3,2,1,0:T(8,128)} custom-call(bf16[32,32,256]{2,1,0:T(8,128)(2,1)S(1)} %get-tuple-element.140.refs_0_.refs_5_, bf16[32,32,256]{2,1,0:T(8,128)(2,1)S(1)} %get-tuple-element.143.refs_1_.refs_6_, ...), custom_call_target="tpu_custom_call", output_to_operand_aliasing={{}: (15, {})} | custom-call | tf_op jit(solution)/shard_map/pallas_call | solution.py:273
  99.9 4.2 %collective-permute-done.19 = bf16[4,64,256]{2,1,0:T(8,128)(2,1)S(1)} collective-permute-done((bf16[4,64,256]{2,1,0:T(8,128)(2,1)S(1)}, bf16[4,64,256]{2,1,0:T(8,128)(2,1)S(1)}, u32[]{:S(2)}, u32[]{:S(2)}) %collective-permute-start.19) | collective-permute-done | bytes 131104 | tf_op jit(solution)/shard_map/ppermute | solution.py:295
  104.1 2.8 %collective-permute-done.20 = bf16[4,64,256]{2,1,0:T(8,128)(2,1)S(1)} collective-permute-done((bf16[4,64,256]{2,1,0:T(8,128)(2,1)S(1)}, bf16[4,64,256]{2,1,0:T(8,128)(2,1)S(1)}, u32[]{:S(2)}, u32[]{:S(2)}) %collective-permute-start.20) | collective-permute-done | bytes 131104 | tf_op jit(solution)/shard_map/ppermute | solution.py:295
  106.9 2.5 %collective-permute-done.21.refs_13_.refs_14_.refs_27_ = bf16[20,64,256]{2,1,0:T(8,128)(2,1)S(1)} collective-permute-done((bf16[20,64,256]{2,1,0:T(8,128)(2,1)S(1)}, bf16[20,64,256]{2,1,0:T(8,128)(2,1)S(1)}, u32[]{:S(2)}, u32[]{:S(2)}) %collective-permute-start.21) | collective-permute-done | bytes 655392 | tf_op jit(solution)/shard_map/ppermute | solution.py:295
  113.0 1.9 %collective-permute-start.27 = (bf16[2,24,64,256]{3,2,1,0:T(8,128)(2,1)S(1)}, bf16[2,24,64,256]{3,2,1,0:T(8,128)(2,1)S(1)}, u32[]{:S(2)}, u32[]{:S(2)}) collective-permute-start(bf16[2,24,64,256]{3,2,1,0:T(8,128)(2,1)S(1)} %pad_maximum_fusion.1), channel_id=1, source_target_pairs={{0,4},{4,0},{8,12},{12,8},{16,20},{20,16},{24,28},{28,24},{1,5},{5... | collective-permute-start | bytes 4718600 | tf_op jit(solution)/shard_map/ppermute | solution.py:295
  114.9 4.3 %shard_map.41.refs_20_ = f32[32,2,256,1280]{3,2,1,0:T(8,128)} custom-call(bf16[32,32,256]{2,1,0:T(8,128)(2,1)S(1)} %get-tuple-element.140.refs_0_.refs_5_, bf16[32,32,256]{2,1,0:T(8,128)(2,1)S(1)} %get-tuple-element.143.refs_1_.refs_6_, ...), custom_call_target="tpu_custom_call", output_to_operand_aliasing={{}: (15, {})} | custom-call | tf_op jit(solution)/shard_map/pallas_call | solution.py:273
  120.5 6.6 %collective-permute-done.26.refs_13_.refs_14_.refs_17_ = bf16[20,64,256]{2,1,0:T(8,128)(2,1)S(1)} collective-permute-done((bf16[20,64,256]{2,1,0:T(8,128)(2,1)S(1)}, bf16[20,64,256]{2,1,0:T(8,128)(2,1)S(1)}, u32[]{:S(2)}, u32[]{:S(2)}) %collective-permute-start.26) | collective-permute-done | bytes 655392 | tf_op jit(solution)/shard_map/ppermute | solution.py:295
  127.5 2.4 %collective-permute-done.25 = bf16[4,64,256]{2,1,0:T(8,128)(2,1)S(1)} collective-permute-done((bf16[4,64,256]{2,1,0:T(8,128)(2,1)S(1)}, bf16[4,64,256]{2,1,0:T(8,128)(2,1)S(1)}, u32[]{:S(2)}, u32[]{:S(2)}) %collective-permute-start.25) | collective-permute-done | bytes 131104 | tf_op jit(solution)/shard_map/ppermute | solution.py:295
  130.0 4.6 %shard_map.42.refs_20_ = f32[32,2,256,1280]{3,2,1,0:T(8,128)} custom-call(bf16[32,32,256]{2,1,0:T(8,128)(2,1)S(1)} %get-tuple-element.140.refs_0_.refs_5_, bf16[32,32,256]{2,1,0:T(8,128)(2,1)S(1)} %get-tuple-element.143.refs_1_.refs_6_, ...), custom_call_target="tpu_custom_call", output_to_operand_aliasing={{}: (20, {})} | custom-call | tf_op jit(solution)/shard_map/pallas_call | solution.py:273
  134.9 2.2 %collective-permute-start.28 = (bf16[2,24,64,256]{3,2,1,0:T(8,128)(2,1)S(1)}, bf16[2,24,64,256]{3,2,1,0:T(8,128)(2,1)S(1)}, u32[]{:S(2)}, u32[]{:S(2)}) collective-permute-start(bf16[2,24,64,256]{3,2,1,0:T(8,128)(2,1)S(1)} %pad_maximum_fusion.2), channel_id=1, source_target_pairs={{0,4},{4,0},{8,12},{12,8},{16,20},{20,16},{24,28},{28,24},{1,5},{5... | collective-permute-start | bytes 4718600 | tf_op jit(solution)/shard_map/ppermute | solution.py:295
  140.2 4.6 %shard_map.43.refs_20_ = f32[32,2,256,1280]{3,2,1,0:T(8,128)} custom-call(bf16[32,32,256]{2,1,0:T(8,128)(2,1)S(1)} %get-tuple-element.140.refs_0_.refs_5_, bf16[32,32,256]{2,1,0:T(8,128)(2,1)S(1)} %get-tuple-element.143.refs_1_.refs_6_, ...), custom_call_target="tpu_custom_call", output_to_operand_aliasing={{}: (20, {})} | custom-call | tf_op jit(solution)/shard_map/pallas_call | solution.py:273
  146.1 2.4 %collective-permute-done.30.refs_8_.refs_9_.refs_18_.refs_19_.refs_12_.refs_22_ = bf16[2,20,64,256]{3,2,1,0:T(8,128)(2,1)S(1)} collective-permute-done((bf16[2,20,64,256]{3,2,1,0:T(8,128)(2,1)S(1)}, bf16[2,20,64,256]{3,2,1,0:T(8,128)(2,1)S(1)}, u32[]{:S(2)}, u32[]{:S(2)}) %collective-permute-start.30) | collective-permute-done | bytes 1310752 | tf_op jit(solution)/shard_map/ppermute | solution.py:295
  149.1 4.6 %shard_map.44.refs_30_ = f32[32,2,256,1280]{3,2,1,0:T(8,128)} custom-call(bf16[32,32,256]{2,1,0:T(8,128)(2,1)S(1)} %get-tuple-element.140.refs_0_.refs_5_, bf16[32,32,256]{2,1,0:T(8,128)(2,1)S(1)} %get-tuple-element.143.refs_1_.refs_6_, ...), custom_call_target="tpu_custom_call", output_to_operand_aliasing={{}: (20, {})} | custom-call | tf_op jit(solution)/shard_map/pallas_call | solution.py:273
  155.0 6.5 %shard_map.45.refs_30_ = f32[32,2,256,1280]{3,2,1,0:T(8,128)} custom-call(bf16[32,32,256]{2,1,0:T(8,128)(2,1)S(1)} %get-tuple-element.140.refs_0_.refs_5_, bf16[32,32,256]{2,1,0:T(8,128)(2,1)S(1)} %get-tuple-element.143.refs_1_.refs_6_, ...), custom_call_target="tpu_custom_call", output_to_operand_aliasing={{}: (30, {})} | custom-call | tf_op jit(solution)/shard_map/pallas_call | solution.py:273
  161.6 5.0 %shard_map.46.refs_30_ = f32[32,2,256,1280]{3,2,1,0:T(8,128)} custom-call(bf16[32,32,256]{2,1,0:T(8,128)(2,1)S(1)} %get-tuple-element.140.refs_0_.refs_5_, bf16[32,32,256]{2,1,0:T(8,128)(2,1)S(1)} %get-tuple-element.143.refs_1_.refs_6_, ...), custom_call_target="tpu_custom_call", output_to_operand_aliasing={{}: (30, {})} | custom-call | tf_op jit(solution)/shard_map/pallas_call | solution.py:273
  166.5 5.0 %shard_map.47 = f32[32,2,256,1280]{3,2,1,0:T(8,128)} custom-call(bf16[32,32,256]{2,1,0:T(8,128)(2,1)S(1)} %get-tuple-element.140.refs_0_.refs_5_, bf16[32,32,256]{2,1,0:T(8,128)(2,1)S(1)} %get-tuple-element.143.refs_1_.refs_6_, ...), custom_call_target="tpu_custom_call", output_to_operand_aliasing={{}: (30, {})} | custom-call | tf_op jit(solution)/shard_map/pallas_call | solution.py:273
  (92 shorter events, 25.1 us)
Async XLA Ops:
  1.0 11.9 %collective-permute-start = (bf16[2,256,384]{2,1,0:T(8,128)(2,1)S(1)}, bf16[2,256,384]{2,1,0:T(8,128)(2,1)S(1)}, u32[]{:S(2)}, u32[]{:S(2)}) collective-permute-start(bf16[2,256,384]{2,1,0:T(8,128)(2,1)S(1)} %slice.4), channel_id=1, source_target_pairs={{1,0},{2,1},{3,2},{5,4},{6,5},{7,6},{9,8},{10,9},{11,10},{13,12},{... | collective-permute-start | bytes 1179656 | tf_op jit(solution)/shard_map/ppermute | solution.py:386
  8.9 14.7 %collective-permute-start.8 = (bf16[32,32,256]{2,1,0:T(8,128)(2,1)S(1)}, bf16[32,32,256]{2,1,0:T(8,128)(2,1)S(1)}, u32[]{:S(2)}, u32[]{:S(2)}) collective-permute-start(bf16[32,32,256]{2,1,0:T(8,128)(2,1)S(1)} %get-tuple-element.140.refs_0_.refs_5_), channel_id=1, source_target_pairs={{0,16},{4,20},{8,24},{12,28},{16,0},{20,4},{24,8},{28,12},{1,17},{... | collective-permute-start | bytes 1572872 | tf_op jit(solution)/shard_map/ppermute | solution.py:295
  18.8 12.3 %collective-permute-start.2 = (bf16[6,64,256]{2,1,0:T(8,128)(2,1)S(1)}, bf16[6,64,256]{2,1,0:T(8,128)(2,1)S(1)}, u32[]{:S(2)}, u32[]{:S(2)}) collective-permute-start(bf16[6,64,256]{2,1,0:T(8,128)(2,1)S(1)} %get-tuple-element.102), channel_id=1, source_target_pairs={{0,2},{1,3},{2,0},{3,1},{4,6},{5,7},{6,4},{7,5},{8,10},{9,11},{10,... | collective-permute-start | bytes 589832 | tf_op jit(solution)/shard_map/ppermute | solution.py:295
  19.0 16.4 %collective-permute-start.3 = (bf16[6,64,256]{2,1,0:T(8,128)(2,1)S(1)}, bf16[6,64,256]{2,1,0:T(8,128)(2,1)S(1)}, u32[]{:S(2)}, u32[]{:S(2)}) collective-permute-start(bf16[6,64,256]{2,1,0:T(8,128)(2,1)S(1)} %get-tuple-element.103), channel_id=1, source_target_pairs={{0,3},{1,2},{2,1},{3,0},{4,7},{5,6},{6,5},{7,4},{8,11},{9,10},{10,... | collective-permute-start | bytes 589832 | tf_op jit(solution)/shard_map/ppermute | solution.py:295
  19.3 20.3 %collective-permute-start.7 = (bf16[32,32,256]{2,1,0:T(8,128)(2,1)S(1)}, bf16[32,32,256]{2,1,0:T(8,128)(2,1)S(1)}, u32[]{:S(2)}, u32[]{:S(2)}) collective-permute-start(bf16[32,32,256]{2,1,0:T(8,128)(2,1)S(1)} %get-tuple-element.143.refs_1_.refs_6_), channel_id=1, source_target_pairs={{0,16},{4,20},{8,24},{12,28},{16,0},{20,4},{24,8},{28,12},{1,17},{... | collective-permute-start | bytes 1572872 | tf_op jit(solution)/shard_map/ppermute | solution.py:295
  20.5 17.1 %collective-permute-start.1 = (bf16[12,64,256]{2,1,0:T(8,128)(2,1)S(1)}, bf16[12,64,256]{2,1,0:T(8,128)(2,1)S(1)}, u32[]{:S(2)}, u32[]{:S(2)}) collective-permute-start(bf16[12,64,256]{2,1,0:T(8,128)(2,1)S(1)} %get-tuple-element.99), channel_id=1, source_target_pairs={{0,1},{1,0},{2,3},{3,2},{4,5},{5,4},{6,7},{7,6},{8,9},{9,8},{10,11... | collective-permute-start | bytes 1179656 | tf_op jit(solution)/shard_map/ppermute | solution.py:295
  23.7 16.6 %collective-permute-start.9 = (bf16[32,32,256]{2,1,0:T(8,128)(2,1)S(1)}, bf16[32,32,256]{2,1,0:T(8,128)(2,1)S(1)}, u32[]{:S(2)}, u32[]{:S(2)}) collective-permute-start(bf16[32,32,256]{2,1,0:T(8,128)(2,1)S(1)} %broadcast_select_fusion.4), channel_id=1, source_target_pairs={{0,8},{4,12},{8,0},{12,4},{16,24},{20,28},{24,16},{28,20},{1,9},{5... | collective-permute-start | bytes 1572872 | tf_op jit(solution)/shard_map/ppermute | solution.py:295
  35.4 19.7 %collective-permute-start.6 = (bf16[6,64,256]{2,1,0:T(8,128)(2,1)S(1)}, bf16[6,64,256]{2,1,0:T(8,128)(2,1)S(1)}, u32[]{:S(2)}, u32[]{:S(2)}) collective-permute-start(bf16[6,64,256]{2,1,0:T(8,128)(2,1)S(1)} %get-tuple-element.109), channel_id=1, source_target_pairs={{0,3},{1,2},{2,1},{3,0},{4,7},{5,6},{6,5},{7,4},{8,11},{9,10},{10,... | collective-permute-start | bytes 589832 | tf_op jit(solution)/shard_map/ppermute | solution.py:295
  37.6 17.5 %collective-permute-start.4 = (bf16[12,64,256]{2,1,0:T(8,128)(2,1)S(1)}, bf16[12,64,256]{2,1,0:T(8,128)(2,1)S(1)}, u32[]{:S(2)}, u32[]{:S(2)}) collective-permute-start(bf16[12,64,256]{2,1,0:T(8,128)(2,1)S(1)} %get-tuple-element.105), channel_id=1, source_target_pairs={{0,1},{1,0},{2,3},{3,2},{4,5},{5,4},{6,7},{7,6},{8,9},{9,8},{10,11... | collective-permute-start | bytes 1179656 | tf_op jit(solution)/shard_map/ppermute | solution.py:295
  39.5 32.6 %collective-permute-start.13 = (bf16[24,64,256]{2,1,0:T(8,128)(2,1)S(1)}, bf16[24,64,256]{2,1,0:T(8,128)(2,1)S(1)}, u32[]{:S(2)}, u32[]{:S(2)}) collective-permute-start(bf16[24,64,256]{2,1,0:T(8,128)(2,1)S(1)} %constant_dynamic-update-slice_fusion.3.refs_2_.refs_3_.refs_4_.refs_7_.refs_8_.refs_9_), channel_id=1, source_target_pairs={{0,16},{4,20},{8,24},{12,28},{16,0},{20,4},{24,8},{28,12},{1,17},{... | collective-permute-start | bytes 2359304 | tf_op jit(solution)/shard_map/ppermute | solution.py:295
  40.3 31.8 %collective-permute-start.14 = (bf16[32,32,256]{2,1,0:T(8,128)(2,1)S(1)}, bf16[32,32,256]{2,1,0:T(8,128)(2,1)S(1)}, u32[]{:S(2)}, u32[]{:S(2)}) collective-permute-start(bf16[32,32,256]{2,1,0:T(8,128)(2,1)S(1)} %broadcast_select_fusion.3), channel_id=1, source_target_pairs={{0,8},{4,12},{8,0},{12,4},{16,24},{20,28},{24,16},{28,20},{1,9},{5... | collective-permute-start | bytes 1572872 | tf_op jit(solution)/shard_map/ppermute | solution.py:295
  55.1 14.7 %collective-permute-start.11 = (bf16[6,64,256]{2,1,0:T(8,128)(2,1)S(1)}, bf16[6,64,256]{2,1,0:T(8,128)(2,1)S(1)}, u32[]{:S(2)}, u32[]{:S(2)}) collective-permute-start(bf16[6,64,256]{2,1,0:T(8,128)(2,1)S(1)} %get-tuple-element.117), channel_id=1, source_target_pairs={{0,2},{1,3},{2,0},{3,1},{4,6},{5,7},{6,4},{7,5},{8,10},{9,11},{10,... | collective-permute-start | bytes 589832 | tf_op jit(solution)/shard_map/ppermute | solution.py:295
  55.1 17.0 %collective-permute-start.12 = (bf16[6,64,256]{2,1,0:T(8,128)(2,1)S(1)}, bf16[6,64,256]{2,1,0:T(8,128)(2,1)S(1)}, u32[]{:S(2)}, u32[]{:S(2)}) collective-permute-start(bf16[6,64,256]{2,1,0:T(8,128)(2,1)S(1)} %get-tuple-element.118), channel_id=1, source_target_pairs={{0,3},{1,2},{2,1},{3,0},{4,7},{5,6},{6,5},{7,4},{8,11},{9,10},{10,... | collective-permute-start | bytes 589832 | tf_op jit(solution)/shard_map/ppermute | solution.py:295
  55.1 14.6 %collective-permute-start.10 = (bf16[8,64,256]{2,1,0:T(8,128)(2,1)S(1)}, bf16[8,64,256]{2,1,0:T(8,128)(2,1)S(1)}, u32[]{:S(2)}, u32[]{:S(2)}) collective-permute-start(bf16[8,64,256]{2,1,0:T(8,128)(2,1)S(1)} %get-tuple-element.114), channel_id=1, source_target_pairs={{0,1},{1,0},{2,3},{3,2},{4,5},{5,4},{6,7},{7,6},{8,9},{9,8},{10,11... | collective-permute-start | bytes 786440 | tf_op jit(solution)/shard_map/ppermute | solution.py:295
  72.2 21.5 %collective-permute-start.18 = (bf16[24,64,256]{2,1,0:T(8,128)(2,1)S(1)}, bf16[24,64,256]{2,1,0:T(8,128)(2,1)S(1)}, u32[]{:S(2)}, u32[]{:S(2)}) collective-permute-start(bf16[24,64,256]{2,1,0:T(8,128)(2,1)S(1)} %broadcast_select_fusion.1), channel_id=1, source_target_pairs={{0,8},{4,12},{8,0},{12,4},{16,24},{20,28},{24,16},{28,20},{1,9},{5... | collective-permute-start | bytes 2359304 | tf_op jit(solution)/shard_map/ppermute | solution.py:295
  72.4 21.3 %collective-permute-start.17 = (bf16[24,64,256]{2,1,0:T(8,128)(2,1)S(1)}, bf16[24,64,256]{2,1,0:T(8,128)(2,1)S(1)}, u32[]{:S(2)}, u32[]{:S(2)}) collective-permute-start(bf16[24,64,256]{2,1,0:T(8,128)(2,1)S(1)} %constant_dynamic-update-slice_fusion.6.refs_3_.refs_4_.refs_8_.refs_9_.refs_2_.refs_7_), channel_id=1, source_target_pairs={{0,16},{4,20},{8,24},{12,28},{16,0},{20,4},{24,8},{28,12},{1,17},{... | collective-permute-start | bytes 2359304 | tf_op jit(solution)/shard_map/ppermute | solution.py:295
  73.7 9.1 %collective-permute-start.15 = (bf16[6,64,256]{2,1,0:T(8,128)(2,1)S(1)}, bf16[6,64,256]{2,1,0:T(8,128)(2,1)S(1)}, u32[]{:S(2)}, u32[]{:S(2)}) collective-permute-start(bf16[6,64,256]{2,1,0:T(8,128)(2,1)S(1)} %get-tuple-element.127), channel_id=1, source_target_pairs={{0,2},{1,3},{2,0},{3,1},{4,6},{5,7},{6,4},{7,5},{8,10},{9,11},{10,... | collective-permute-start | bytes 589832 | tf_op jit(solution)/shard_map/ppermute | solution.py:295
  73.7 20.0 %collective-permute-start.16 = (bf16[6,64,256]{2,1,0:T(8,128)(2,1)S(1)}, bf16[6,64,256]{2,1,0:T(8,128)(2,1)S(1)}, u32[]{:S(2)}, u32[]{:S(2)}) collective-permute-start(bf16[6,64,256]{2,1,0:T(8,128)(2,1)S(1)} %get-tuple-element.128), channel_id=1, source_target_pairs={{0,3},{1,2},{2,1},{3,0},{4,7},{5,6},{6,5},{7,4},{8,11},{9,10},{10,... | collective-permute-start | bytes 589832 | tf_op jit(solution)/shard_map/ppermute | solution.py:295
  76.3 36.4 %collective-permute-start.23 = (bf16[4,32,32,256]{3,2,1,0:T(8,128)(2,1)S(1)}, bf16[4,32,32,256]{3,2,1,0:T(8,128)(2,1)S(1)}, u32[]{:S(2)}, u32[]{:S(2)}) collective-permute-start(bf16[4,32,32,256]{3,2,1,0:T(8,128)(2,1)S(1)} %pad_maximum_fusion), channel_id=1, source_target_pairs={{0,4},{4,0},{8,12},{12,8},{16,20},{20,16},{24,28},{28,24},{1,5},{5... | collective-permute-start | bytes 6291464 | tf_op jit(solution)/shard_map/ppermute | solution.py:295
  93.8 18.5 %collective-permute-start.22 = (bf16[24,64,256]{2,1,0:T(8,128)(2,1)S(1)}, bf16[24,64,256]{2,1,0:T(8,128)(2,1)S(1)}, u32[]{:S(2)}, u32[]{:S(2)}) collective-permute-start(bf16[24,64,256]{2,1,0:T(8,128)(2,1)S(1)} %broadcast_select_fusion), channel_id=1, source_target_pairs={{0,8},{4,12},{8,0},{12,4},{16,24},{20,28},{24,16},{28,20},{1,9},{5... | collective-permute-start | bytes 2359304 | tf_op jit(solution)/shard_map/ppermute | solution.py:295
  94.1 15.3 %collective-permute-start.21 = (bf16[20,64,256]{2,1,0:T(8,128)(2,1)S(1)}, bf16[20,64,256]{2,1,0:T(8,128)(2,1)S(1)}, u32[]{:S(2)}, u32[]{:S(2)}) collective-permute-start(bf16[20,64,256]{2,1,0:T(8,128)(2,1)S(1)} %constant_dynamic-update-slice_fusion.refs_3_.refs_4_.refs_8_.refs_9_.refs_2_.refs_7_), channel_id=1, source_target_pairs={{0,16},{4,20},{8,24},{12,28},{16,0},{20,4},{24,8},{28,12},{1,17},{... | collective-permute-start | bytes 1966088 | tf_op jit(solution)/shard_map/ppermute | solution.py:295
  95.4 8.7 %collective-permute-start.19 = (bf16[4,64,256]{2,1,0:T(8,128)(2,1)S(1)}, bf16[4,64,256]{2,1,0:T(8,128)(2,1)S(1)}, u32[]{:S(2)}, u32[]{:S(2)}) collective-permute-start(bf16[4,64,256]{2,1,0:T(8,128)(2,1)S(1)} %get-tuple-element.135), channel_id=1, source_target_pairs={{0,2},{1,3},{2,0},{3,1},{4,6},{5,7},{6,4},{7,5},{8,10},{9,11},{10,... | collective-permute-start | bytes 393224 | tf_op jit(solution)/shard_map/ppermute | solution.py:295
  95.4 11.5 %collective-permute-start.20 = (bf16[4,64,256]{2,1,0:T(8,128)(2,1)S(1)}, bf16[4,64,256]{2,1,0:T(8,128)(2,1)S(1)}, u32[]{:S(2)}, u32[]{:S(2)}) collective-permute-start(bf16[4,64,256]{2,1,0:T(8,128)(2,1)S(1)} %get-tuple-element.136), channel_id=1, source_target_pairs={{0,3},{1,2},{2,1},{3,0},{4,7},{5,6},{6,5},{7,4},{8,11},{9,10},{10,... | collective-permute-start | bytes 393224 | tf_op jit(solution)/shard_map/ppermute | solution.py:295
  109.4 9.7 %collective-permute-start.29 = (bf16[12,64,256]{2,1,0:T(8,128)(2,1)S(1)}, bf16[12,64,256]{2,1,0:T(8,128)(2,1)S(1)}, u32[]{:S(2)}, u32[]{:S(2)}) collective-permute-start(bf16[12,64,256]{2,1,0:T(8,128)(2,1)S(1)} %constant_dynamic-update-slice_fusion.11.refs_3_.refs_4_.refs_8_.refs_9_), channel_id=1, source_target_pairs={{0,16},{4,20},{8,24},{12,28},{16,0},{20,4},{24,8},{28,12},{1,17},{... | collective-permute-start | bytes 1179656 | tf_op jit(solution)/shard_map/ppermute | solution.py:295
  112.4 14.8 %collective-permute-start.26 = (bf16[20,64,256]{2,1,0:T(8,128)(2,1)S(1)}, bf16[20,64,256]{2,1,0:T(8,128)(2,1)S(1)}, u32[]{:S(2)}, u32[]{:S(2)}) collective-permute-start(bf16[20,64,256]{2,1,0:T(8,128)(2,1)S(1)} %broadcast_select_fusion.2), channel_id=1, source_target_pairs={{0,8},{4,12},{8,0},{12,4},{16,24},{20,28},{24,16},{28,20},{1,9},{5... | collective-permute-start | bytes 1966088 | tf_op jit(solution)/shard_map/ppermute | solution.py:295
  113.0 17.0 %collective-permute-start.27 = (bf16[2,24,64,256]{3,2,1,0:T(8,128)(2,1)S(1)}, bf16[2,24,64,256]{3,2,1,0:T(8,128)(2,1)S(1)}, u32[]{:S(2)}, u32[]{:S(2)}) collective-permute-start(bf16[2,24,64,256]{3,2,1,0:T(8,128)(2,1)S(1)} %pad_maximum_fusion.1), channel_id=1, source_target_pairs={{0,4},{4,0},{8,12},{12,8},{16,20},{20,16},{24,28},{28,24},{1,5},{5... | collective-permute-start | bytes 4718600 | tf_op jit(solution)/shard_map/ppermute | solution.py:295
  119.2 8.3 %collective-permute-start.24 = (bf16[4,64,256]{2,1,0:T(8,128)(2,1)S(1)}, bf16[4,64,256]{2,1,0:T(8,128)(2,1)S(1)}, u32[]{:S(2)}, u32[]{:S(2)}) collective-permute-start(bf16[4,64,256]{2,1,0:T(8,128)(2,1)S(1)} %get-tuple-element.147), channel_id=1, source_target_pairs={{0,2},{1,3},{2,0},{3,1},{4,6},{5,7},{6,4},{7,5},{8,10},{9,11},{10,... | collective-permute-start | bytes 393224 | tf_op jit(solution)/shard_map/ppermute | solution.py:295
  119.2 10.8 %collective-permute-start.25 = (bf16[4,64,256]{2,1,0:T(8,128)(2,1)S(1)}, bf16[4,64,256]{2,1,0:T(8,128)(2,1)S(1)}, u32[]{:S(2)}, u32[]{:S(2)}) collective-permute-start(bf16[4,64,256]{2,1,0:T(8,128)(2,1)S(1)} %get-tuple-element.148), channel_id=1, source_target_pairs={{0,3},{1,2},{2,1},{3,0},{4,7},{5,6},{6,5},{7,4},{8,11},{9,10},{10,... | collective-permute-start | bytes 393224 | tf_op jit(solution)/shard_map/ppermute | solution.py:295
  119.2 17.9 %collective-permute-start.31 = (bf16[8,64,256]{2,1,0:T(8,128)(2,1)S(1)}, bf16[8,64,256]{2,1,0:T(8,128)(2,1)S(1)}, u32[]{:S(2)}, u32[]{:S(2)}) collective-permute-start(bf16[8,64,256]{2,1,0:T(8,128)(2,1)S(1)} %constant_dynamic-update-slice_fusion.13.refs_3_.refs_4_.refs_8_.refs_9_), channel_id=1, source_target_pairs={{0,16},{4,20},{8,24},{12,28},{16,0},{20,4},{24,8},{28,12},{1,17},{... | collective-permute-start | bytes 786440 | tf_op jit(solution)/shard_map/ppermute | solution.py:295
  127.2 9.9 %collective-permute-start.32 = (bf16[12,64,256]{2,1,0:T(8,128)(2,1)S(1)}, bf16[12,64,256]{2,1,0:T(8,128)(2,1)S(1)}, u32[]{:S(2)}, u32[]{:S(2)}) collective-permute-start(bf16[12,64,256]{2,1,0:T(8,128)(2,1)S(1)} %broadcast_select_fusion.5), channel_id=1, source_target_pairs={{0,8},{4,12},{8,0},{12,4},{16,24},{20,28},{24,16},{28,20},{1,9},{5... | collective-permute-start | bytes 1179656 | tf_op jit(solution)/shard_map/ppermute | solution.py:295
  137.2 8.7 %collective-permute-start.33 = (bf16[8,64,256]{2,1,0:T(8,128)(2,1)S(1)}, bf16[8,64,256]{2,1,0:T(8,128)(2,1)S(1)}, u32[]{:S(2)}, u32[]{:S(2)}) collective-permute-start(bf16[8,64,256]{2,1,0:T(8,128)(2,1)S(1)} %broadcast_select_fusion.7), channel_id=1, source_target_pairs={{0,8},{4,12},{8,0},{12,4},{16,24},{20,28},{24,16},{28,20},{1,9},{5... | collective-permute-start | bytes 786440 | tf_op jit(solution)/shard_map/ppermute | solution.py:295
  137.6 8.2 %collective-permute-start.34 = (bf16[8,64,256]{2,1,0:T(8,128)(2,1)S(1)}, bf16[8,64,256]{2,1,0:T(8,128)(2,1)S(1)}, u32[]{:S(2)}, u32[]{:S(2)}) collective-permute-start(bf16[8,64,256]{2,1,0:T(8,128)(2,1)S(1)} %constant_dynamic-update-slice_fusion.9.refs_3_.refs_4_.refs_8_.refs_9_), channel_id=1, source_target_pairs={{0,16},{4,20},{8,24},{12,28},{16,0},{20,4},{24,8},{28,12},{1,17},{... | collective-permute-start | bytes 786440 | tf_op jit(solution)/shard_map/ppermute | solution.py:295
  (6 other events, 35.4 us)
